TPU v7x, 128 devices: a whole 4x4x4 slice. The times are simulated.
128 devices in a mesh: px: 8 (over y, z_hi), py: 16 (over z_lo, x, core).
Axes of the slice: x: 4, y: 4, z: 4 (z_hi: 2, z_lo: 2; z = z_hi * 2 + z_lo), core: 2. Of those that a mesh axis runs over, the one named last changes fastest.
Arguments:
- flow_field: bfloat16 [640, 1280, 128], P('px', 'py'), may hold values from -6 to 6
- cotangent: bfloat16 [640, 1280, 128], P('px', 'py'), may hold values from -6 to 6
- spec_weight: float32 [2, 64, 64, 128, 128], P(None, 'px', 'py'), may hold values from -0.375 to 0.375
- skip_weight: bfloat16 [128, 128], replicated, may hold values from -0.5 to 0.5
- ctx_weight: bfloat16 [8, 128, 128], replicated, may hold values from -0.1875 to 0.1875
- up_weight: bfloat16 [128, 512], replicated, may hold values from -0.5 to 0.5
- down_weight: bfloat16 [512, 128], replicated, may hold values from -0.25 to 0.25
- ctx_level: int32 [128, 8], replicated, may hold values from 0 to 2
- ctx_offset: int32 [128, 8, 2], replicated, may hold values from 0 to 60
Outputs:
- layer_output: bfloat16 [640, 1280, 128], P('px', 'py')
- grad_field: bfloat16 [640, 1280, 128], P('px', 'py')
- grad_spec: float32 [2, 64, 64, 128, 128], P(None, 'px', 'py')
- grad_skip: float32 [128, 128], replicated
- grad_ctx: float32 [8, 128, 128], replicated
- grad_up: float32 [128, 512], replicated
- grad_down: float32 [512, 128], replicated
Inputs may be any that keep to these rules, and one draw needn't show every extreme that they name: `ctx_level`: levels name 0, 1 or 2.
All inputs are finite; a program needn't handle non-finite values.
Results may differ from a plain program's by a relative error of at most 0.0075.
Values may be sent and summed in bfloat16 or wider, within the bound.
A program may use at most 256 MiB of HBM per device.

v0:
```python
import math

import jax
import jax.numpy as jnp
from jax import lax
from jax.sharding import PartitionSpec as P

TANH_SCALE = 0.7978845608028654
CUBIC_TERM = 0.044715
HIGHEST = lax.Precision.HIGHEST
STEP_ROWS = (-1, -1, -1, 0, 0, 1, 1, 1)
STEP_COLS = (-1, 0, 1, -1, 1, -1, 0, 1)


def shifted(block, axis, distance):
    devices = range(lax.axis_size(axis))
    route = [((i - distance) % len(devices), i) for i in devices]
    return lax.ppermute(block, axis, route)


def gelu_value(values):
    return (
        0.5
        * values
        * (1.0 + jnp.tanh(TANH_SCALE * (values + CUBIC_TERM * values * values * values)))
    )


def gelu_slope(values):
    tanh_part = jnp.tanh(TANH_SCALE * (values + CUBIC_TERM * values * values * values))
    return 0.5 * (1.0 + tanh_part) + 0.5 * values * (1.0 - tanh_part * tanh_part) * TANH_SCALE * (
        1.0 + 3.0 * CUBIC_TERM * values * values
    )


def angles(positions, wave_list, length):
    turn_count = jnp.mod(positions[:, None] * wave_list[None, :], length)
    phase_angle = turn_count.astype(jnp.float32) * (2.0 * math.pi / length)
    return (jnp.cos(phase_angle), jnp.sin(phase_angle))


def forward_tables(positions, wave_list, length):
    cosine, sine_part = angles(positions, wave_list, length)
    return (
        (cosine / math.sqrt(length)).astype(jnp.bfloat16),
        (-sine_part / math.sqrt(length)).astype(jnp.bfloat16),
    )


def along_y(values, cos_table, sin_table):
    real_part = jnp.einsum("xyc,yk->kxc", values, cos_table, preferred_element_type=jnp.float32)
    imag_part = jnp.einsum("xyc,yk->kxc", values, sin_table, preferred_element_type=jnp.float32)
    return jnp.stack([real_part, imag_part], axis=1)


def forward_y(values, factor, col_index, grid_cols, modes_y):
    edge_cells = values.shape[1]
    span_y = edge_cells * grid_cols
    positions = col_index * edge_cells + jnp.arange(edge_cells, dtype=jnp.int32)

    def term(first_row, row_count):
        wave_list = jnp.arange(row_count, dtype=jnp.int32) - modes_y // 2
        cos_table, sin_table = forward_tables(positions, wave_list, span_y)
        return along_y(values, cos_table, sin_table)

    spectrum = lax.psum_scatter(
        term(jnp.int32(0), modes_y // grid_cols * lax.axis_size("py")),
        "py",
        scatter_dimension=0,
        tiled=True,
    )
    return spectrum * factor


def forward_x(spectrum, factor, row_index, grid_rows, modes_x):
    edge_cells = spectrum.shape[2]
    span_x = edge_cells * grid_rows
    positions = row_index * edge_cells + jnp.arange(edge_cells, dtype=jnp.int32)
    first_part = spectrum[:, 0]
    second = spectrum[:, 1]

    def term(first_row, row_count):
        wave_list = jnp.arange(row_count, dtype=jnp.int32) - modes_x // 2
        cosine, sine_part = angles(positions, wave_list, span_x)
        cos_table = cosine / math.sqrt(span_x)
        sin_table = -sine_part / math.sqrt(span_x)
        real_part = jnp.einsum(
            "kxc,xm->mkc", first_part, cos_table, precision=HIGHEST
        ) - jnp.einsum("kxc,xm->mkc", second, sin_table, precision=HIGHEST)
        imag_part = jnp.einsum(
            "kxc,xm->mkc", first_part, sin_table, precision=HIGHEST
        ) + jnp.einsum("kxc,xm->mkc", second, cos_table, precision=HIGHEST)
        return jnp.stack([real_part, imag_part], axis=2)

    return (
        lax.psum_scatter(
            term(jnp.int32(0), modes_x // grid_rows * lax.axis_size("px")),
            "px",
            scatter_dimension=0,
            tiled=True,
        )
        * factor
    )


def mix_modes(spectrum_modes, weights):
    mode_real = spectrum_modes[:, :, 0]
    mode_imag = spectrum_modes[:, :, 1]
    real_part = jnp.einsum("mkc,mkco->mko", mode_real, weights[0], precision=HIGHEST) - jnp.einsum(
        "mkc,mkco->mko", mode_imag, weights[1], precision=HIGHEST
    )
    imag_part = jnp.einsum("mkc,mkco->mko", mode_real, weights[1], precision=HIGHEST) + jnp.einsum(
        "mkc,mkco->mko", mode_imag, weights[0], precision=HIGHEST
    )
    return jnp.stack([real_part, imag_part], axis=2)


def mode_grads(spectrum_modes, grad_modes, weights):
    mode_real = spectrum_modes[:, :, 0]
    mode_imag = spectrum_modes[:, :, 1]
    grad_real = grad_modes[:, :, 0]
    grad_imag = grad_modes[:, :, 1]
    outer_real = jnp.einsum("mkc,mko->mkco", mode_real, grad_real, precision=HIGHEST) + jnp.einsum(
        "mkc,mko->mkco", mode_imag, grad_imag, precision=HIGHEST
    )
    outer_imag = jnp.einsum("mkc,mko->mkco", mode_real, grad_imag, precision=HIGHEST) - jnp.einsum(
        "mkc,mko->mkco", mode_imag, grad_real, precision=HIGHEST
    )
    back_real = jnp.einsum("mko,mkco->mkc", grad_real, weights[0], precision=HIGHEST) + jnp.einsum(
        "mko,mkco->mkc", grad_imag, weights[1], precision=HIGHEST
    )
    back_imag = jnp.einsum("mko,mkco->mkc", grad_imag, weights[0], precision=HIGHEST) - jnp.einsum(
        "mko,mkco->mkc", grad_real, weights[1], precision=HIGHEST
    )
    return (jnp.stack([outer_real, outer_imag]), jnp.stack([back_real, back_imag], axis=2))


def inverse_x(spectrum_modes, factor, row_index, grid_rows, edge_cells, modes_x):
    span_x = edge_cells * grid_rows
    positions = row_index * edge_cells + jnp.arange(edge_cells, dtype=jnp.int32)

    def accumulate(running, shard_piece, first_mode):
        wave_list = jnp.arange(shard_piece.shape[0], dtype=jnp.int32) - modes_x // 2
        cosine, sine_part = angles(positions, wave_list, span_x)
        cos_table = cosine / math.sqrt(modes_x)
        sin_table = sine_part / math.sqrt(modes_x)
        part_real = shard_piece[:, :, 0]
        part_imag = shard_piece[:, :, 1]
        real_part = jnp.einsum("mkc,xm->kxc", part_real, cos_table, precision=HIGHEST) - jnp.einsum(
            "mkc,xm->kxc", part_imag, sin_table, precision=HIGHEST
        )
        imag_part = jnp.einsum("mkc,xm->kxc", part_real, sin_table, precision=HIGHEST) + jnp.einsum(
            "mkc,xm->kxc", part_imag, cos_table, precision=HIGHEST
        )
        return jnp.stack([real_part, imag_part], axis=1)

    initial = jnp.zeros(
        (spectrum_modes.shape[1], 2, edge_cells, spectrum_modes.shape[3]), jnp.float32
    )
    return (
        accumulate(initial, lax.all_gather(spectrum_modes, "px", axis=0, tiled=True), jnp.int32(0))
        * factor
    )


def inverse_y(spectrum, factor, col_index, grid_cols, modes_y):
    edge_cells = spectrum.shape[2]
    channels = spectrum.shape[3]
    span_y = edge_cells * grid_cols
    positions = col_index * edge_cells + jnp.arange(edge_cells, dtype=jnp.int32)

    def accumulate(running, shard_piece, first_mode):
        wave_list = jnp.arange(shard_piece.shape[0], dtype=jnp.int32) - modes_y // 2
        cosine, sine_part = angles(positions, wave_list, span_y)
        return jnp.einsum(
            "kxc,yk->xyc", shard_piece[:, 0], cosine / math.sqrt(modes_y), precision=HIGHEST
        ) - jnp.einsum(
            "kxc,yk->xyc", shard_piece[:, 1], sine_part / math.sqrt(modes_y), precision=HIGHEST
        )

    initial = jnp.zeros((edge_cells, edge_cells, channels), jnp.float32)
    whole_cells = accumulate(
        initial, lax.all_gather(spectrum, "py", axis=0, tiled=True), jnp.int32(0)
    )
    return whole_cells * factor


def coarsen(values, factor):
    edge_cells = values.shape[0]
    channels = values.shape[2]
    grouped = values.astype(jnp.float32).reshape(
        edge_cells // factor, factor, edge_cells // factor, factor, channels
    )
    return jnp.mean(grouped, axis=(1, 3)).astype(jnp.bfloat16)


def pick_block(pooled, level_value, offset, block_side):
    edge_cells = pooled[0].shape[0]
    channels = pooled[0].shape[2]
    candidates = []
    for depth_level in range(3):
        limit_start = edge_cells // 2**depth_level - block_side
        start_row = jnp.minimum(offset[0] // 2**depth_level, limit_start)
        start_col = jnp.minimum(offset[1] // 2**depth_level, limit_start)
        candidates.append(
            lax.dynamic_slice(
                pooled[depth_level],
                (start_row, start_col, jnp.int32(0)),
                (block_side, block_side, channels),
            )
        )
    return jnp.where(
        level_value == 0, candidates[0], jnp.where(level_value == 1, candidates[1], candidates[2])
    )


def place_block(gradient, level_value, offset, edge_cells):
    block_side = gradient.shape[0]
    channels = gradient.shape[2]
    candidates = []
    for depth_level in range(3):
        factor = 2**depth_level
        coarse_side = edge_cells // factor
        limit_start = coarse_side - block_side
        start_row = jnp.minimum(offset[0] // factor, limit_start)
        start_col = jnp.minimum(offset[1] // factor, limit_start)
        canvas = lax.dynamic_update_slice(
            jnp.zeros((coarse_side, coarse_side, channels), jnp.float32),
            gradient,
            (start_row, start_col, jnp.int32(0)),
        )
        spread = jnp.broadcast_to(
            canvas[:, None, :, None, :], (coarse_side, factor, coarse_side, factor, channels)
        )
        candidates.append(spread.reshape(edge_cells, edge_cells, channels) / float(factor * factor))
    return jnp.where(
        level_value == 0, candidates[0], jnp.where(level_value == 1, candidates[1], candidates[2])
    )


def shift_cols(blocks, amount):
    return shifted(blocks, "py", amount)


def shift_rows(blocks, amount):
    return shifted(blocks, "px", amount)


def back_rows(blocks, amount):
    return shifted(blocks.astype(jnp.bfloat16), "px", amount).astype(blocks.dtype)


def back_cols(blocks, amount):
    return shifted(blocks.astype(jnp.bfloat16), "py", amount).astype(blocks.dtype)


def deliver(outgoing):
    lower = shift_cols(jnp.stack([outgoing[0], outgoing[3], outgoing[5]]), 1)
    upper = shift_cols(jnp.stack([outgoing[2], outgoing[4], outgoing[7]]), -1)
    sectioned = [
        lower[0],
        outgoing[1],
        upper[0],
        lower[1],
        upper[1],
        lower[2],
        outgoing[6],
        upper[2],
    ]
    lower = shift_rows(jnp.stack(sectioned[0:3]), 1)
    upper = shift_rows(jnp.stack(sectioned[5:8]), -1)
    return [lower[0], lower[1], lower[2], sectioned[3], sectioned[4], upper[0], upper[1], upper[2]]


def give_back(gradients):
    lower = back_rows(jnp.stack(gradients[0:3]), -1)
    upper = back_rows(jnp.stack(gradients[5:8]), 1)
    sectioned = [
        lower[0],
        lower[1],
        lower[2],
        gradients[3],
        gradients[4],
        upper[0],
        upper[1],
        upper[2],
    ]
    lower = back_cols(jnp.stack([sectioned[0], sectioned[3], sectioned[5]]), -1)
    upper = back_cols(jnp.stack([sectioned[2], sectioned[4], sectioned[7]]), 1)
    return [lower[0], sectioned[1], upper[0], lower[1], upper[1], lower[2], sectioned[6], upper[2]]


def shards(
    flow_field,
    cotangent,
    spec_weight,
    skip_weight,
    ctx_weight,
    up_weight,
    down_weight,
    ctx_level,
    ctx_offset,
):
    edge_cells = flow_field.shape[0]
    channels = flow_field.shape[2]
    block_side = edge_cells // 4
    grid_rows = lax.axis_size("px")
    grid_cols = lax.axis_size("py")
    row_index = lax.axis_index("px")
    col_index = lax.axis_index("py")
    modes_x = spec_weight.shape[1] * grid_rows
    modes_y = spec_weight.shape[2] * grid_cols
    span_x = edge_cells * grid_rows
    span_y = edge_cells * grid_cols
    inv_cells = 1.0 / math.sqrt(span_x * span_y)
    cell_count = edge_cells * edge_cells
    step_rows = jnp.array(STEP_ROWS, dtype=jnp.int32)
    step_cols = jnp.array(STEP_COLS, dtype=jnp.int32)
    targets = jnp.mod(row_index - step_rows, grid_rows) * grid_cols + jnp.mod(
        col_index - step_cols, grid_cols
    )
    direction_ids = jnp.arange(8, dtype=jnp.int32)
    levels = ctx_level[targets, direction_ids]
    offsets = ctx_offset[targets, direction_ids]
    pooled = (flow_field, coarsen(flow_field, 2), coarsen(flow_field, 4))
    outgoing = [
        pick_block(pooled, levels[direction], offsets[direction], block_side)
        for direction in range(8)
    ]
    arrived_stack = jnp.stack(deliver(outgoing))
    coarse = jnp.einsum(
        "dabc,dco->abo", arrived_stack, ctx_weight, preferred_element_type=jnp.float32
    )
    context_full = jnp.broadcast_to(
        coarse[:, None, :, None, :], (block_side, 4, block_side, 4, channels)
    ).reshape(cell_count, channels)
    spectrum_y = forward_y(flow_field, 1.0, col_index, grid_cols, modes_y)
    spectrum_modes = forward_x(spectrum_y, 1.0, row_index, grid_rows, modes_x)
    mixed = mix_modes(spectrum_modes, spec_weight)
    spectral = inverse_y(
        inverse_x(mixed, 1.0, row_index, grid_rows, edge_cells, modes_x),
        1.0,
        col_index,
        grid_cols,
        modes_y,
    )
    spectral = lax.optimization_barrier(spectral.astype(jnp.bfloat16))
    flat_field = flow_field.reshape(cell_count, channels)
    preact = (
        spectral.astype(jnp.float32).reshape(cell_count, channels)
        + jnp.dot(flat_field, skip_weight, preferred_element_type=jnp.float32)
        + context_full
    )
    middle = lax.optimization_barrier(gelu_value(preact).astype(jnp.bfloat16))
    lifted = jnp.dot(middle, up_weight, preferred_element_type=jnp.float32)
    hidden = gelu_value(lifted).astype(jnp.bfloat16)
    layer_output = (
        middle.astype(jnp.float32)
        + jnp.dot(hidden, down_weight, preferred_element_type=jnp.float32)
    ).astype(jnp.bfloat16)
    flat_grad = cotangent.reshape(cell_count, channels)
    lift_grad = (
        jnp.dot(flat_grad, down_weight.T, preferred_element_type=jnp.float32) * gelu_slope(lifted)
    ).astype(jnp.bfloat16)
    middle_grad = flat_grad.astype(jnp.float32) + jnp.dot(
        lift_grad, up_weight.T, preferred_element_type=jnp.float32
    )
    pre_grad = (middle_grad * gelu_slope(preact)).astype(jnp.bfloat16)
    pre_grid = pre_grad.reshape(edge_cells, edge_cells, channels)
    cell_grad = (
        pre_grid.astype(jnp.float32)
        .reshape(block_side, 4, block_side, 4, channels)
        .sum(axis=(1, 3))
    )
    ctx_partial = jnp.einsum(
        "dabc,abo->dco", arrived_stack.astype(jnp.float32), cell_grad, precision=HIGHEST
    )
    block_grad = jnp.einsum(
        "abo,dco->dabc", cell_grad, ctx_weight.astype(jnp.float32), precision=HIGHEST
    )
    returned = give_back([block_grad[direction] for direction in range(8)])
    ctx_back = place_block(returned[0], levels[0], offsets[0], edge_cells)
    for direction in range(1, 8):
        ctx_back = ctx_back + place_block(
            returned[direction], levels[direction], offsets[direction], edge_cells
        )
    totals = lax.psum(
        (
            jnp.dot(flat_field.T, pre_grad, preferred_element_type=jnp.float32),
            ctx_partial,
            jnp.dot(middle.T, lift_grad, preferred_element_type=jnp.float32),
            jnp.dot(hidden.T, flat_grad, preferred_element_type=jnp.float32),
        ),
        ("px", "py"),
    )
    grad_y = forward_y(pre_grid, math.sqrt(span_y / modes_y), col_index, grid_cols, modes_y)
    grad_modes = forward_x(grad_y, math.sqrt(span_x / modes_x), row_index, grid_rows, modes_x)
    grad_spec, back_modes = mode_grads(spectrum_modes, grad_modes, spec_weight)
    spec_back = inverse_y(
        inverse_x(
            back_modes, math.sqrt(modes_x / span_x), row_index, grid_rows, edge_cells, modes_x
        ),
        math.sqrt(modes_y / span_y),
        col_index,
        grid_cols,
        modes_y,
    )
    skip_back = jnp.dot(pre_grad, skip_weight.T, preferred_element_type=jnp.float32).reshape(
        edge_cells, edge_cells, channels
    )
    grad_field = (spec_back + skip_back + ctx_back).astype(jnp.bfloat16)
    return (
        layer_output.reshape(edge_cells, edge_cells, channels),
        grad_field,
        grad_spec,
        totals[0] * inv_cells,
        totals[1] * inv_cells,
        totals[2] * inv_cells,
        totals[3] * inv_cells,
    )


def solution(mesh):
    return jax.shard_map(
        shards,
        mesh=mesh,
        in_specs=(
            P("px", "py", None),
            P("px", "py", None),
            P(None, "px", "py", None, None),
            P(),
            P(),
            P(),
            P(),
            P(),
            P(),
        ),
        out_specs=(
            P("px", "py", None),
            P("px", "py", None),
            P(None, "px", "py", None, None),
            P(),
            P(),
            P(),
            P(),
        ),
        check_vma=False,
    )
```

profile of v0, /device:TPU:1, one launch (start us, length us, event | category | flops | bytes accessed | tf_op | source)
XLA Modules:
  0.0 779.0 jit_solution(4550686284794795698)
XLA Ops:
  7.3 2.2 convolution_bitcast_fusion.3
  11.0 5.4 copy.89
  16.5 68.3 %reduce-scatter.5.cloned.1.call-done = f32[4,2,80,128]{3,2,1,0:T(8,128)} async-done(((f32[64,2,80,128]{3,2,1,0:T(8,128)}), f32[4,2,80,128]{3,2,1,0:T(8,128)}) %reduce-scatter.5.cloned.1.call-update) | async-done | bytes 327696 | tf_op jit(solution)/shard_map/reduce_scatter | solution.py:66
  91.3 70.7 %reduce-scatter.7.cloned.1.call-done = f32[8,4,2,128]{3,0,1,2:T(8,128)} async-done(((f32[64,4,2,128]{3,0,1,2:T(8,128)}), f32[8,4,2,128]{3,0,1,2:T(8,128)}) %reduce-scatter.7.cloned.1.call-update) | async-done | bytes 32784 | tf_op jit(solution)/shard_map/reduce_scatter | solution.py:96
  163.5 3.4 fusion.30
  166.9 3.4 fusion.40
  174.1 28.1 %all_gather.12 = f32[64,4,2,128]{3,0,1,2:T(8,128)S(1)} all-gather(f32[8,4,2,128]{3,0,1,2:T(8,128)S(1)} %pad_maximum_fusion.15), channel_id=1, replica_groups=mesh['px'=8,'py'=16] {'px'}, dimensions={0}, use_global_device_ids=true | all-gather | bytes 294912 | tf_op jit(solution)/shard_map/all_gather | solution.py:161
  263.6 2.8 reduce_sum.28
  266.4 4.3 reduce_sum.27
  271.8 9.0 %collective-permute-start.1 = (bf16[3,20,20,128]{3,2,1,0:T(8,128)(2,1)S(1)}, bf16[3,20,20,128]{3,2,1,0:T(8,128)(2,1)S(1)}, u32[]{:S(2)}, u32[]{:S(2)}) collective-permute-start(bf16[3,20,20,128]{3,2,1,0:T(8,128)(2,1)S(1)} %pad_maximum_fusion.6), channel_id=1, source_target_pairs={{1,0},{2,1},{3,2},{4,3},{5,4},{6,5},{7,6},{8,7},{9,8},{10,9},{11,1... | collective-permute-start | bytes 921608 | tf_op jit(solution)/shard_map/ppermute | solution.py:18
  291.9 2.5 collective-permute-start.3
  295.6 15.9 %collective-permute-done.3 = bf16[3,20,20,128]{3,2,1,0:T(8,128)(2,1)S(1)} collective-permute-done((bf16[3,20,20,128]{3,2,1,0:T(8,128)(2,1)S(1)}, bf16[3,20,20,128]{3,2,1,0:T(8,128)(2,1)S(1)}, u32[]{:S(2)}, u32[]{:S(2)}) %collective-permute-start.3) | collective-permute-done | bytes 307232 | tf_op jit(solution)/shard_map/ppermute | solution.py:18
  311.9 2.9 slice_bitcast_fusion.3
  314.9 3.8 fusion.22
  318.6 4.0 fusion.54
  325.0 6.1 multiply_convert_fusion
  331.1 9.3 %fusion.6 = bf16[6400,512]{1,0:T(8,128)(2,1)S(1)} fusion(f32[6400,512]{1,0:T(8,128)S(1)} %get-tuple-element.113, bf16[6400,128]{1,0:T(8,128)(2,1)S(1)} %bitcast.414, bf16[512,128]{1,0:T(8,128)(2,1)S(1)} %copy-done.29), kind=kOutput, calls=%fused_computation.10 | convolution fusion | flops 901120000 | bytes 21430272 | tf_op jit(solution)/shard_map/dot_general | solution.py:363
  340.4 2.7 fusion.9
  345.4 5.3 copy.96
  353.9 5.5 fusion.371
  359.4 55.9 %reduce-scatter.9.cloned.1.call-done = f32[4,2,80,128]{3,2,1,0:T(8,128)} async-done(((f32[64,2,80,128]{3,2,1,0:T(8,128)}), f32[4,2,80,128]{3,2,1,0:T(8,128)}) %reduce-scatter.9.cloned.1.call-update) | async-done | bytes 327696 | tf_op jit(solution)/shard_map/reduce_scatter | solution.py:66
  419.0 3.4 convolution_bitcast_fusion.4
  422.4 4.6 fusion.370
  427.5 63.2 %reduce-scatter.11.cloned.1.call-done = f32[8,4,2,128]{3,0,1,2:T(8,128)} async-done(((f32[64,4,2,128]{3,0,1,2:T(8,128)}), f32[8,4,2,128]{3,0,1,2:T(8,128)}) %reduce-scatter.11.cloned.1.call-update) | async-done | bytes 32784 | tf_op jit(solution)/shard_map/reduce_scatter | solution.py:96
  492.3 4.9 fusion.26
  497.2 4.9 fusion.36
  502.2 3.4 fusion.34
  505.5 3.4 fusion.28
  508.9 28.3 %all_gather.14 = f32[64,4,2,128]{3,0,1,2:T(8,128)S(1)} all-gather(f32[8,4,2,128]{3,0,1,2:T(8,128)S(1)} %pad_maximum_fusion.16), channel_id=1, replica_groups=mesh['px'=8,'py'=16] {'px'}, dimensions={0}, use_global_device_ids=true | all-gather | bytes 294912 | tf_op jit(solution)/shard_map/all_gather | solution.py:161
  545.6 5.9 fusion.10
  551.5 2.3 fusion.369
  553.8 4.9 collective-permute-start.4
  570.9 7.8 %collective-permute-start.6 = (bf16[3,20,20,128]{3,2,1,0:T(8,128)(2,1)}, bf16[3,20,20,128]{3,2,1,0:T(8,128)(2,1)}, u32[]{:S(2)}, u32[]{:S(2)}) collective-permute-start(bf16[3,20,20,128]{3,2,1,0:T(8,128)(2,1)} %pad_maximum_fusion.9), channel_id=1, source_target_pairs={{1,0},{2,1},{3,2},{4,3},{5,4},{6,5},{7,6},{8,7},{9,8},{10,9},{11,1... | collective-permute-start | bytes 921608 | tf_op jit(solution)/shard_map/ppermute | solution.py:18
  584.9 64.5 %all-reduce.3.cloned.1.call-done = (f32[128,128]{0,1:T(8,128)}, f32[8,128,128]{2,1,0:T(8,128)}, f32[128,512]{1,0:T(8,128)}, f32[512,128]{1,0:T(8,128)}) async-done(((f32[128,128]{0,1:T(8,128)}, f32[8,128,128]{2,1,0:T(8,128)}, f32[128,512]{1,0:T(8,128)}, f32[512,128]{1,0:T(8,128)}), (f32[128,128]{0,1:T(8,128)}, f32[8,128,128]{2,1,0:T(8,128)}, f32[128,512]{1,0:T(8,128)}, ...) | async-done | bytes 1114128 | tf_op jit(solution)/shard_map/psum | solution.py:387
  690.1 2.2 dynamic_update_slice.82
  702.9 2.3 pad_maximum_fusion.2
  705.1 4.4 slice_bitcast_fusion.1
  709.6 3.7 fusion.18
  713.3 2.8 broadcast_in_dim.47
  716.1 2.7 broadcast_in_dim.41
  718.8 2.8 broadcast_in_dim.51
  721.6 2.7 broadcast_in_dim.55
  724.3 2.7 broadcast_in_dim.49
  727.0 2.7 broadcast_in_dim.45
  729.8 3.1 broadcast_in_dim.43
  732.9 2.8 broadcast_in_dim.53
  744.5 2.3 broadcast_in_dim.44
  753.3 18.5 %fusion.17 = bf16[80,80,128]{2,1,0:T(8,128)(2,1)} fusion(f32[80,80,128]{2,1,0:T(8,128)S(1)} %bitcast.386, f32[80,80,128]{2,1,0:T(8,128)} %dynamic_update_slice.86, f32[80,80,128]{2,1,0:T(8,128)} %bitcast.399, f32[80,80,128]{2,1,0:T(8,128)} %bitcast.389, f32[80,80,128]{2,1,0:T(8,128)} %dynamic_update_slice.84, f32[80,80,128]{2,1,0:T(8,128)} %bitcast.403, ...), kind=kOutput, calls=%fused_computation.32 | convolution fusion | flops 652134400 | bytes 89457232 | tf_op jit(solution)/shard_map/kxc,yk->xyc/dot_general | solution.py:175
  (265 shorter events, 133.7 us)
Async XLA Ops:
  7.2 304.3 %copy-start = (bf16[8,128,128]{2,1,0:T(8,128)(2,1)S(1)}, bf16[8,128,128]{2,1,0:T(8,128)(2,1)}, u32[]{:S(2)}) copy-start(bf16[8,128,128]{2,1,0:T(8,128)(2,1)} %param.15) | copy-start | bytes 786436
  7.2 77.6 %reduce-scatter.5.cloned.1.call-start = ((), (), s32[]{:S(2)}) async-start(), calls=%async_computation.4 | async-start | bytes 5570560 | tf_op jit(solution)/shard_map/reduce_scatter | solution.py:66
  16.4 145.6 %reduce-scatter.7.cloned.1.call-start = ((), (), s32[]{:S(2)}) async-start(), calls=%async_computation.5 | async-start | bytes 294912 | tf_op jit(solution)/shard_map/reduce_scatter | solution.py:96
  91.0 220.9 %all-gather.3.cloned.1.call-start = ((), (), s32[]{:S(2)}) async-start(), calls=%async_computation.6 | async-start | bytes 5570560 | tf_op jit(solution)/shard_map/all_gather | solution.py:183
  162.0 8.4 %copy-start.1 = (f32[2,8,4,128,128]{4,3,2,1,0:T(8,128)S(1)}, f32[2,8,4,128,128]{4,3,2,1,0:T(8,128)}, u32[]{:S(2)}) copy-start(f32[2,8,4,128,128]{4,3,2,1,0:T(8,128)} %param.13) | copy-start | bytes 12582916
  170.4 35.0 %copy-start.40 = (s32[8]{0:T(128)S(1)}, s32[8]{0:T(128)}, u32[]{:S(2)}) copy-start(s32[8]{0:T(128)} %constant.633) | copy-start | bytes 100
  170.4 35.1 %copy-start.41 = (s32[8]{0:T(128)S(1)}, s32[8]{0:T(128)}, u32[]{:S(2)}) copy-start(s32[8]{0:T(128)} %constant.632) | copy-start | bytes 100
  170.4 35.1 %copy-start.3 = (s32[128,8]{0,1:T(8,128)S(1)}, s32[128,8]{0,1:T(8,128)}, u32[]{:S(2)}) copy-start(s32[128,8]{0,1:T(8,128)} %param.18) | copy-start | bytes 12292
  172.3 43.7 %copy-start.39 = (s32[128,8,2]{0,2,1:T(2,128)S(1)}, s32[128,8,2]{0,2,1:T(2,128)}, u32[]{:S(2)}) copy-start(s32[128,8,2]{0,2,1:T(2,128)} %param.19) | copy-start | bytes 24580
  205.1 210.2 %reduce-scatter.9.cloned.1.call-start = ((), (), s32[]{:S(2)}) async-start(), calls=%async_computation.7 | async-start | bytes 5570560 | tf_op jit(solution)/shard_map/reduce_scatter | solution.py:66
  271.8 18.9 %collective-permute-start.1 = (bf16[3,20,20,128]{3,2,1,0:T(8,128)(2,1)S(1)}, bf16[3,20,20,128]{3,2,1,0:T(8,128)(2,1)S(1)}, u32[]{:S(2)}, u32[]{:S(2)}) collective-permute-start(bf16[3,20,20,128]{3,2,1,0:T(8,128)(2,1)S(1)} %pad_maximum_fusion.6), channel_id=1, source_target_pairs={{1,0},{2,1},{3,2},{4,3},{5,4},{6,5},{7,6},{8,7},{9,8},{10,9},{11,1... | collective-permute-start | bytes 921608 | tf_op jit(solution)/shard_map/ppermute | solution.py:18
  281.5 9.2 %collective-permute-start = (bf16[3,20,20,128]{3,2,1,0:T(8,128)(2,1)}, bf16[3,20,20,128]{3,2,1,0:T(8,128)(2,1)}, u32[]{:S(2)}, u32[]{:S(2)}) collective-permute-start(bf16[3,20,20,128]{3,2,1,0:T(8,128)(2,1)} %pad_maximum_fusion.5), channel_id=1, source_target_pairs={{15,0},{0,1},{1,2},{2,3},{3,4},{4,5},{5,6},{6,7},{7,8},{8,9},{9,10... | collective-permute-start | bytes 921608 | tf_op jit(solution)/shard_map/ppermute | solution.py:18
  290.7 24.1 %copy-start.33 = (bf16[1,20,20,128]{3,2,1,0:T(8,128)(2,1)}, bf16[1,20,20,128]{3,2,1,0:T(8,128)(2,1)S(1)}, u32[]{:S(2)}) copy-start(bf16[1,20,20,128]{3,2,1,0:T(8,128)(2,1)S(1)} %get-tuple-element.75) | copy-start | bytes 307204
  291.8 23.0 %copy-start.34 = (bf16[1,20,20,128]{3,2,1,0:T(8,128)(2,1)}, bf16[1,20,20,128]{3,2,1,0:T(8,128)(2,1)S(1)}, u32[]{:S(2)}) copy-start(bf16[1,20,20,128]{3,2,1,0:T(8,128)(2,1)S(1)} %get-tuple-element.72) | copy-start | bytes 307204
  291.9 19.5 %collective-permute-start.3 = (bf16[3,20,20,128]{3,2,1,0:T(8,128)(2,1)S(1)}, bf16[3,20,20,128]{3,2,1,0:T(8,128)(2,1)S(1)}, u32[]{:S(2)}, u32[]{:S(2)}) collective-permute-start(bf16[3,20,20,128]{3,2,1,0:T(8,128)(2,1)S(1)} %pad_maximum_fusion.8), channel_id=1, source_target_pairs={{16,0},{32,16},{48,32},{64,48},{80,64},{96,80},{112,96},{0,112},{1... | collective-permute-start | bytes 921608 | tf_op jit(solution)/shard_map/ppermute | solution.py:18
  294.5 17.0 %collective-permute-start.2 = (bf16[3,20,20,128]{3,2,1,0:T(8,128)(2,1)S(1)}, bf16[3,20,20,128]{3,2,1,0:T(8,128)(2,1)S(1)}, u32[]{:S(2)}, u32[]{:S(2)}) collective-permute-start(bf16[3,20,20,128]{3,2,1,0:T(8,128)(2,1)S(1)} %pad_maximum_fusion.7), channel_id=1, source_target_pairs={{112,0},{0,16},{16,32},{32,48},{48,64},{64,80},{80,96},{96,112},{1... | collective-permute-start | bytes 921608 | tf_op jit(solution)/shard_map/ppermute | solution.py:18
  311.4 3.4 copy-start.44
  311.5 3.4 copy-start.45
  324.9 6.1 copy-start.5
  324.9 6.1 copy-start.29
  325.0 6.1 copy-start.42
  350.7 140.0 %reduce-scatter.11.cloned.1.call-start = ((), (), s32[]{:S(2)}) async-start(), calls=%async_computation.8 | async-start | bytes 294912 | tf_op jit(solution)/shard_map/reduce_scatter | solution.py:96
  418.2 4.2 copy-start.6
  418.9 230.4 %all-reduce.3.cloned.1.call-start = ((), (), s32[]{:S(2)}) async-start(), calls=%async_computation.10 | async-start | bytes 2228224 | tf_op jit(solution)/shard_map/psum | solution.py:387
  427.1 278.1 %all-gather.5.cloned.1.call-start = ((), (), s32[]{:S(2)}) async-start(), calls=%async_computation.9 | async-start | bytes 5570560 | tf_op jit(solution)/shard_map/all_gather | solution.py:183
  490.8 11.4 %copy-start.2 = (f32[2,8,4,128,128]{4,3,2,1,0:T(8,128)S(1)}, f32[2,8,4,128,128]{4,3,2,1,0:T(8,128)}, u32[]{:S(2)}) copy-start(f32[2,8,4,128,128]{4,3,2,1,0:T(8,128)} %param.13) | copy-start | bytes 12582916
  540.2 5.3 copy-start.30
  545.2 6.2 copy-start.32
  545.3 13.9 %collective-permute-start.5 = (bf16[3,20,20,128]{3,2,1,0:T(8,128)(2,1)S(1)}, bf16[3,20,20,128]{3,2,1,0:T(8,128)(2,1)S(1)}, u32[]{:S(2)}, u32[]{:S(2)}) collective-permute-start(bf16[3,20,20,128]{3,2,1,0:T(8,128)(2,1)S(1)} %copy.135), channel_id=1, source_target_pairs={{112,0},{0,16},{16,32},{32,48},{48,64},{64,80},{80,96},{96,112},{1... | collective-permute-start | bytes 921608 | tf_op jit(solution)/shard_map/ppermute | solution.py:18
  553.8 12.0 %collective-permute-start.4 = (bf16[3,20,20,128]{3,2,1,0:T(8,128)(2,1)S(1)}, bf16[3,20,20,128]{3,2,1,0:T(8,128)(2,1)S(1)}, u32[]{:S(2)}, u32[]{:S(2)}) collective-permute-start(bf16[3,20,20,128]{3,2,1,0:T(8,128)(2,1)S(1)} %copy.134), channel_id=1, source_target_pairs={{16,0},{32,16},{48,32},{64,48},{80,64},{96,80},{112,96},{0,112},{1... | collective-permute-start | bytes 921608 | tf_op jit(solution)/shard_map/ppermute | solution.py:18
  570.9 98.8 %collective-permute-start.6 = (bf16[3,20,20,128]{3,2,1,0:T(8,128)(2,1)}, bf16[3,20,20,128]{3,2,1,0:T(8,128)(2,1)}, u32[]{:S(2)}, u32[]{:S(2)}) collective-permute-start(bf16[3,20,20,128]{3,2,1,0:T(8,128)(2,1)} %pad_maximum_fusion.9), channel_id=1, source_target_pairs={{1,0},{2,1},{3,2},{4,3},{5,4},{6,5},{7,6},{8,7},{9,8},{10,9},{11,1... | collective-permute-start | bytes 921608 | tf_op jit(solution)/shard_map/ppermute | solution.py:18
  579.5 76.7 %collective-permute-start.7 = (bf16[3,20,20,128]{3,0,2,1:T(4,128)(2,1)S(1)}, bf16[3,20,20,128]{3,0,2,1:T(4,128)(2,1)S(1)}, u32[]{:S(2)}, u32[]{:S(2)}) collective-permute-start(bf16[3,20,20,128]{3,0,2,1:T(4,128)(2,1)S(1)} %pad_maximum_fusion.4), channel_id=1, source_target_pairs={{15,0},{0,1},{1,2},{2,3},{3,4},{4,5},{5,6},{6,7},{7,8},{8,9},{9,10... | collective-permute-start | bytes 921608 | tf_op jit(solution)/shard_map/ppermute | solution.py:18
  656.6 4.8 copy-start.18
  656.6 9.0 %copy-start.17 = (f32[1,20,20,128]{3,0,2,1:T(1,128)}, f32[1,20,20,128]{3,0,2,1:T(1,128)S(1)}, u32[]{:S(2)}) copy-start(f32[1,20,20,128]{3,0,2,1:T(1,128)S(1)} %get-tuple-element.63) | copy-start | bytes 614404
  709.6 3.8 copy-start.16
  718.8 5.5 copy-start.15
  721.6 5.4 copy-start.14
  724.3 5.4 copy-start.13
  727.0 5.8 copy-start.12
  729.8 5.9 copy-start.27
  732.9 5.0 copy-start.22
  735.6 4.4 copy-start.21
  737.8 4.4 copy-start.20
  740.0 4.4 copy-start.24
  742.2 4.5 copy-start.23
  744.5 4.4 copy-start.26
  746.7 4.3 copy-start.25
  748.9 4.4 copy-start.7
  (14 other events, 24.3 us)
Sparse Core Ops, SparseCore 0:
  16.6 68.1 reduce-scatter.4
  91.2 70.7 reduce-scatter.6
  205.2 46.7 all-gather.2
  350.8 64.4 reduce-scatter.8
  419.7 70.9 reduce-scatter.10
  496.6 152.7 all-reduce.2
  651.2 38.0 all-gather.4
where the time goes:
time: 787 us; the launch traced here: 779 us
  waiting for transfers between devices  340 us (43%)
  matrix products  118 us (15%)
  local copies, waits for them, and re-layouts  114 us (14%)
  between operations  76.7 us (10%)
  blocking collectives  56.4 us (7%)
  other arithmetic  44.8 us (6%)
  starting transfers between devices  29.3 us (4%)
    reduce_scatter x2, waiting for transfers between devices, forward_x(): lax.psum_scatter(term(jnp.int32(0), modes_x // grid_rows * lax.axis_size(...  134 us
    reduce_scatter x2, waiting for transfers between devices, forward_y(): lax.psum_scatter(term(jnp.int32(0), modes_y // grid_cols * lax.axis_size(...  124 us
    psum x1, waiting for transfers between devices, shards(): lax.psum((jnp.dot(flat_field.T, pre_grad, preferred_element_type=jnp.floa...  64.5 us
    all_gather x2, blocking collectives, inverse_x(): lax.all_gather(spectrum_modes, 'px', axis=0, tiled=True)  56.4 us
    broadcast_in_dim x24, local copies, waits for them, and re-layouts, place_block(): jnp.broadcast_to(canvas[:, None, :, None, :], (coarse_side, factor, coars...  43 us
    ppermute x8, starting transfers between devices, shifted(): return lax.ppermute(block, axis, route)  27.9 us
    dynamic_update_slice x16, local copies, waits for them, and re-layouts, place_block(): lax.dynamic_update_slice(jnp.zeros((coarse_side, coarse_side, channels),...  22.5 us
    dot_general x2, matrix products, accumulate(): jnp.einsum('kxc,yk->xyc', shard_piece[:, 0], cosine / math.sqrt(modes_y),...  22.4 us
  transfers between devices with their start and end apart: 15, of which 7 were waited for; matrix products, arithmetic and copies ran while one was open for 17% of the time, Pallas kernels for 0%

commit v1 on v0

v1 whole, which is shorter than its diff:
```python
import functools
import math

import jax
import jax.numpy as jnp
import ml_dtypes
import numpy as np
from jax import lax
from jax.experimental import pallas as pl
from jax.experimental.pallas import tpu as pltpu
from jax.sharding import PartitionSpec as P

BF = jnp.bfloat16
F32 = jnp.float32
TANH_SCALE = 0.7978845608028654
CUBIC_TERM = 0.044715
STEP_ROWS = (-1, -1, -1, 0, 0, 1, 1, 1)
STEP_COLS = (-1, 0, 1, -1, 1, -1, 0, 1)
ROWS, COLS = 8, 16
SIDE, C, H, BLK = 80, 128, 512, 20
NX, NY, MX, MY = 640, 1280, 64, 64
TOT = 2304
PIECE = TOT // COLS
VMEM_LIMIT = 56 * 1024 * 1024
MESH = pl.DeviceIdType.MESH
VM = pl.BlockSpec(memory_space=pltpu.VMEM)
SM = pl.BlockSpec(memory_space=pltpu.SMEM)
HB = pl.BlockSpec(memory_space=pl.ANY)


def wave_tables():
    waves = np.arange(64) - 32

    def parts(length, side):
        turns = (np.arange(length)[:, None] * waves[None, :]) % length
        phase = turns * (2.0 * math.pi / length)
        return np.cos(phase).reshape(-1, side, 64), np.sin(phase).reshape(-1, side, 64)

    cos_y, sin_y = parts(NY, SIDE)
    cos_x, sin_x = parts(NX, SIDE)
    to_modes_y = np.stack([cos_y, -sin_y], axis=-1).reshape(COLS, SIDE, 128) / math.sqrt(NY)
    to_modes_y = to_modes_y.transpose(0, 2, 1)
    to_cells_y = np.stack([cos_y, -sin_y], axis=-1).reshape(COLS, SIDE, 128) / math.sqrt(MY)
    cx, sx = cos_x.transpose(0, 2, 1), -sin_x.transpose(0, 2, 1)
    real = np.concatenate([cx, -sx], axis=2)
    imag = np.concatenate([sx, cx], axis=2)
    to_modes_x = np.stack([real, imag], axis=2).reshape(ROWS, 128, 2 * SIDE) / math.sqrt(NX)
    real = np.stack([cos_x, -sin_x], axis=-1).reshape(ROWS, SIDE, 128)
    imag = np.stack([sin_x, cos_x], axis=-1).reshape(ROWS, SIDE, 128)
    to_cells_x = np.concatenate([real, imag], axis=1) / math.sqrt(MX)
    return [
        np.ascontiguousarray(t).astype(ml_dtypes.bfloat16)
        for t in (to_modes_y, to_cells_y, to_modes_x, to_cells_x)
    ]


def iota(shape, axis):
    return lax.broadcasted_iota(jnp.int32, shape, axis)


def dot(a, b):
    return jnp.dot(a, b, preferred_element_type=F32)


def dot_tb(a, b):
    return lax.dot_general(a, b, (((1,), (1,)), ((), ())), preferred_element_type=F32)


def dot_ta(a, b):
    return lax.dot_general(a, b, (((0,), (0,)), ((), ())), preferred_element_type=F32)


def over_80(v):
    return (v * 52429) >> 22


def over_20(v):
    return (v * 52429) >> 20


def build_to_modes(table, big_ref):
    lane = iota((SIDE, 640), 1)
    tile = (lane - 80 * over_80(lane) == iota((SIDE, 640), 0)).astype(F32).astype(BF)
    for part in range(8):
        rep = ((iota((128, 128), 0) >> 3) + 16 * part == iota((128, 128), 1)).astype(F32)
        rows = dot(dot(rep.astype(BF), table).astype(BF), tile)
        mask = (iota((128, 640), 0) & 7) == over_80(iota((128, 640), 1))
        big_ref[pl.ds(128 * part, 128), :] = jnp.where(mask, rows, 0.0).astype(BF)


def build_to_cells(table, big_ref):
    rep = ((iota((128, 1024), 1) >> 3) == iota((128, 1024), 0)).astype(F32)
    wide = dot(table, rep.astype(BF))
    lane = iota((SIDE, 1024), 1) & 7
    for x in range(8):
        big_ref[pl.ds(SIDE * x, SIDE), :] = jnp.where(lane == x, wide, 0.0).astype(BF)


def x_to_modes(table, ay_ref, out_ref):
    def step(pair, carry):
        wide = []
        for ky in (2 * pair, 2 * pair + 1):
            real = ay_ref[:, 2 * ky].reshape(SIDE, C).astype(BF)
            imag = ay_ref[:, 2 * ky + 1].reshape(SIDE, C).astype(BF)
            wide.append(jnp.concatenate([real, imag], axis=0))
        modes = dot(table, jnp.concatenate(wide, axis=1))
        out_ref[2 * pair] = modes[:, :C].astype(BF)
        out_ref[2 * pair + 1] = modes[:, C:].astype(BF)
        return carry

    lax.fori_loop(0, 32, step, 0)


def x_to_cells(table, z_ref, p_ref):
    def step(pair, carry):
        wide = jnp.concatenate([z_ref[2 * pair], z_ref[2 * pair + 1]], axis=1)
        cells = dot(table, wide)
        for h in range(2):
            for r in range(2):
                piece = cells[r * SIDE : (r + 1) * SIDE, h * C : (h + 1) * C]
                p_ref[:, 2 * (2 * pair + h) + r] = piece.reshape(10, 8, C)
        return carry

    lax.fori_loop(0, 32, step, 0)


def y_store(modes, ay_ref, pair):
    ay_ref[2 * pair] = modes[:, :C].reshape(128, 8, C)
    ay_ref[2 * pair + 1] = modes[:, C:].reshape(128, 8, C)


def first_kernel(level, offset, field, ty, tx, s_out, blocks, big_out, ay, p0, p1, p2, tmp):
    row, col = lax.axis_index("px"), lax.axis_index("py")
    build_to_modes(ty[col], big_out)

    def y_step(pair, carry):
        first = field[pl.ds(16 * pair, 8)].reshape(640, C)
        second = field[pl.ds(16 * pair + 8, 8)].reshape(640, C)
        y_store(dot(big_out[...], jnp.concatenate([first, second], axis=1)), ay, pair)
        return carry

    lax.fori_loop(0, 5, y_step, 0)
    x_to_modes(tx[row], ay, s_out)

    def widen(x, carry):
        p0[x, pl.ds(0, SIDE)] = field[x].astype(F32)
        return carry

    lax.fori_loop(0, SIDE, widen, 0)

    def pool1(x, carry):
        total = jnp.zeros((40, C), F32)
        for a in range(2):
            for b in range(2):
                total = total + p0[2 * x + a, pl.ds(b, 40, stride=2)]
        p1[x, pl.ds(0, 40)] = (total * 0.25).astype(BF).astype(F32)
        return carry

    lax.fori_loop(0, 40, pool1, 0)

    def pool2(x, carry):
        total = jnp.zeros((20, C), F32)
        for a in range(4):
            for b in range(4):
                total = total + p0[4 * x + a, pl.ds(b, 20, stride=4)]
        p2[x, pl.ds(0, 20)] = (total * 0.0625).astype(BF).astype(F32)
        return carry

    lax.fori_loop(0, 20, pool2, 0)
    for d in range(8):
        target = lax.rem(row - STEP_ROWS[d] + ROWS, ROWS) * COLS
        target = target + lax.rem(col - STEP_COLS[d] + COLS, COLS)
        depth = level[target, d]
        for l, grid in enumerate((p0, p1, p2)):

            @pl.when(depth == l)
            def _():
                last = SIDE // 2**l - BLK
                sx = jnp.minimum(offset[target, 2 * d] >> l, last)
                sy = jnp.minimum(offset[target, 2 * d + 1] >> l, last)
                for a in range(BLK):
                    tmp[pl.ds(BLK * a, 24)] = grid[sx + a, pl.ds(sy, 24)]

        blocks[d] = tmp[pl.ds(0, 400)].astype(BF)


def first_call(level, offset, field, ty, tx):
    return pl.pallas_call(
        first_kernel,
        out_shape=(
            jax.ShapeDtypeStruct((64, 128, C), BF),
            jax.ShapeDtypeStruct((8, 400, C), BF),
            jax.ShapeDtypeStruct((1024, 640), BF),
        ),
        in_specs=[SM, SM, VM, VM, VM],
        out_specs=(VM, VM, VM),
        scratch_shapes=[
            pltpu.VMEM((10, 128, 8, C), F32),
            pltpu.VMEM((SIDE, 88, C), F32),
            pltpu.VMEM((40, 48, C), F32),
            pltpu.VMEM((20, 32, C), F32),
            pltpu.VMEM((408, C), F32),
        ],
        compiler_params=pltpu.CompilerParams(vmem_limit_bytes=VMEM_LIMIT),
        name="pick_and_forward",
    )(level, offset, field, ty, tx)


def exchange_kernel(back, *refs):
    if back:
        s, t, b, w, z, to, bo, u = refs[:8]
        refs = refs[8:]
    else:
        s, b, w, z, bo, u = refs[:6]
        refs = refs[6:]
    r0, s1, r1, s2, r2, zs, zp, wv, acc = refs[:9]
    send0, recv0, send1, recv1, send2, recv2, send3, recv3 = refs[9:17]
    send4, recv4, send5, recv5, sendc, recvc, local = refs[17:24]
    if back:
        t0, t1, q1, t2, q2, tacc, tout = refs[24:31]
        tsend0, trecv0, tsend1, trecv1, tsend2, trecv2 = refs[31:37]
        tsend4, trecv4, tsend5, trecv5 = refs[37:41]
    i, j = lax.axis_index("px"), lax.axis_index("py")
    c, q = j % 2, j // 2
    sibling = (i, 2 * q + 1 - c)

    def chip(n):
        return (i, 2 * n + c)

    def remote(src, dst, send, recv, device):
        return pltpu.make_async_remote_copy(
            src_ref=src,
            dst_ref=dst,
            send_sem=send,
            recv_sem=recv,
            device_id=device,
            device_id_type=MESH,
        )

    def loop(low, high, body):
        def step(n, carry):
            body(n)
            return carry

        lax.fori_loop(low, high, step, 0)

    def neighbour(d, sign):
        return (
            (i + sign * STEP_ROWS[d] + ROWS) % ROWS,
            (j + sign * STEP_COLS[d] + COLS) % COLS,
        )

    barrier = pltpu.get_barrier_semaphore()

    def greet(device):
        pl.semaphore_signal(barrier, inc=1, device_id=device, device_id_type=MESH)

    greet(sibling)

    def greet_more(r):
        greet(chip((q + r) % 8))
        greet(((i + r) % 8, j))

    loop(1, 8, greet_more)
    for d in range(8):
        greet(neighbour(d, 1))
    pl.semaphore_wait(barrier, 23)

    weights = pltpu.make_async_copy(w, wv, local.at[0])
    weights.start()

    def core_copy(n):
        return remote(s.at[2 * n + 1 - c], r0.at[n], send0.at[n], recv0.at[n], sibling)

    def core_copy_t(n):
        return remote(t.at[2 * n + 1 - c], t0.at[n], tsend0.at[n], trecv0.at[n], sibling)

    loop(1, 9, lambda r: core_copy((q + r) % 8).start())
    if back:
        loop(1, 9, lambda r: core_copy_t((q + r) % 8).start())

    def chip_copy(n, slot, device):
        return remote(s1.at[n], r1.at[slot], send1.at[n], recv1.at[slot], device)

    def chip_copy_t(n, slot, device):
        return remote(q1.at[n], t1.at[slot], tsend1.at[n], trecv1.at[slot], device)

    def pass_on(r):
        n = (q + r) % 8
        core_copy(n).wait_recv()
        s1[n] = (s[2 * n + c].astype(F32) + r0[n].astype(F32)).astype(BF)
        chip_copy(n, q, chip(n)).start()

    loop(1, 8, pass_on)
    core_copy(q).wait_recv()
    acc[...] = s[2 * q + c].astype(F32) + r0[q].astype(F32)

    def block_copy(d):
        sign = 1 if back else -1
        return remote(b.at[d], bo.at[d], sendc.at[d], recvc.at[d], neighbour(d, sign))

    for d in range(8):
        block_copy(d).start()
    if back:

        def pass_on_t(r):
            n = (q + r) % 8
            core_copy_t(n).wait_recv()
            q1[n] = (t[2 * n + c].astype(F32) + t0[n].astype(F32)).astype(BF)
            chip_copy_t(n, q, chip(n)).start()

        loop(1, 8, pass_on_t)
        core_copy_t(q).wait_recv()
        tacc[...] = t[2 * q + c].astype(F32) + t0[q].astype(F32)

    def gather_chip(r):
        n = (q - r + 8) % 8
        chip_copy(n, n, chip(n)).wait_recv()
        acc[...] = acc[...] + r1[n].astype(F32)

    loop(1, 8, gather_chip)
    s2[...] = acc[...].astype(BF).reshape(4, 128, C)

    def rows_of(n):
        return pl.ds(pl.multiple_of(n * 16, 16), 16)

    def row_copy(n, slot, device):
        return remote(s2.at[:, rows_of(n)], r2.at[slot], send2.at[n], recv2.at[slot], device)

    def send_row(r):
        n = (i + r) % 8
        row_copy(n, i, (n, j)).start()

    loop(1, 8, send_row)
    u[...] = s2[:, rows_of(i)].astype(F32)

    def gather_row(r):
        n = (i - r + 8) % 8
        row_copy(n, n, (n, j)).wait_recv()
        u[...] = u[...] + r2[n].astype(F32)

    loop(1, 8, gather_row)
    if back:
        u[...] = u[...] * math.sqrt(NX * NY / (MX * MY))
    weights.wait()
    same = iota((16, 16), 0) ^ 1
    turn = jnp.where(iota((16, 16), 1) == same, 1.0, 0.0)
    odd = (iota((16, 16), 0) & 1) == 1
    flip = odd if back else jnp.logical_not(odd)
    turn = jnp.where(flip, -turn, turn).astype(BF)

    def mix(ky):
        first = u[ky].astype(BF)
        both = jnp.concatenate([first, dot(turn, first).astype(BF)], axis=1)
        total = jnp.zeros((16, C), F32)
        for kx in range(8):
            if back:
                mat = jnp.concatenate([wv[0, kx, ky], wv[1, kx, ky]], axis=1).astype(BF)
                res = dot_tb(both, mat)
            else:
                mat = jnp.concatenate([wv[0, kx, ky], wv[1, kx, ky]], axis=0).astype(BF)
                res = dot(both, mat)
            total = jnp.where((iota((16, C), 0) >> 1) == kx, res, total)
        zs[ky] = total.astype(BF)

    loop(0, 4, mix)
    zp[:, rows_of(i)] = zs[...]

    def mode_copy(slot, sem, device):
        return remote(zs, zp.at[:, rows_of(slot)], send3.at[sem], recv3.at[slot], device)

    def send_mode(r):
        n = (i + r) % 8
        mode_copy(i, n, (n, j)).start()

    loop(1, 8, send_mode)
    if back:

        def gather_chip_t(r):
            n = (q - r + 8) % 8
            chip_copy_t(n, n, chip(n)).wait_recv()
            tacc[...] = tacc[...] + t1[n].astype(F32)

        loop(1, 8, gather_chip_t)
        q2[...] = tacc[...].astype(BF)
        t2[i] = q2[...]

        def row_copy_t(n, slot, device):
            return remote(q2, t2.at[slot], tsend2.at[n], trecv2.at[slot], device)

        def send_row_t(r):
            n = (i + r) % 8
            row_copy_t(n, i, (n, j)).start()

        loop(1, 8, send_row_t)

    def gather_mode(r):
        n = (i - r + 8) % 8
        mode_copy(n, n, (n, j)).wait_recv()

    loop(1, 8, gather_mode)

    own = pltpu.make_async_copy(zp, z.at[j], local.at[1])
    own.start()

    def all_copy(slot, sem, recv, device):
        return remote(zp, z.at[slot], send4.at[sem], recv, device)

    def send_all(r):
        n = (q + r) % 8
        all_copy(j, n, recv4.at[q], chip(n)).start()

    loop(1, 8, send_all)
    all_copy(j, q, recv5.at[q], sibling).start()
    if back:

        def gather_row_t(r):
            n = (i - r + 8) % 8
            row_copy_t(n, n, (n, j)).wait_recv()

        loop(1, 8, gather_row_t)
        total = t2[0].astype(F32)
        for n in range(1, 8):
            total = total + t2[n].astype(F32)
        tout[...] = total.astype(BF)
        own_t = pltpu.make_async_copy(tout, to.at[j], local.at[2])
        own_t.start()

        def all_copy_t(slot, sem, recv, device):
            return remote(tout, to.at[slot], tsend4.at[sem], recv, device)

        def send_all_t(r):
            n = (q + r) % 8
            all_copy_t(j, n, trecv4.at[q], chip(n)).start()

        loop(1, 8, send_all_t)
        all_copy_t(j, q, trecv5.at[q], sibling).start()

    def forward_copy(n):
        piece = z.at[2 * n + c]
        return remote(piece, piece, send5.at[n], recv5.at[n], sibling)

    def forward(r):
        n = (q - r + 8) % 8
        all_copy(2 * n + c, n, recv4.at[n], chip(n)).wait_recv()
        forward_copy(n).start()

    loop(1, 8, forward)
    if back:

        def forward_copy_t(n):
            piece = to.at[2 * n + c]
            return remote(piece, piece, tsend5.at[n], trecv5.at[n], sibling)

        def forward_t(r):
            n = (q - r + 8) % 8
            all_copy_t(2 * n + c, n, trecv4.at[n], chip(n)).wait_recv()
            forward_copy_t(n).start()

        loop(1, 8, forward_t)

    def settle(r):
        n = (q + r) % 8
        all_copy(2 * n + 1 - c, n, recv5.at[n], sibling).wait_recv()
        core_copy(n).wait_send()
        all_copy(j, n, recv4.at[q], chip(n)).wait_send()
        if back:
            all_copy_t(2 * n + 1 - c, n, trecv5.at[n], sibling).wait_recv()
            core_copy_t(n).wait_send()
            all_copy_t(j, n, trecv4.at[q], chip(n)).wait_send()

    loop(1, 9, settle)

    def settle_most(r):
        n = (q + r) % 8
        forward_copy(n).wait_send()
        chip_copy(n, q, chip(n)).wait_send()
        m = (i + r) % 8
        row_copy(m, i, (m, j)).wait_send()
        mode_copy(i, m, (m, j)).wait_send()
        if back:
            forward_copy_t(n).wait_send()
            chip_copy_t(n, q, chip(n)).wait_send()
            row_copy_t(m, i, (m, j)).wait_send()

    loop(1, 8, settle_most)
    own.wait()
    if back:
        own_t.wait()
    for d in range(8):
        block_copy(d).wait()


def exchange(back, s, blocks, weights, totals=None):
    shape = jax.ShapeDtypeStruct
    out_shape = [shape((16, 4, 128, C), BF)]
    out_specs = [HB]
    operands = [s.reshape(16, 512, C)]
    in_specs = [VM]
    if back:
        out_shape.append(shape((16, PIECE, C), BF))
        out_specs.append(HB)
        operands.append(totals)
        in_specs.append(VM)
    out_shape += [shape((8, 400, C), BF), shape((4, 16, C), F32)]
    out_specs += [HB, VM]
    operands += [blocks, weights]
    in_specs += [HB, HB]
    sem = pltpu.SemaphoreType.DMA((8,))
    scratch = [
        pltpu.VMEM((8, 512, C), BF),
        pltpu.VMEM((8, 512, C), BF),
        pltpu.VMEM((8, 512, C), BF),
        pltpu.VMEM((4, 128, C), BF),
        pltpu.VMEM((8, 4, 16, C), BF),
        pltpu.VMEM((4, 16, C), BF),
        pltpu.VMEM((4, 128, C), BF),
        pltpu.VMEM((2, 8, 4, C, C), F32),
        pltpu.VMEM((512, C), F32),
    ] + [sem] * 15
    if back:
        scratch += [
            pltpu.VMEM((8, PIECE, C), BF),
            pltpu.VMEM((8, PIECE, C), BF),
            pltpu.VMEM((8, PIECE, C), BF),
            pltpu.VMEM((8, PIECE, C), BF),
            pltpu.VMEM((PIECE, C), BF),
            pltpu.VMEM((PIECE, C), F32),
            pltpu.VMEM((PIECE, C), BF),
        ] + [sem] * 10
    return pl.pallas_call(
        functools.partial(exchange_kernel, back),
        out_shape=tuple(out_shape),
        in_specs=in_specs,
        out_specs=tuple(out_specs),
        scratch_shapes=scratch,
        compiler_params=pltpu.CompilerParams(
            collective_id=2 if back else 1,
            has_side_effects=True,
            vmem_limit_bytes=VMEM_LIMIT,
        ),
        name="exchange_back" if back else "exchange",
    )(*operands)


def gelu_both(v):
    square = v * v
    t = jnp.tanh(v * (TANH_SCALE + (TANH_SCALE * CUBIC_TERM) * square))
    half = 0.5 + 0.5 * t
    inner = (0.5 * TANH_SCALE) + (1.5 * TANH_SCALE * CUBIC_TERM) * square
    return v * half, half + v * (1.0 - t * t) * inner


def middle_kernel(
    field, cot, z, blk, skip, ctx, up, down, gy, gx, tx, big_in,
    layer, pre_out, s_out, tot, bgrad,
    p, ay, cells_big, spread, gather, coarse, cell, pre, slope, mid, lifted, dh, hid, lg,
    acc_skip, acc_up, acc_down,
):
    step = pl.program_id(0)
    row, col = lax.axis_index("px"), lax.axis_index("py")

    @pl.when(step == 0)
    def _():
        x_to_cells(gx[row], z, p)
        build_to_cells(gy[col], cells_big)
        total = dot(blk[0], ctx[0])
        for d in range(1, 8):
            total = total + dot(blk[d], ctx[d])
        coarse[...] = total
        n, l = iota((1280, 160), 0), iota((1280, 160), 1)
        l = jnp.where(l >= 80, l - 80, l)
        x = over_80(n)
        y = n - 80 * x
        a = over_20(l)
        hit = ((x >> 2) == a) & ((y >> 2) == l - 20 * a)
        spread[...] = jnp.where(hit, 1.0, 0.0).astype(BF)
        l, n = iota((80, 1280), 0), iota((80, 1280), 1)
        x = over_80(n)
        y = n - 80 * x
        a = over_20(l)
        hit = ((x >> 2) == a) & ((y >> 2) == l - 20 * a)
        gather[...] = jnp.where(hit, 1.0, 0.0).astype(BF)
        acc_skip[...] = jnp.zeros_like(acc_skip)
        acc_up[...] = jnp.zeros_like(acc_up)
        acc_down[...] = jnp.zeros_like(acc_down)

    own_rows = pl.ds(pl.multiple_of(80 * step, 8), 80)
    flat = field[...].reshape(1280, C)
    flat_cot = cot[...].reshape(1280, C)
    wide = jnp.concatenate(
        [p[2 * step].reshape(1024, C).astype(BF), p[2 * step + 1].reshape(1024, C).astype(BF)],
        axis=1,
    )
    spectral = dot(cells_big[...], wide)
    own = coarse[own_rows]
    high = own.astype(BF)
    low = (own - high.astype(F32)).astype(BF)
    rest = dot(flat, skip[...]) + dot(spread[...], jnp.concatenate([high, low], axis=0))
    pre[pl.ds(0, 640)] = spectral[:, :C].astype(BF).astype(F32) + rest[:640]
    pre[pl.ds(640, 640)] = spectral[:, C:].astype(BF).astype(F32) + rest[640:]

    def activate(n, carry):
        rows = pl.ds(pl.multiple_of(64 * n, 64), 64)
        value, slant = gelu_both(pre[rows])
        mid[rows] = value.astype(BF)
        slope[rows] = slant
        return carry

    lax.fori_loop(0, 20, activate, 0)
    lifted[...] = dot(mid[...], up[...])
    dh[...] = dot_tb(flat_cot, down[...])

    def activate_wide(n, carry):
        rows = pl.ds(pl.multiple_of(16 * n, 16), 16)
        value, slant = gelu_both(lifted[rows])
        hid[rows] = value.astype(BF)
        lg[rows] = (dh[rows] * slant).astype(BF)
        return carry

    lax.fori_loop(0, 80, activate_wide, 0)
    result = mid[...].astype(F32) + dot(hid[...], down[...])
    layer[...] = result.astype(BF).reshape(16, SIDE, C)
    grad = flat_cot.astype(F32) + dot_tb(lg[...], up[...])
    grad = (grad * slope[...]).astype(BF)
    pre_out[...] = grad.reshape(16, SIDE, C)
    acc_skip[...] += dot_ta(flat, grad)
    acc_up[...] += dot_ta(mid[...], lg[...])
    acc_down[...] += dot_ta(flat_cot, hid[...])
    cell[own_rows] = dot(gather[...], grad)
    y_store(dot(big_in[...], jnp.concatenate([grad[:640], grad[640:]], axis=1)), ay, step)

    @pl.when(step == 4)
    def _():
        x_to_modes(tx[row], ay, s_out)
        narrow = cell[...].astype(BF)
        tot[pl.ds(0, 128)] = acc_skip[...].astype(BF)
        for d in range(8):
            tot[pl.ds(128 + 128 * d, 128)] = dot_ta(blk[d], narrow).astype(BF)
            bgrad[d] = dot_tb(narrow, ctx[d]).astype(BF)
        for part in range(4):
            cut = slice(128 * part, 128 * part + 128)
            tot[pl.ds(1152 + 128 * part, 128)] = acc_up[:, cut].astype(BF)
            tot[pl.ds(1664 + 128 * part, 128)] = acc_down[:, cut].T.astype(BF)
        tot[pl.ds(2176, 128)] = jnp.zeros((128, C), BF)


def whole(*shape):
    zeros = (0,) * len(shape)
    return pl.BlockSpec(shape, lambda n: zeros)


def middle_call(field, cot, z, blk, skip, ctx, up, down, gy, gx, tx, big):
    shape = jax.ShapeDtypeStruct
    tile = pl.BlockSpec((16, SIDE, C), lambda n: (n, 0, 0))
    return pl.pallas_call(
        middle_kernel,
        grid=(5,),
        out_shape=(
            shape((SIDE, SIDE, C), BF),
            shape((SIDE, SIDE, C), BF),
            shape((64, 128, C), BF),
            shape((TOT, C), BF),
            shape((8, 400, C), BF),
        ),
        in_specs=[
            tile, tile, whole(64, 128, C), whole(8, 400, C), whole(C, C), whole(8, C, C),
            whole(C, H), whole(H, C), whole(COLS, SIDE, 128), whole(ROWS, 160, 128),
            whole(ROWS, 128, 160), whole(1024, 640),
        ],
        out_specs=(tile, tile, whole(64, 128, C), whole(TOT, C), whole(8, 400, C)),
        scratch_shapes=[
            pltpu.VMEM((10, 128, 8, C), F32),
            pltpu.VMEM((10, 128, 8, C), F32),
            pltpu.VMEM((640, 1024), BF),
            pltpu.VMEM((1280, 160), BF),
            pltpu.VMEM((80, 1280), BF),
            pltpu.VMEM((400, C), F32),
            pltpu.VMEM((400, C), F32),
            pltpu.VMEM((1280, C), F32),
            pltpu.VMEM((1280, C), F32),
            pltpu.VMEM((1280, C), BF),
            pltpu.VMEM((1280, H), F32),
            pltpu.VMEM((1280, H), F32),
            pltpu.VMEM((1280, H), BF),
            pltpu.VMEM((1280, H), BF),
            pltpu.VMEM((C, C), F32),
            pltpu.VMEM((C, H), F32),
            pltpu.VMEM((C, H), F32),
        ],
        compiler_params=pltpu.CompilerParams(vmem_limit_bytes=VMEM_LIMIT),
        name="cells",
    )(field, cot, z, blk, skip, ctx, up, down, gy, gx, tx, big)


def last_kernel(level, offset, pre, z, back, skip, gy, gx, out, p, cells_big, place, grads, wide):
    step = pl.program_id(0)
    row, col = lax.axis_index("px"), lax.axis_index("py")
    starts = []
    for d in range(8):
        target = lax.rem(row - STEP_ROWS[d] + ROWS, ROWS) * COLS
        target = target + lax.rem(col - STEP_COLS[d] + COLS, COLS)
        depth = level[target, d]
        last = jnp.where(depth == 0, 60, jnp.where(depth == 1, 20, 0))
        sx = jnp.minimum(offset[target, 2 * d] >> depth, last)
        sy = jnp.minimum(offset[target, 2 * d + 1] >> depth, last)
        starts.append((depth, sx, sy))

    @pl.when(step == 0)
    def _():
        x_to_cells(gx[row], z, p)
        build_to_cells(gy[col], cells_big)
        y, lane = iota((SIDE, 192), 0), iota((SIDE, 192), 1)
        total = jnp.zeros((SIDE, 192), F32)
        for d in range(8):
            depth, sx, sy = starts[d]
            share = jnp.where(depth == 0, 1.0, jnp.where(depth == 1, 0.25, 0.0625))
            spot = lane - 24 * d
            line = jnp.where(depth == 0, y, jnp.where(depth == 1, y >> 1, y >> 2))
            hit = (spot >= 0) & (spot < BLK) & (line - sy == spot)
            total = jnp.where(hit, share, total)
        place[...] = total.astype(BF)
        wide[pl.ds(400, 8)] = jnp.zeros((8, C), F32)
        for d in range(8):
            wide[pl.ds(0, 400)] = back[d].astype(F32)
            for a in range(BLK):
                grads[d, a] = wide[pl.ds(BLK * a, 24)]
            grads[d, BLK] = jnp.zeros((24, C), F32)

    both = jnp.concatenate(
        [p[2 * step].reshape(1024, C).astype(BF), p[2 * step + 1].reshape(1024, C).astype(BF)],
        axis=1,
    )
    factor = math.sqrt(MX * MY / (NX * NY))
    spectral = dot(cells_big[...], both) * factor
    straight = dot_tb(pre[...].reshape(1280, C), skip[...])
    for x in range(16):
        pieces = []
        for d in range(8):
            depth, sx, sy = starts[d]
            a = ((16 * step + x) >> depth) - sx
            a = jnp.where((a >= 0) & (a < BLK), a, BLK)
            pieces.append(grads[d, a])
        context = dot(place[...], jnp.concatenate(pieces, axis=0).astype(BF))
        h, k = x // 8, x % 8
        total = spectral[80 * k : 80 * k + 80, C * h : C * h + C]
        total = total + straight[80 * x : 80 * x + 80] + context
        out[x] = total.astype(BF)


def last_call(level, offset, pre, z, back, skip, gy, gx):
    tile = pl.BlockSpec((16, SIDE, C), lambda n: (n, 0, 0))
    return pl.pallas_call(
        last_kernel,
        grid=(5,),
        out_shape=jax.ShapeDtypeStruct((SIDE, SIDE, C), BF),
        in_specs=[
            SM, SM, tile, whole(64, 128, C), whole(8, 400, C), whole(C, C),
            whole(COLS, SIDE, 128), whole(ROWS, 160, 128),
        ],
        out_specs=tile,
        scratch_shapes=[
            pltpu.VMEM((10, 128, 8, C), F32),
            pltpu.VMEM((640, 1024), BF),
            pltpu.VMEM((SIDE, 192), BF),
            pltpu.VMEM((8, BLK + 1, 24, C), F32),
            pltpu.VMEM((408, C), F32),
        ],
        compiler_params=pltpu.CompilerParams(vmem_limit_bytes=VMEM_LIMIT),
        name="field_gradient",
    )(level, offset, pre, z, back, skip, gy, gx)


def outer_kernel(u, g, tot, spec, skip, ctx, up, down):
    kx = pl.program_id(0)
    mask = (iota((16, C), 0) >> 1) == kx
    turn = jnp.where(iota((16, 16), 1) == (iota((16, 16), 0) ^ 1), 1.0, 0.0)
    turn = jnp.where((iota((16, 16), 0) & 1) == 1, -turn, turn)
    for ky in range(4):
        left = jnp.where(mask, u[ky], 0.0)
        left_high = left.astype(BF)
        left_low = (left - left_high.astype(F32)).astype(BF)
        right = g[ky]
        right_high = right.astype(BF)
        right_low = (right - right_high.astype(F32)).astype(BF)
        narrow = turn.astype(BF)
        high = jnp.concatenate([right_high, dot(narrow, right_high).astype(BF)], axis=1)
        low = jnp.concatenate([right_low, dot(narrow, right_low).astype(BF)], axis=1)
        lefts = jnp.concatenate([left_high, left_high, left_low], axis=0)
        rights = jnp.concatenate([high, low, high], axis=0)
        res = dot_ta(lefts, rights)
        spec[0, 0, ky] = res[:, :C]
        spec[1, 0, ky] = res[:, C:]

    @pl.when(kx == 0)
    def _():
        inv = 1.0 / math.sqrt(NX * NY)
        skip[...] = tot[pl.ds(0, 128)].astype(F32) * inv
        for d in range(8):
            ctx[d] = tot[pl.ds(128 + 128 * d, 128)].astype(F32) * inv
        for part in range(4):
            cut = slice(128 * part, 128 * part + 128)
            up[:, cut] = tot[pl.ds(1152 + 128 * part, 128)].astype(F32) * inv
        down[...] = tot[pl.ds(1664, 512)].astype(F32) * inv


def outer_call(u, g, tot):
    shape = jax.ShapeDtypeStruct
    return pl.pallas_call(
        outer_kernel,
        grid=(8,),
        out_shape=(
            shape((2, 8, 4, C, C), F32),
            shape((C, C), F32),
            shape((8, C, C), F32),
            shape((C, H), F32),
            shape((H, C), F32),
        ),
        in_specs=[whole(4, 16, C), whole(4, 16, C), whole(TOT, C)],
        out_specs=(
            pl.BlockSpec((2, 1, 4, C, C), lambda n: (0, n, 0, 0, 0)),
            whole(C, C),
            whole(8, C, C),
            whole(C, H),
            whole(H, C),
        ),
        compiler_params=pltpu.CompilerParams(vmem_limit_bytes=VMEM_LIMIT),
        name="weight_gradients",
    )(u, g, tot)


def shards(
    flow_field, cotangent, spec_weight, skip_weight, ctx_weight, up_weight, down_weight,
    ctx_level, ctx_offset,
):
    ty, gy, tx, gx = (jnp.asarray(t) for t in wave_tables())
    offset = ctx_offset.reshape(ROWS * COLS, 16)
    s, blocks, big = first_call(ctx_level, offset, flow_field, ty, tx)
    z, arrived, u = exchange(False, s, blocks, spec_weight)
    layer, pre, s, tot, bgrad = middle_call(
        flow_field, cotangent, z.reshape(64, 128, C), arrived, skip_weight, ctx_weight,
        up_weight, down_weight, gy, gx, tx, big,
    )
    z, tot, back, g = exchange(True, s, bgrad, spec_weight, tot.reshape(16, PIECE, C))
    spec, skip, ctx, up, down = outer_call(u, g, tot.reshape(TOT, C))
    grad = last_call(
        ctx_level, offset, pre, z.reshape(64, 128, C), back, skip_weight, gy, gx
    )
    return layer, grad, spec, skip, ctx, up, down


def solution(mesh):
    return jax.shard_map(
        shards,
        mesh=mesh,
        in_specs=(
            P("px", "py", None),
            P("px", "py", None),
            P(None, "px", "py", None, None),
            P(),
            P(),
            P(),
            P(),
            P(),
            P(),
        ),
        out_specs=(
            P("px", "py", None),
            P("px", "py", None),
            P(None, "px", "py", None, None),
            P(),
            P(),
            P(),
            P(),
        ),
        check_vma=False,
    )
```

time: 787 us -> 222 us (0.28)
  waiting for transfers between devices: 340 us -> 0 us
  Pallas kernels: 0 us -> 217 us
  matrix products: 118 us -> 0 us
  local copies, waits for them, and re-layouts: 114 us -> 2.84 us
  between operations: 76.7 us -> 0.65 us
  blocking collectives: 56.4 us -> 0 us
  other arithmetic: 44.8 us -> 0 us
  starting transfers between devices: 29.3 us -> 0 us
    reduce_scatter x4 -> x0, waiting for transfers between devices: 258 us -> none  [the longest x2 134 us: forward_x(): lax.psum_scatter(term(jnp.int32(0), modes_x // grid_rows * lax.axis_size(...]
    pallas_call x0 -> x6, Pallas kernels: none -> 217 us  [the longest x2 128 us: exchange(): pl.pallas_call(functools.partial(exchange_kernel, back), out_shape=tuple(...]
    dot_general x44 -> x0, matrix products: 118 us -> none  [the longest x2 22.4 us: accumulate(): jnp.einsum('kxc,yk->xyc', shard_piece[:, 0], cosine / math.sqrt(modes_y),...]
    psum x1 -> x0, waiting for transfers between devices: 64.5 us -> none  [shards(): lax.psum((jnp.dot(flat_field.T, pre_grad, preferred_element_type=jnp.floa...]
    all_gather x2 -> x0, blocking collectives: 56.4 us -> none  [inverse_x(): lax.all_gather(spectrum_modes, 'px', axis=0, tiled=True)]
    broadcast_in_dim x25 -> x0, local copies, waits for them, and re-layouts: 43.5 us -> none  [the longest x24 43 us: place_block(): jnp.broadcast_to(canvas[:, None, :, None, :], (coarse_side, factor, coars...]
    ppermute x8 -> x0, starting transfers between devices: 27.9 us -> none  [shifted(): return lax.ppermute(block, axis, route)]
    another operation x10 -> x0, local copies, waits for them, and re-layouts: 26.1 us -> none
  transfers between devices with their start and end apart: 15 -> 0, of which waited for: 7 -> 0; matrix products, arithmetic and copies ran while one was open for 17% -> 0% of each run, Pallas kernels for 0% -> 0%
where the time goes in v1:
time: 222 us; the launch traced here: 221 us
  Pallas kernels  217 us (98%)
  local copies, waits for them, and re-layouts  2.84 us (1%)
    pallas_call x2, Pallas kernels, exchange(): pl.pallas_call(functools.partial(exchange_kernel, back), out_shape=tuple(...  128 us
    pallas_call x1, Pallas kernels, middle_call(): pl.pallas_call(middle_kernel, grid=(5,), out_shape=(shape((SIDE, SIDE, C)...  51.5 us
    pallas_call x1, Pallas kernels, first_call(): pl.pallas_call(first_kernel, out_shape=(jax.ShapeDtypeStruct((64, 128, C)...  16.3 us
    pallas_call x1, Pallas kernels, last_call(): pl.pallas_call(last_kernel, grid=(5,), out_shape=jax.ShapeDtypeStruct((SI...  14.5 us
    pallas_call x1, Pallas kernels, outer_call(): pl.pallas_call(outer_kernel, grid=(8,), out_shape=(shape((2, 8, 4, C, C),...  7.03 us

profile of v1, /device:TPU:1, one launch (start us, length us, event | category | flops | bytes accessed | tf_op | source)
XLA Modules:
  0.0 220.8 jit_solution(13329056292258369272)
XLA Ops:
  0.6 1.4 copy.23.level
  2.0 1.4 copy.24.offset
  3.5 16.3 %pick_and_forward.1 = (bf16[64,128,128]{2,1,0:T(8,128)(2,1)}, bf16[8,400,128]{2,1,0:T(8,128)(2,1)}, bf16[1024,640]{1,0:T(8,128)(2,1)}) custom-call(s32[128,8]{1,0:T(8,128)} %copy.23.level, s32[128,16]{1,0:T(8,128)} %copy.24.offset, bf16[80,80,128]{2,1,0:T(8,128)(2,1)} %field.3, bf16[16,128,80]{2,1,0:T(8,128)(2,1)} %constant.8.clone.ty, ...), custom_call_target="tpu_custom_call" | custom-call | tf_op jit(solution)/shard_map/pick_and_forward/pallas_call | solution.py:188
  19.8 63.3 %exchange.1 = (bf16[16,4,128,128]{3,2,1,0:T(8,128)(2,1)}, bf16[8,400,128]{2,1,0:T(8,128)(2,1)}, f32[4,16,128]{2,1,0:T(8,128)}) custom-call(bf16[16,512,128]{2,1,0:T(8,128)(2,1)} %bitcast.7, bf16[8,400,128]{2,1,0:T(8,128)(2,1)} %get-tuple-element.28.refs_1_, f32[2,8,4,128,128]{4,3,2,1,0:T(8,128)} %refs_3_.1), custom_call_target="tpu_custom_call" | custom-call | tf_op jit(solution)/shard_map/exchange/pallas_call | solution.py:531
  83.1 51.5 %cells.1 = (bf16[80,80,128]{2,1,0:T(8,128)(2,1)}, bf16[80,80,128]{2,1,0:T(8,128)(2,1)}, bf16[64,128,128]{2,1,0:T(8,128)(2,1)}, bf16[2304,128]{1,0:T(8,128)(2,1)}, bf16[8,400,128]{2,1,0:T(8,128)(2,1)}) custom-call(bf16[80,80,128]{2,1,0:T(8,128)(2,1)} %field.3, bf16[80,80,128]{2,1,0:T(8,128)(2,1)} %cot.1, bf16[64,128,128]{2,1,0:T(8,128)(2,1)} %bitcast.10, ...), custom_call_target="tpu_custom_call" | custom-call | tf_op jit(solution)/shard_map/cells/pallas_call | solution.py:656
  134.7 64.6 %exchange_back.1 = (bf16[16,4,128,128]{3,2,1,0:T(8,128)(2,1)}, bf16[16,144,128]{2,1,0:T(8,128)(2,1)}, bf16[8,400,128]{2,1,0:T(8,128)(2,1)}, f32[4,16,128]{2,1,0:T(8,128)}) custom-call(bf16[16,512,128]{2,1,0:T(8,128)(2,1)} %bitcast.9, bf16[16,144,128]{2,1,0:T(8,128)(2,1)} %bitcast.12, bf16[8,400,128]{2,1,0:T(8,128)(2,1)} %get-tuple-element.36.refs_2_, ...), custom_call_target="tpu_custom_call" | custom-call | tf_op jit(solution)/shard_map/exchange_back/pallas_call | solution.py:531
  199.2 14.5 %field_gradient.1 = bf16[80,80,128]{2,1,0:T(8,128)(2,1)} custom-call(s32[128,8]{1,0:T(8,128)} %copy.23.level, s32[128,16]{1,0:T(8,128)} %copy.24.offset, bf16[80,80,128]{2,1,0:T(8,128)(2,1)} %get-tuple-element.33.pre, bf16[64,128,128]{2,1,0:T(8,128)(2,1)} %bitcast.8, bf16[8,400,128]{2,1,0:T(8,128)(2,1)} %get-tuple-element.38.back, bf16[128,128]{1,0:T(8,128)(2,1)} %skip.3, ...), custom_call_target="tpu_custom_call" | custom-call | tf_op jit(solution)/shard_map/field_gradient/pallas_call | solution.py:753
  213.7 7.0 %weight_gradients.1 = (f32[2,8,4,128,128]{4,3,2,1,0:T(8,128)}, f32[128,128]{1,0:T(8,128)}, f32[8,128,128]{2,1,0:T(8,128)}, f32[128,512]{1,0:T(8,128)}, f32[512,128]{1,0:T(8,128)}) custom-call(f32[4,16,128]{2,1,0:T(8,128)} %get-tuple-element.39.u, f32[4,16,128]{2,1,0:T(8,128)} %get-tuple-element.40.g, bf16[2304,128]{1,0:T(8,128)(2,1)} %bitcast.11), custom_call_target="tpu_custom_call" | custom-call | tf_op jit(solution)/shard_map/weight_gradients/pallas_call | solution.py:809

commit v2 on v1

v2 whole, which is shorter than its diff:
```python
import functools
import math

import jax
import jax.numpy as jnp
import ml_dtypes
import numpy as np
from jax import lax
from jax.experimental import pallas as pl
from jax.experimental.pallas import tpu as pltpu
from jax.sharding import PartitionSpec as P

BF = jnp.bfloat16
F32 = jnp.float32
TANH_SCALE = 0.7978845608028654
CUBIC_TERM = 0.044715
STEP_ROWS = (-1, -1, -1, 0, 0, 1, 1, 1)
STEP_COLS = (-1, 0, 1, -1, 1, -1, 0, 1)
ROWS, COLS = 8, 16
SIDE, C, H, BLK = 80, 128, 512, 20
NX, NY, MX, MY = 640, 1280, 64, 64
PIECE = 80
TOT = 32 * PIECE
VMEM_LIMIT = 56 * 1024 * 1024
MESH = pl.DeviceIdType.MESH
VM = pl.BlockSpec(memory_space=pltpu.VMEM)
SM = pl.BlockSpec(memory_space=pltpu.SMEM)
HB = pl.BlockSpec(memory_space=pl.ANY)


def wave_tables():
    waves = np.arange(64) - 32

    def parts(length, side):
        turns = (np.arange(length)[:, None] * waves[None, :]) % length
        phase = turns * (2.0 * math.pi / length)
        return np.cos(phase).reshape(-1, side, 64), np.sin(phase).reshape(-1, side, 64)

    cos_y, sin_y = parts(NY, SIDE)
    cos_x, sin_x = parts(NX, SIDE)
    to_modes_y = np.stack([cos_y, -sin_y], axis=-1).reshape(COLS, SIDE, 128) / math.sqrt(NY)
    to_modes_y = to_modes_y.transpose(0, 2, 1)
    to_cells_y = np.stack([cos_y, -sin_y], axis=-1).reshape(COLS, SIDE, 128) / math.sqrt(MY)
    cx, sx = cos_x.transpose(0, 2, 1), -sin_x.transpose(0, 2, 1)
    real = np.concatenate([cx, -sx], axis=2)
    imag = np.concatenate([sx, cx], axis=2)
    to_modes_x = np.stack([real, imag], axis=2).reshape(ROWS, 128, 2 * SIDE) / math.sqrt(NX)
    real = np.stack([cos_x, -sin_x], axis=-1).reshape(ROWS, SIDE, 128)
    imag = np.stack([sin_x, cos_x], axis=-1).reshape(ROWS, SIDE, 128)
    to_cells_x = np.concatenate([real, imag], axis=1) / math.sqrt(MX)

    def rounded(t):
        return np.ascontiguousarray(t).astype(ml_dtypes.bfloat16)

    def rest(t):
        return rounded(t - rounded(t).astype(np.float64))

    high, low = rounded(to_modes_x), rest(to_modes_x)
    wide_modes_x = np.concatenate([high, low, high], axis=2)
    wide_cells_x = np.concatenate([rounded(to_cells_x), rest(to_cells_x)], axis=2)
    return rounded(to_modes_y), rounded(to_cells_y), wide_modes_x, wide_cells_x


def iota(shape, axis):
    return lax.broadcasted_iota(jnp.int32, shape, axis)


def dot(a, b):
    return jnp.dot(a, b, preferred_element_type=F32)


def dot_tb(a, b):
    return lax.dot_general(a, b, (((1,), (1,)), ((), ())), preferred_element_type=F32)


def dot_ta(a, b):
    return lax.dot_general(a, b, (((0,), (0,)), ((), ())), preferred_element_type=F32)


def over_80(v):
    return (v * 52429) >> 22


def over_20(v):
    return (v * 52429) >> 20


def build_to_modes(table, big_ref):
    lane = iota((SIDE, 640), 1)
    tile = (lane - 80 * over_80(lane) == iota((SIDE, 640), 0)).astype(F32).astype(BF)
    for part in range(8):
        rep = ((iota((128, 128), 0) >> 3) + 16 * part == iota((128, 128), 1)).astype(F32)
        rows = dot(dot(rep.astype(BF), table).astype(BF), tile)
        mask = (iota((128, 640), 0) & 7) == over_80(iota((128, 640), 1))
        big_ref[pl.ds(128 * part, 128), :] = jnp.where(mask, rows, 0.0).astype(BF)


def build_to_cells(table, big_ref):
    rep = ((iota((128, 1024), 1) >> 3) == iota((128, 1024), 0)).astype(F32)
    wide = dot(table, rep.astype(BF))
    lane = iota((SIDE, 1024), 1) & 7
    for x in range(8):
        big_ref[pl.ds(SIDE * x, SIDE), :] = jnp.where(lane == x, wide, 0.0).astype(BF)


def x_to_modes(table, ay_ref, kys):
    wide = []
    for ky in kys:
        both = [ay_ref[:, 2 * ky + r].reshape(SIDE, C) for r in range(2)]
        high = [v.astype(BF) for v in both]
        low = [(v - h.astype(F32)).astype(BF) for v, h in zip(both, high)]
        wide.append(jnp.concatenate(high + high + low, axis=0))
    modes = dot(table, jnp.concatenate(wide, axis=1)).astype(BF)
    return modes[:, :C], modes[:, C:]


def x_to_cells(table, z_ref, p_ref):
    def step(pair, carry):
        wide = jnp.concatenate([z_ref[2 * pair], z_ref[2 * pair + 1]], axis=1)
        cells = dot(table, jnp.concatenate([wide, wide], axis=0))
        for h in range(2):
            for r in range(2):
                piece = cells[r * SIDE : (r + 1) * SIDE, h * C : (h + 1) * C]
                p_ref[:, 2 * (2 * pair + h) + r] = piece.reshape(10, 8, C)
        return carry

    lax.fori_loop(0, 32, step, 0, unroll=4)


def y_store(modes, ay_ref, pair):
    ay_ref[2 * pair] = modes[:, :C].reshape(128, 8, C)
    ay_ref[2 * pair + 1] = modes[:, C:].reshape(128, 8, C)


def y_to_modes(big, field, ay):
    def y_step(pair, carry):
        first = field[pl.ds(16 * pair, 8)].reshape(640, C)
        second = field[pl.ds(16 * pair + 8, 8)].reshape(640, C)
        y_store(dot(big[...], jnp.concatenate([first, second], axis=1)), ay, pair)
        return carry

    lax.fori_loop(0, 5, y_step, 0)


def start_of(pick):
    depth = pick & 3
    first, second = (pick >> 2) & 127, pick >> 9

    def choose(zero, one, two):
        return jnp.where(depth == 0, zero, jnp.where(depth == 1, one, two))

    last = choose(SIDE - BLK, SIDE // 2 - BLK, 0)
    sx = jnp.minimum(choose(first, first >> 1, first >> 2), last)
    sy = jnp.minimum(choose(second, second >> 1, second >> 2), last)
    return depth, sx, sy


def pick_of(picks, row, col, d):
    target = lax.rem(row - STEP_ROWS[d] + ROWS, ROWS) * COLS
    return picks[target + lax.rem(col - STEP_COLS[d] + COLS, COLS), d]


def pick_blocks(picks, row, col, field, grid, tmp, blocks):
    def widen(x, carry):
        grid[x, pl.ds(0, SIDE)] = field[x].astype(F32)
        return carry

    lax.fori_loop(0, SIDE, widen, 0, unroll=4)

    def pool1(x, carry):
        total = jnp.zeros((40, C), F32)
        for a in range(2):
            for b in range(2):
                total = total + grid[2 * x + a, pl.ds(b, 40, stride=2)]
        grid[SIDE + x, pl.ds(0, 40)] = (total * 0.25).astype(BF).astype(F32)
        return carry

    lax.fori_loop(0, 40, pool1, 0, unroll=4)

    def pool2(x, carry):
        total = jnp.zeros((20, C), F32)
        for a in range(4):
            for b in range(4):
                total = total + grid[4 * x + a, pl.ds(b, 20, stride=4)]
        grid[SIDE + 40 + x, pl.ds(0, 20)] = (total * 0.0625).astype(BF).astype(F32)
        return carry

    lax.fori_loop(0, 20, pool2, 0, unroll=4)
    for d in range(8):
        depth, sx, sy = start_of(pick_of(picks, row, col, d))
        base = sx + jnp.where(depth == 0, 0, jnp.where(depth == 1, SIDE, SIDE + 40))
        for a in range(BLK):
            tmp[pl.ds(BLK * a, 24)] = grid[base + a, pl.ds(sy, 24)]
        blocks[d] = tmp[pl.ds(0, 400)].astype(BF)


def exchange_kernel(back, *refs):
    refs = list(refs)

    def take(n):
        taken = refs[:n]
        del refs[:n]
        return taken

    if back:
        s, b, w, t = take(4)
        z, bo, u, to = take(4)
    else:
        picks, field, ty, tx, w = take(5)
        z, bo, u, big_out = take(4)
    r0, sa, sb, r1a, r1b, acca, accb, r2a, r2b, ab, r3, zs, zz, za, zb, wv = take(16)
    core_a, core_b, one_a, one_b, two_a, two_b, three, wide3 = take(8)
    wide2_a, wide2_b, wide1_a, wide1_b, share_a, share_b, blocks, local = take(8)
    if back:
        t0, t1s, t1, t2s, t2, t3s, t3, tall = take(8)
        core_t, one_t, two_t, three_t, wide2_t, wide1_t, share_t = take(7)
    else:
        s, b, big, ay, grid, tmp, ty_own, tx_own = take(8)
    i, j = lax.axis_index("px"), lax.axis_index("py")
    y, zh = i // 2, i % 2
    zl, x, c = j // 8, (j // 2) % 4, j % 2
    spot = 2 * zl + zh
    sibling = (i, 8 * zl + 2 * x + 1 - c)

    def at_x(n):
        return (i, 8 * zl + 2 * n + c)

    def at_y(n):
        return (2 * n + zh, j)

    def at_z(n):
        return (2 * y + n % 2, 8 * (n // 2) + 2 * x + c)

    def remote(src, dst, sems, sent, landed, device):
        return pltpu.make_async_remote_copy(
            src_ref=src,
            dst_ref=dst,
            send_sem=sems.at[0, sent],
            recv_sem=sems.at[1, landed],
            device_id=device,
            device_id_type=MESH,
        )

    def neighbour(d, sign):
        return (
            (i + sign * STEP_ROWS[d] + ROWS) % ROWS,
            (j + sign * STEP_COLS[d] + COLS) % COLS,
        )

    def band(n, size=32):
        return pl.ds(pl.multiple_of(n * size, size), size)

    barrier = pltpu.get_barrier_semaphore()
    partners = [sibling]
    for r in (1, 2, 3):
        partners += [at_x((x + r) % 4), at_y((y + r) % 4), at_z((spot + r) % 4)]
    partners += [neighbour(d, 1) for d in range(8)]
    for device in partners:
        pl.semaphore_signal(barrier, inc=1, device_id=device, device_id_type=MESH)
    weights = pltpu.make_async_copy(w, wv, local.at[0])
    weights.start()
    if not back:
        table_y = pltpu.make_async_copy(ty.at[j], ty_own, local.at[3])
        table_y.start()
        table_x = pltpu.make_async_copy(tx.at[i], tx_own, local.at[4])
        table_x.start()
        pick_blocks(picks, i, j, field, grid, tmp, b)
    pl.semaphore_wait(barrier, len(partners))
    waits = []

    def begin(copy):
        copy.start()
        waits.append(copy)

    def core_copy_a(n):
        return remote(s.at[:, n, 1 - c, 0:2], r0.at[:, n, 0:2], core_a, n, n, sibling)

    def core_copy_b(n):
        src = s.at[:, :, 1 - c, 2:4, band(n)]
        return remote(src, r0.at[:, :, 2:4, band(n)], core_b, n, n, sibling)

    def block_copy(d):
        device = neighbour(d, 1 if back else -1)
        return remote(b.at[d], bo.at[d], blocks, d, d, device)

    def fill(n, half):
        def step(m, carry):
            a, e = m // 2, m % 2
            ky = 4 * (8 * a + 2 * n + e) + 2 * half
            first, second = x_to_modes(tx_own[...], ay, (ky, ky + 1))
            s[a, n, e, 2 * half] = first
            s[a, n, e, 2 * half + 1] = second
            return carry

        lax.fori_loop(0, 4, step, 0, unroll=2)

    if back:
        for r in (2, 1, 3, 0):
            begin(core_copy_a((x + r) % 4))
            begin(core_copy_b((y + r) % 4))
    else:
        for d in range(8):
            begin(block_copy(d))
        table_y.wait()
        build_to_modes(ty_own[...], big)
        keep = pltpu.make_async_copy(big, big_out, local.at[5])
        keep.start()
        y_to_modes(big, field, ay)
        table_x.wait()
        for r in (2, 1, 3, 0):
            n = (x + r) % 4
            fill(n, 0)
            begin(core_copy_a(n))
    if back:

        def core_copy_t():
            return remote(t.at[1 - c], t0, core_t, 0, 0, sibling)

        begin(core_copy_t())

    def one_copy_a(n, slot, device):
        return remote(sa.at[n], r1a.at[slot], one_a, n, slot, device)

    def one_copy_b(n, slot, device):
        return remote(sb.at[n], r1b.at[slot], one_b, n, slot, device)

    def sum_a(n):
        core_copy_a(n).wait_recv()
        return s[:, n, c, 0:2].astype(F32) + r0[:, n, 0:2].astype(F32)

    def sum_b(n):
        core_copy_b(n).wait_recv()
        rows = band(n)
        return s[:, :, c, 2:4, rows].astype(F32) + r0[:, :, 2:4, rows].astype(F32)

    def pass_a(r):
        n = (x + r) % 4
        sa[n] = sum_a(n).astype(BF)
        begin(one_copy_a(n, x, at_x(n)))

    def pass_b(r):
        n = (y + r) % 4
        sb[n] = sum_b(n).astype(BF)
        begin(one_copy_b(n, y, at_y(n)))

    if back:
        for r in (2, 1, 3):
            pass_a(r)
            pass_b(r)
        for d in range(8):
            begin(block_copy(d))
    else:
        for r in (2, 1, 3, 0):
            fill((x + r) % 4, 1)
            if r:
                pass_a(r)
        for r in (2, 1, 3, 0):
            begin(core_copy_b((y + r) % 4))
        for r in (2, 1, 3):
            pass_b(r)
    acca[...] = sum_a(x)
    accb[...] = sum_b(y)
    if back:

        def one_copy_t(n, slot, device):
            return remote(t1s.at[n], t1.at[slot], one_t, n, slot, device)

        core_copy_t().wait_recv()
        t1s[...] = (t[c].astype(F32) + t0[...].astype(F32)).astype(BF)
        for r in (2, 1, 3):
            n = (x + r) % 4
            begin(one_copy_t(n, x, at_x(n)))
    for r in (1, 3, 2):
        n = (x + r) % 4
        one_copy_a(n, n, at_x(n)).wait_recv()
        acca[...] = acca[...] + r1a[n].astype(F32)

    def two_copy_a(n, slot, device):
        return remote(acca.at[:, :, band(n)], r2a.at[slot], two_a, n, slot, device)

    def two_copy_b(n, slot, device):
        return remote(accb.at[:, n], r2b.at[slot], two_b, n, slot, device)

    for r in (2, 1, 3):
        n = (y + r) % 4
        begin(two_copy_a(n, y, at_y(n)))
    for r in (1, 3, 2):
        n = (y + r) % 4
        one_copy_b(n, n, at_y(n)).wait_recv()
        accb[...] = accb[...] + r1b[n].astype(F32)
    for r in (2, 1, 3):
        n = (x + r) % 4
        begin(two_copy_b(n, x, at_x(n)))
    ab[:, 0:2] = acca[:, :, band(y)]
    ab[:, 2:4] = accb[:, x]
    for r in (1, 3, 2):
        n = (y + r) % 4
        two_copy_a(n, n, at_y(n)).wait_recv()
        ab[:, 0:2] = ab[:, 0:2] + r2a[n]
    for r in (1, 3, 2):
        n = (x + r) % 4
        two_copy_b(n, n, at_x(n)).wait_recv()
        ab[:, 2:4] = ab[:, 2:4] + r2b[n]

    def three_copy(n, slot, device):
        return remote(ab.at[n // 2, :, band(n % 2, 16)], r3.at[slot], three, n, slot, device)

    for r in (2, 1, 3):
        n = (spot + r) % 4
        begin(three_copy(n, spot, at_z(n)))
    if back:

        def two_copy_t(n, slot, device):
            return remote(t2s.at[n], t2.at[slot], two_t, n, slot, device)

        total = t1s[x].astype(F32)
        for r in (1, 3, 2):
            n = (x + r) % 4
            one_copy_t(n, n, at_x(n)).wait_recv()
            total = total + t1[n].astype(F32)
        t2s[...] = total.astype(BF)
        for r in (2, 1, 3):
            n = (y + r) % 4
            begin(two_copy_t(n, y, at_y(n)))
    u[...] = ab[zl, :, band(zh, 16)]
    for r in (1, 3, 2):
        n = (spot + r) % 4
        three_copy(n, n, at_z(n)).wait_recv()
        u[...] = u[...] + r3[n]
    if back:
        u[...] = u[...] * math.sqrt(NX * NY / (MX * MY))
    weights.wait()
    same = iota((16, 16), 0) ^ 1
    turn = jnp.where(iota((16, 16), 1) == same, 1.0, 0.0)
    odd = (iota((16, 16), 0) & 1) == 1
    flip = odd if back else jnp.logical_not(odd)
    turn = jnp.where(flip, -turn, turn).astype(BF)

    def mix(ky, carry):
        first = u[ky]
        high = first.astype(BF)
        low = (first - high.astype(F32)).astype(BF)
        both = jnp.concatenate([high, low], axis=0)
        turned = jnp.concatenate([dot(turn, high), dot(turn, low)], axis=0).astype(BF)
        both = jnp.concatenate([both, turned], axis=1)
        total = jnp.zeros((16, C), F32)
        for kx in range(8):
            if back:
                mat = jnp.concatenate([wv[0, kx, ky], wv[1, kx, ky]], axis=1).astype(BF)
                res = dot_tb(both, mat)
            else:
                mat = jnp.concatenate([wv[0, kx, ky], wv[1, kx, ky]], axis=0).astype(BF)
                res = dot(both, mat)
            total = jnp.where((iota((16, C), 0) >> 1) == kx, res[:16] + res[16:], total)
        zs[ky] = total.astype(BF)
        return carry

    lax.fori_loop(0, 4, mix, 0)

    def wide_copy3(slot, sent, device):
        dst = zz.at[slot // 2, :, band(slot % 2, 16)]
        return remote(zs, dst, wide3, sent, slot, device)

    for r in (2, 1, 3):
        n = (spot + r) % 4
        begin(wide_copy3(spot, n, at_z(n)))
    zz[zl, :, band(zh, 16)] = zs[...]
    if back:
        t3s[...] = t2s[y]
        total = t3s[...].astype(F32)
        for r in (1, 3, 2):
            n = (y + r) % 4
            two_copy_t(n, n, at_y(n)).wait_recv()
            total = total + t2[n].astype(F32)
        t3s[...] = total.astype(BF)
        t3[spot] = t3s[...]

        def three_copy_t(slot, sent, device):
            return remote(t3s, t3.at[slot], three_t, sent, slot, device)

        for r in (2, 1, 3):
            n = (spot + r) % 4
            begin(three_copy_t(spot, n, at_z(n)))
    for r in (1, 3, 2):
        n = (spot + r) % 4
        wide_copy3(n, n, at_z(n)).wait_recv()

    def wide_copy2_a(slot, sent, device):
        return remote(zz.at[:, 0:2], za.at[:, :, band(slot)], wide2_a, sent, slot, device)

    def wide_copy2_b(slot, sent, device):
        return remote(zz.at[:, 2:4], zb.at[:, slot], wide2_b, sent, slot, device)

    for r in (2, 1, 3):
        n = (y + r) % 4
        begin(wide_copy2_a(y, n, at_y(n)))
        n = (x + r) % 4
        begin(wide_copy2_b(x, n, at_x(n)))
    za[:, :, band(y)] = zz[:, 0:2]
    zb[:, x] = zz[:, 2:4]

    def part_a(n, core):
        return z.at[:, n, core, 0:2]

    def part_b(n, core):
        return z.at[:, :, core, 2:4, band(n)]

    def wide_copy1_a(slot, sent, device):
        return remote(za, part_a(slot, c), wide1_a, sent, slot, device)

    def wide_copy1_b(slot, sent, device):
        return remote(zb, part_b(slot, c), wide1_b, sent, slot, device)

    for r in (1, 3, 2):
        n = (y + r) % 4
        wide_copy2_a(n, n, at_y(n)).wait_recv()
    for r in (2, 1, 3):
        n = (x + r) % 4
        begin(wide_copy1_a(x, n, at_x(n)))
    for r in (1, 3, 2):
        n = (x + r) % 4
        wide_copy2_b(n, n, at_x(n)).wait_recv()
    for r in (2, 1, 3):
        n = (y + r) % 4
        begin(wide_copy1_b(y, n, at_y(n)))
    own_a = pltpu.make_async_copy(za, part_a(x, c), local.at[1])
    own_a.start()
    own_b = pltpu.make_async_copy(zb, part_b(y, c), local.at[2])
    own_b.start()
    begin(remote(za, part_a(x, c), share_a, x, x, sibling))
    begin(remote(zb, part_b(y, c), share_b, y, y, sibling))
    if back:
        for r in (1, 3, 2):
            n = (spot + r) % 4
            three_copy_t(n, n, at_z(n)).wait_recv()
        total = t3[0].astype(F32)
        for n in range(1, 4):
            total = total + t3[n].astype(F32)
        tall[x, y] = total.astype(BF)

        def wide_copy2_t(slot, sent, device):
            piece = tall.at[x, slot]
            return remote(piece, piece, wide2_t, sent, slot, device)

        for r in (2, 1, 3):
            n = (y + r) % 4
            begin(wide_copy2_t(y, n, at_y(n)))
        for r in (1, 3, 2):
            n = (y + r) % 4
            wide_copy2_t(n, n, at_y(n)).wait_recv()

        def wide_copy1_t(slot, sent, device):
            piece = tall.at[slot]
            return remote(piece, piece, wide1_t, sent, slot, device)

        for r in (2, 1, 3):
            n = (x + r) % 4
            begin(wide_copy1_t(x, n, at_x(n)))

    def share_copy_a(n, core):
        return remote(part_a(n, core), part_a(n, core), share_a, n, n, sibling)

    def share_copy_b(n, core):
        return remote(part_b(n, core), part_b(n, core), share_b, n, n, sibling)

    for r in (1, 3, 2):
        n = (x + r) % 4
        wide_copy1_a(n, n, at_x(n)).wait_recv()
        begin(share_copy_a(n, c))
        n = (y + r) % 4
        wide_copy1_b(n, n, at_y(n)).wait_recv()
        begin(share_copy_b(n, c))
    if back:
        for r in (1, 3, 2):
            n = (x + r) % 4
            wide_copy1_t(n, n, at_x(n)).wait_recv()
        share = remote(tall, to.at[c], share_t, 0, 0, sibling)
        begin(share)
        own_t = pltpu.make_async_copy(tall, to.at[c], local.at[3])
        own_t.start()
    for n in range(4):
        share_copy_a(n, 1 - c).wait_recv()
        share_copy_b(n, 1 - c).wait_recv()
    for d in range(8):
        block_copy(d).wait_recv()
    own_a.wait()
    own_b.wait()
    if back:
        share.wait_recv()
        own_t.wait()
    else:
        keep.wait()
    for copy in waits:
        copy.wait_send()


def exchange(back, *operands):
    shape = jax.ShapeDtypeStruct
    out_shape = [shape((2, 4, 2, 4, 128, C), BF), shape((8, 400, C), BF), shape((4, 16, C), F32)]
    out_specs = [HB, HB, VM, HB]
    if back:
        out_shape.append(shape((2, 4, 4, PIECE, C), BF))
        in_specs = [VM, HB, HB, VM]
    else:
        out_shape.append(shape((1024, 640), BF))
        in_specs = [SM, VM, HB, HB, HB]
    sem = pltpu.SemaphoreType.DMA((2, 4))
    scratch = [
        pltpu.VMEM((2, 4, 4, 128, C), BF),
        pltpu.VMEM((4, 2, 2, 128, C), BF),
        pltpu.VMEM((4, 2, 4, 2, 32, C), BF),
        pltpu.VMEM((4, 2, 2, 128, C), BF),
        pltpu.VMEM((4, 2, 4, 2, 32, C), BF),
        pltpu.VMEM((2, 2, 128, C), F32),
        pltpu.VMEM((2, 4, 2, 32, C), F32),
        pltpu.VMEM((4, 2, 2, 32, C), F32),
        pltpu.VMEM((4, 2, 2, 32, C), F32),
        pltpu.VMEM((2, 4, 32, C), F32),
        pltpu.VMEM((4, 4, 16, C), F32),
        pltpu.VMEM((4, 16, C), BF),
        pltpu.VMEM((2, 4, 32, C), BF),
        pltpu.VMEM((2, 2, 128, C), BF),
        pltpu.VMEM((2, 4, 2, 32, C), BF),
        pltpu.VMEM((2, 8, 4, C, C), F32),
    ]
    scratch += [sem] * 14 + [pltpu.SemaphoreType.DMA((2, 8)), pltpu.SemaphoreType.DMA((6,))]
    if back:
        scratch += [
            pltpu.VMEM((4, 4, PIECE, C), BF),
            pltpu.VMEM((4, 4, PIECE, C), BF),
            pltpu.VMEM((4, 4, PIECE, C), BF),
            pltpu.VMEM((4, PIECE, C), BF),
            pltpu.VMEM((4, PIECE, C), BF),
            pltpu.VMEM((PIECE, C), BF),
            pltpu.VMEM((4, PIECE, C), BF),
            pltpu.VMEM((4, 4, PIECE, C), BF),
        ] + [sem] * 7
    else:
        scratch += [
            pltpu.VMEM((2, 4, 2, 4, 128, C), BF),
            pltpu.VMEM((8, 400, C), BF),
            pltpu.VMEM((1024, 640), BF),
            pltpu.VMEM((10, 128, 8, C), F32),
            pltpu.VMEM((SIDE + 60, 88, C), F32),
            pltpu.VMEM((408, C), F32),
            pltpu.VMEM((128, SIDE), BF),
            pltpu.VMEM((128, 480), BF),
        ]
    return pl.pallas_call(
        functools.partial(exchange_kernel, back),
        out_shape=tuple(out_shape),
        in_specs=in_specs,
        out_specs=tuple(out_specs),
        scratch_shapes=scratch,
        compiler_params=pltpu.CompilerParams(
            collective_id=2 if back else 1,
            has_side_effects=True,
            vmem_limit_bytes=VMEM_LIMIT,
        ),
        name="exchange_back" if back else "exchange",
    )(*operands)


def gelu_both(v):
    square = v * v
    t = jnp.tanh(v * (TANH_SCALE + (TANH_SCALE * CUBIC_TERM) * square))
    half = 0.5 + 0.5 * t
    inner = (0.5 * TANH_SCALE) + (1.5 * TANH_SCALE * CUBIC_TERM) * square
    return v * half, half + v * (1.0 - t * t) * inner


def middle_kernel(
    field, cot, z, blk, skip, ctx, up, down, gy, gx, tx, big_in,
    layer, pre_out, s_out, tot, bgrad,
    p, ay, cells_big, spread, gather, coarse, cell, pre, slope, mid, lifted, dh, hid, lg,
    acc_skip, acc_up, acc_down,
):
    step = pl.program_id(0)
    row, col = lax.axis_index("px"), lax.axis_index("py")

    @pl.when(step == 0)
    def _():
        x_to_cells(gx[row], z, p)
        build_to_cells(gy[col], cells_big)
        total = dot(blk[0], ctx[0])
        for d in range(1, 8):
            total = total + dot(blk[d], ctx[d])
        coarse[...] = total
        n, l = iota((1280, 160), 0), iota((1280, 160), 1)
        l = jnp.where(l >= 80, l - 80, l)
        x = over_80(n)
        y = n - 80 * x
        a = over_20(l)
        hit = ((x >> 2) == a) & ((y >> 2) == l - 20 * a)
        spread[...] = jnp.where(hit, 1.0, 0.0).astype(BF)
        l, n = iota((80, 1280), 0), iota((80, 1280), 1)
        x = over_80(n)
        y = n - 80 * x
        a = over_20(l)
        hit = ((x >> 2) == a) & ((y >> 2) == l - 20 * a)
        gather[...] = jnp.where(hit, 1.0, 0.0).astype(BF)
        acc_skip[...] = jnp.zeros_like(acc_skip)
        acc_up[...] = jnp.zeros_like(acc_up)
        acc_down[...] = jnp.zeros_like(acc_down)

    own_rows = pl.ds(pl.multiple_of(80 * step, 8), 80)
    flat = field[...].reshape(1280, C)
    flat_cot = cot[...].reshape(1280, C)
    wide = jnp.concatenate(
        [p[2 * step].reshape(1024, C).astype(BF), p[2 * step + 1].reshape(1024, C).astype(BF)],
        axis=1,
    )
    spectral = dot(cells_big[...], wide)
    own = coarse[own_rows]
    high = own.astype(BF)
    low = (own - high.astype(F32)).astype(BF)
    rest = dot(flat, skip[...]) + dot(spread[...], jnp.concatenate([high, low], axis=0))
    pre[pl.ds(0, 640)] = spectral[:, :C].astype(BF).astype(F32) + rest[:640]
    pre[pl.ds(640, 640)] = spectral[:, C:].astype(BF).astype(F32) + rest[640:]

    def activate(n, carry):
        rows = pl.ds(pl.multiple_of(64 * n, 64), 64)
        value, slant = gelu_both(pre[rows])
        mid[rows] = value.astype(BF)
        slope[rows] = slant
        return carry

    lax.fori_loop(0, 20, activate, 0, unroll=2)
    lifted[...] = dot(mid[...], up[...])
    dh[...] = dot_tb(flat_cot, down[...])

    def activate_wide(n, carry):
        rows = pl.ds(pl.multiple_of(16 * n, 16), 16)
        value, slant = gelu_both(lifted[rows])
        hid[rows] = value.astype(BF)
        lg[rows] = (dh[rows] * slant).astype(BF)
        return carry

    lax.fori_loop(0, 80, activate_wide, 0, unroll=8)
    result = mid[...].astype(F32) + dot(hid[...], down[...])
    layer[...] = result.astype(BF).reshape(16, SIDE, C)
    grad = flat_cot.astype(F32) + dot_tb(lg[...], up[...])
    grad = (grad * slope[...]).astype(BF)
    pre_out[...] = grad.reshape(16, SIDE, C)
    acc_skip[...] += dot_ta(flat, grad)
    acc_up[...] += dot_ta(mid[...], lg[...])
    acc_down[...] += dot_ta(flat_cot, hid[...])
    cell[own_rows] = dot(gather[...], grad)
    y_store(dot(big_in[...], jnp.concatenate([grad[:640], grad[640:]], axis=1)), ay, step)

    @pl.when(step == 4)
    def _():

        def modes_step(pair, carry):
            first, second = x_to_modes(tx[row], ay, (2 * pair, 2 * pair + 1))
            s_out[2 * pair] = first
            s_out[2 * pair + 1] = second
            return carry

        lax.fori_loop(0, 32, modes_step, 0, unroll=4)
        narrow = cell[...].astype(BF)
        tot[pl.ds(0, 128)] = acc_skip[...].astype(BF)
        for d in range(8):
            tot[pl.ds(128 + 128 * d, 128)] = dot_ta(blk[d], narrow).astype(BF)
            bgrad[d] = dot_tb(narrow, ctx[d]).astype(BF)
        for part in range(4):
            cut = slice(128 * part, 128 * part + 128)
            tot[pl.ds(1152 + 128 * part, 128)] = acc_up[:, cut].astype(BF)
            tot[pl.ds(1664 + 128 * part, 128)] = acc_down[:, cut].T.astype(BF)
        tot[pl.ds(2176, TOT - 2176)] = jnp.zeros((TOT - 2176, C), BF)


def whole(*shape):
    zeros = (0,) * len(shape)
    return pl.BlockSpec(shape, lambda n: zeros)


def middle_call(field, cot, z, blk, skip, ctx, up, down, gy, gx, tx, big):
    shape = jax.ShapeDtypeStruct
    tile = pl.BlockSpec((16, SIDE, C), lambda n: (n, 0, 0))
    return pl.pallas_call(
        middle_kernel,
        grid=(5,),
        out_shape=(
            shape((SIDE, SIDE, C), BF),
            shape((SIDE, SIDE, C), BF),
            shape((64, 128, C), BF),
            shape((TOT, C), BF),
            shape((8, 400, C), BF),
        ),
        in_specs=[
            tile, tile, whole(64, 128, C), whole(8, 400, C), whole(C, C), whole(8, C, C),
            whole(C, H), whole(H, C), whole(COLS, SIDE, 128), whole(ROWS, 160, 256),
            whole(ROWS, 128, 480), whole(1024, 640),
        ],
        out_specs=(tile, tile, whole(64, 128, C), whole(TOT, C), whole(8, 400, C)),
        scratch_shapes=[
            pltpu.VMEM((10, 128, 8, C), F32),
            pltpu.VMEM((10, 128, 8, C), F32),
            pltpu.VMEM((640, 1024), BF),
            pltpu.VMEM((1280, 160), BF),
            pltpu.VMEM((80, 1280), BF),
            pltpu.VMEM((400, C), F32),
            pltpu.VMEM((400, C), F32),
            pltpu.VMEM((1280, C), F32),
            pltpu.VMEM((1280, C), F32),
            pltpu.VMEM((1280, C), BF),
            pltpu.VMEM((1280, H), F32),
            pltpu.VMEM((1280, H), F32),
            pltpu.VMEM((1280, H), BF),
            pltpu.VMEM((1280, H), BF),
            pltpu.VMEM((C, C), F32),
            pltpu.VMEM((C, H), F32),
            pltpu.VMEM((C, H), F32),
        ],
        compiler_params=pltpu.CompilerParams(vmem_limit_bytes=VMEM_LIMIT),
        name="cells",
    )(field, cot, z, blk, skip, ctx, up, down, gy, gx, tx, big)


def last_kernel(picks, pre, z, back, skip, gy, gx, out, p, cells_big, place, grads, wide):
    step = pl.program_id(0)
    row, col = lax.axis_index("px"), lax.axis_index("py")
    starts = [start_of(pick_of(picks, row, col, d)) for d in range(8)]

    @pl.when(step == 0)
    def _():
        x_to_cells(gx[row], z, p)
        build_to_cells(gy[col], cells_big)
        y, lane = iota((SIDE, 192), 0), iota((SIDE, 192), 1)
        total = jnp.zeros((SIDE, 192), F32)
        for d in range(8):
            depth, sx, sy = starts[d]
            share = jnp.where(depth == 0, 1.0, jnp.where(depth == 1, 0.25, 0.0625))
            spot = lane - 24 * d
            line = jnp.where(depth == 0, y, jnp.where(depth == 1, y >> 1, y >> 2))
            hit = (spot >= 0) & (spot < BLK) & (line - sy == spot)
            total = jnp.where(hit, share, total)
        place[...] = total.astype(BF)
        wide[pl.ds(400, 8)] = jnp.zeros((8, C), F32)
        for d in range(8):
            wide[pl.ds(0, 400)] = back[d].astype(F32)
            for a in range(BLK):
                grads[d, a] = wide[pl.ds(BLK * a, 24)]
            grads[d, BLK] = jnp.zeros((24, C), F32)

    both = jnp.concatenate(
        [p[2 * step].reshape(1024, C).astype(BF), p[2 * step + 1].reshape(1024, C).astype(BF)],
        axis=1,
    )
    factor = math.sqrt(MX * MY / (NX * NY))
    spectral = dot(cells_big[...], both) * factor
    straight = dot_tb(pre[...].reshape(1280, C), skip[...])
    for x in range(16):
        pieces = []
        for d in range(8):
            depth, sx, sy = starts[d]
            a = ((16 * step + x) >> depth) - sx
            a = jnp.where((a >= 0) & (a < BLK), a, BLK)
            pieces.append(grads[d, a])
        context = dot(place[...], jnp.concatenate(pieces, axis=0).astype(BF))
        h, k = x // 8, x % 8
        total = spectral[80 * k : 80 * k + 80, C * h : C * h + C]
        total = total + straight[80 * x : 80 * x + 80] + context
        out[x] = total.astype(BF)


def last_call(picks, pre, z, back, skip, gy, gx):
    tile = pl.BlockSpec((16, SIDE, C), lambda n: (n, 0, 0))
    return pl.pallas_call(
        last_kernel,
        grid=(5,),
        out_shape=jax.ShapeDtypeStruct((SIDE, SIDE, C), BF),
        in_specs=[
            SM, tile, whole(64, 128, C), whole(8, 400, C), whole(C, C),
            whole(COLS, SIDE, 128), whole(ROWS, 160, 256),
        ],
        out_specs=tile,
        scratch_shapes=[
            pltpu.VMEM((10, 128, 8, C), F32),
            pltpu.VMEM((640, 1024), BF),
            pltpu.VMEM((SIDE, 192), BF),
            pltpu.VMEM((8, BLK + 1, 24, C), F32),
            pltpu.VMEM((408, C), F32),
        ],
        compiler_params=pltpu.CompilerParams(vmem_limit_bytes=VMEM_LIMIT),
        name="field_gradient",
    )(picks, pre, z, back, skip, gy, gx)


def outer_kernel(u, g, tot, spec, skip, ctx, up, down):
    kx = pl.program_id(0)
    mask = (iota((16, C), 0) >> 1) == kx
    turn = jnp.where(iota((16, 16), 1) == (iota((16, 16), 0) ^ 1), 1.0, 0.0)
    turn = jnp.where((iota((16, 16), 0) & 1) == 1, -turn, turn)
    for ky in range(4):
        left = jnp.where(mask, u[ky], 0.0)
        left_high = left.astype(BF)
        left_low = (left - left_high.astype(F32)).astype(BF)
        right = g[ky]
        right_high = right.astype(BF)
        right_low = (right - right_high.astype(F32)).astype(BF)
        narrow = turn.astype(BF)
        high = jnp.concatenate([right_high, dot(narrow, right_high).astype(BF)], axis=1)
        low = jnp.concatenate([right_low, dot(narrow, right_low).astype(BF)], axis=1)
        lefts = jnp.concatenate([left_high, left_high, left_low], axis=0)
        rights = jnp.concatenate([high, low, high], axis=0)
        res = dot_ta(lefts, rights)
        spec[0, 0, ky] = res[:, :C]
        spec[1, 0, ky] = res[:, C:]

    @pl.when(kx == 0)
    def _():
        inv = 1.0 / math.sqrt(NX * NY)
        skip[...] = tot[pl.ds(0, 128)].astype(F32) * inv
        for d in range(8):
            ctx[d] = tot[pl.ds(128 + 128 * d, 128)].astype(F32) * inv
        for part in range(4):
            cut = slice(128 * part, 128 * part + 128)
            up[:, cut] = tot[pl.ds(1152 + 128 * part, 128)].astype(F32) * inv
        down[...] = tot[pl.ds(1664, 512)].astype(F32) * inv


def outer_call(u, g, tot):
    shape = jax.ShapeDtypeStruct
    return pl.pallas_call(
        outer_kernel,
        grid=(8,),
        out_shape=(
            shape((2, 8, 4, C, C), F32),
            shape((C, C), F32),
            shape((8, C, C), F32),
            shape((C, H), F32),
            shape((H, C), F32),
        ),
        in_specs=[whole(4, 16, C), whole(4, 16, C), whole(TOT, C)],
        out_specs=(
            pl.BlockSpec((2, 1, 4, C, C), lambda n: (0, n, 0, 0, 0)),
            whole(C, C),
            whole(8, C, C),
            whole(C, H),
            whole(H, C),
        ),
        compiler_params=pltpu.CompilerParams(vmem_limit_bytes=VMEM_LIMIT),
        name="weight_gradients",
    )(u, g, tot)


def shards(
    flow_field, cotangent, spec_weight, skip_weight, ctx_weight, up_weight, down_weight,
    ctx_level, ctx_offset,
):
    ty, gy, tx, gx = (jnp.asarray(t) for t in wave_tables())
    picks = ctx_level + (ctx_offset[:, :, 0] << 2) + (ctx_offset[:, :, 1] << 9)
    z, arrived, u, big = exchange(False, picks, flow_field, ty, tx, spec_weight)
    layer, pre, s, tot, bgrad = middle_call(
        flow_field, cotangent, z.reshape(64, 128, C), arrived, skip_weight, ctx_weight,
        up_weight, down_weight, gy, gx, tx, big,
    )
    tot = tot.reshape(2, 4, 4, PIECE, C)
    s = s.reshape(2, 4, 2, 4, 128, C)
    z, back, g, tot = exchange(True, s, bgrad, spec_weight, tot)
    spec, skip, ctx, up, down = outer_call(u, g, tot.reshape(TOT, C))
    grad = last_call(picks, pre, z.reshape(64, 128, C), back, skip_weight, gy, gx)
    return layer, grad, spec, skip, ctx, up, down


def solution(mesh):
    return jax.shard_map(
        shards,
        mesh=mesh,
        in_specs=(
            P("px", "py", None),
            P("px", "py", None),
            P(None, "px", "py", None, None),
            P(),
            P(),
            P(),
            P(),
            P(),
            P(),
        ),
        out_specs=(
            P("px", "py", None),
            P("px", "py", None),
            P(None, "px", "py", None, None),
            P(),
            P(),
            P(),
            P(),
        ),
        check_vma=False,
    )
```

time: 222 us -> 176 us (0.79)
  Pallas kernels: 217 us -> 173 us
    pallas_call x1 -> x0, Pallas kernels: 16.3 us -> none  [first_call(): pl.pallas_call(first_kernel, out_shape=(jax.ShapeDtypeStruct((64, 128, C)...]
    pallas_call x2, Pallas kernels: 128 us -> 112 us  [exchange(): pl.pallas_call(functools.partial(exchange_kernel, back), out_shape=tuple(...]
    pallas_call x1, Pallas kernels: 51.5 us -> 43.6 us  [middle_call(): pl.pallas_call(middle_kernel, grid=(5,), out_shape=(shape((SIDE, SIDE, C)...]
    pallas_call x1, Pallas kernels: 14.5 us -> 10.7 us  [last_call(): pl.pallas_call(last_kernel, grid=(5,), out_shape=jax.ShapeDtypeStruct((SI...]
where the time goes in v2:
time: 176 us
  Pallas kernels  173 us (98%)
  local copies, waits for them, and re-layouts  1.77 us (1%)
    pallas_call x2, Pallas kernels, exchange(): pl.pallas_call(functools.partial(exchange_kernel, back), out_shape=tuple(...  112 us
    pallas_call x1, Pallas kernels, middle_call(): pl.pallas_call(middle_kernel, grid=(5,), out_shape=(shape((SIDE, SIDE, C)...  43.6 us
    pallas_call x1, Pallas kernels, last_call(): pl.pallas_call(last_kernel, grid=(5,), out_shape=jax.ShapeDtypeStruct((SI...  10.7 us
    pallas_call x1, Pallas kernels, outer_call(): pl.pallas_call(outer_kernel, grid=(8,), out_shape=(shape((2, 8, 4, C, C),...  7.03 us

profile of v2, /device:TPU:1, one launch (start us, length us, event | category | flops | bytes accessed | tf_op | source)
XLA Modules:
  0.0 176.0 jit_solution(7336288394078973481)
XLA Ops:
  0.6 0.8 fusion
  1.4 0.1 copy.20
  1.5 0.1 copy.22
  1.6 0.8 copy.21
  2.4 0.6 bitcast_add_fusion.refs_0_.picks
  3.0 56.9 %exchange.1 = (bf16[2,4,2,4,128,128]{5,4,3,2,1,0:T(8,128)(2,1)}, bf16[8,400,128]{2,1,0:T(8,128)(2,1)}, f32[4,16,128]{2,1,0:T(8,128)}, bf16[1024,640]{1,0:T(8,128)(2,1)}) custom-call(s32[128,8]{1,0:T(8,128)} %bitcast_add_fusion.refs_0_.picks, bf16[80,80,128]{2,1,0:T(8,128)(2,1)} %field.1, bf16[16,128,80]{2,1,0:T(8,128)(2,1)} %constant.12.clone.refs_2_, ...), custom_call_target="tpu_custom_call" | custom-call | tf_op jit(solution)/shard_map/exchange/pallas_call | solution.py:649
  59.9 43.6 %cells.1 = (bf16[80,80,128]{2,1,0:T(8,128)(2,1)}, bf16[80,80,128]{2,1,0:T(8,128)(2,1)}, bf16[64,128,128]{2,1,0:T(8,128)(2,1)}, bf16[2560,128]{1,0:T(8,128)(2,1)}, bf16[8,400,128]{2,1,0:T(8,128)(2,1)}) custom-call(bf16[80,80,128]{2,1,0:T(8,128)(2,1)} %field.1, bf16[80,80,128]{2,1,0:T(8,128)(2,1)} %cot.1, bf16[64,128,128]{2,1,0:T(8,128)(2,1)} %bitcast.11, ...), custom_call_target="tpu_custom_call" | custom-call | tf_op jit(solution)/shard_map/cells/pallas_call | solution.py:781
  103.5 54.7 %exchange_back.1 = (bf16[2,4,2,4,128,128]{5,4,3,2,1,0:T(8,128)(2,1)}, bf16[8,400,128]{2,1,0:T(8,128)(2,1)}, f32[4,16,128]{2,1,0:T(8,128)}, bf16[2,4,4,80,128]{4,3,2,1,0:T(8,128)(2,1)}) custom-call(bf16[2,4,2,4,128,128]{5,4,3,2,1,0:T(8,128)(2,1)} %bitcast.13, bf16[8,400,128]{2,1,0:T(8,128)(2,1)} %get-tuple-element.31.refs_1_, f32[2,8,4,128,128]{4,3,2,1,0:T(8,128)} %refs_2_.2, ...), custom_call_target="tpu_custom_call" | custom-call | tf_op jit(solution)/shard_map/exchange_back/pallas_call | solution.py:649
  158.2 10.7 %field_gradient.1 = bf16[80,80,128]{2,1,0:T(8,128)(2,1)} custom-call(s32[128,8]{1,0:T(8,128)} %bitcast_add_fusion.refs_0_.picks, bf16[80,80,128]{2,1,0:T(8,128)(2,1)} %get-tuple-element.29.pre, bf16[64,128,128]{2,1,0:T(8,128)(2,1)} %bitcast.12, bf16[8,400,128]{2,1,0:T(8,128)(2,1)} %get-tuple-element.34.back, bf16[128,128]{1,0:T(8,128)(2,1)} %skip.3, ...), custom_call_target="tpu_custom_call" | custom-call | tf_op jit(solution)/shard_map/field_gradient/pallas_call | solution.py:870
  168.9 7.0 %weight_gradients.1 = (f32[2,8,4,128,128]{4,3,2,1,0:T(8,128)}, f32[128,128]{1,0:T(8,128)}, f32[8,128,128]{2,1,0:T(8,128)}, f32[128,512]{1,0:T(8,128)}, f32[512,128]{1,0:T(8,128)}) custom-call(f32[4,16,128]{2,1,0:T(8,128)} %get-tuple-element.35.u, f32[4,16,128]{2,1,0:T(8,128)} %get-tuple-element.36.g, bf16[2560,128]{1,0:T(8,128)(2,1)} %bitcast.14), custom_call_target="tpu_custom_call" | custom-call | tf_op jit(solution)/shard_map/weight_gradients/pallas_call | solution.py:926

commit v3 on v2

v3 whole, which is shorter than its diff:
```python
import functools
import math

import jax
import jax.numpy as jnp
import ml_dtypes
import numpy as np
from jax import lax
from jax.experimental import pallas as pl
from jax.experimental.pallas import tpu as pltpu
from jax.sharding import PartitionSpec as P

BF = jnp.bfloat16
F32 = jnp.float32
TANH_SCALE = 0.7978845608028654
CUBIC_TERM = 0.044715
STEP_ROWS = (-1, -1, -1, 0, 0, 1, 1, 1)
STEP_COLS = (-1, 0, 1, -1, 1, -1, 0, 1)
ROWS, COLS = 8, 16
SIDE, C, H, BLK = 80, 128, 512, 20
NX, NY, MX, MY = 640, 1280, 64, 64
PIECE = 80
TOT = 32 * PIECE
VMEM_LIMIT = 56 * 1024 * 1024
MESH = pl.DeviceIdType.MESH
VM = pl.BlockSpec(memory_space=pltpu.VMEM)
SM = pl.BlockSpec(memory_space=pltpu.SMEM)
HB = pl.BlockSpec(memory_space=pl.ANY)


def wave_tables():
    waves = np.arange(64) - 32

    def parts(length, side):
        turns = (np.arange(length)[:, None] * waves[None, :]) % length
        phase = turns * (2.0 * math.pi / length)
        return np.cos(phase).reshape(-1, side, 64), np.sin(phase).reshape(-1, side, 64)

    cos_y, sin_y = parts(NY, SIDE)
    cos_x, sin_x = parts(NX, SIDE)
    to_modes_y = np.stack([cos_y, -sin_y], axis=-1).reshape(COLS, SIDE, 128) / math.sqrt(NY)
    to_modes_y = to_modes_y.transpose(0, 2, 1)
    to_cells_y = np.stack([cos_y, -sin_y], axis=-1).reshape(COLS, SIDE, 128) / math.sqrt(MY)
    cx, sx = cos_x.transpose(0, 2, 1), -sin_x.transpose(0, 2, 1)
    real = np.concatenate([cx, -sx], axis=2)
    imag = np.concatenate([sx, cx], axis=2)
    to_modes_x = np.stack([real, imag], axis=2).reshape(ROWS, 128, 2 * SIDE) / math.sqrt(NX)
    real = np.stack([cos_x, -sin_x], axis=-1).reshape(ROWS, SIDE, 128)
    imag = np.stack([sin_x, cos_x], axis=-1).reshape(ROWS, SIDE, 128)
    to_cells_x = np.concatenate([real, imag], axis=1) / math.sqrt(MX)

    def rounded(t):
        return np.ascontiguousarray(t).astype(ml_dtypes.bfloat16)

    def rest(t):
        return rounded(t - rounded(t).astype(np.float64))

    high, low = rounded(to_modes_x), rest(to_modes_x)
    wide_modes_x = np.concatenate([high, low, high], axis=2)
    wide_cells_x = np.concatenate([rounded(to_cells_x), rest(to_cells_x)], axis=2)
    return rounded(to_modes_y), rounded(to_cells_y), wide_modes_x, wide_cells_x


def iota(shape, axis):
    return lax.broadcasted_iota(jnp.int32, shape, axis)


def dot(a, b):
    return jnp.dot(a, b, preferred_element_type=F32)


def dot_tb(a, b):
    return lax.dot_general(a, b, (((1,), (1,)), ((), ())), preferred_element_type=F32)


def dot_ta(a, b):
    return lax.dot_general(a, b, (((0,), (0,)), ((), ())), preferred_element_type=F32)


def over_80(v):
    return (v * 52429) >> 22


def over_20(v):
    return (v * 52429) >> 20


def build_to_modes(table, big_ref):
    lane = iota((SIDE, 640), 1)
    tile = (lane - 80 * over_80(lane) == iota((SIDE, 640), 0)).astype(F32).astype(BF)
    for part in range(8):
        rep = ((iota((128, 128), 0) >> 3) + 16 * part == iota((128, 128), 1)).astype(F32)
        rows = dot(dot(rep.astype(BF), table).astype(BF), tile)
        mask = (iota((128, 640), 0) & 7) == over_80(iota((128, 640), 1))
        big_ref[pl.ds(128 * part, 128), :] = jnp.where(mask, rows, 0.0).astype(BF)


def build_to_cells(table, big_ref):
    rep = ((iota((128, 1024), 1) >> 3) == iota((128, 1024), 0)).astype(F32)
    wide = dot(table, rep.astype(BF))
    lane = iota((SIDE, 1024), 1) & 7
    for x in range(8):
        big_ref[pl.ds(SIDE * x, SIDE), :] = jnp.where(lane == x, wide, 0.0).astype(BF)


def x_to_modes(table, ay_ref, kys):
    wide = []
    for ky in kys:
        both = [ay_ref[:, 2 * ky + r].reshape(SIDE, C) for r in range(2)]
        high = [v.astype(BF) for v in both]
        low = [(v - h.astype(F32)).astype(BF) for v, h in zip(both, high)]
        wide.append(jnp.concatenate(high + high + low, axis=0))
    modes = dot(table, jnp.concatenate(wide, axis=1)).astype(BF)
    return modes[:, :C], modes[:, C:]


def x_to_cells(table, z_ref, p_ref):
    def step(pair, carry):
        wide = jnp.concatenate([z_ref[2 * pair], z_ref[2 * pair + 1]], axis=1)
        cells = dot(table, jnp.concatenate([wide, wide], axis=0))
        for h in range(2):
            for r in range(2):
                piece = cells[r * SIDE : (r + 1) * SIDE, h * C : (h + 1) * C]
                p_ref[:, 2 * (2 * pair + h) + r] = piece.reshape(10, 8, C)
        return carry

    lax.fori_loop(0, 32, step, 0, unroll=16)


def y_store(big, pair_cells, ay_ref, pair):
    for part in range(4):
        modes = dot(big[pl.ds(256 * part, 256)], pair_cells)
        spot = pl.ds(32 * part, 32)
        ay_ref[2 * pair, spot] = modes[:, :C].reshape(32, 8, C)
        ay_ref[2 * pair + 1, spot] = modes[:, C:].reshape(32, 8, C)


def y_to_modes(big, field, ay):
    def y_step(pair, carry):
        first = field[pl.ds(16 * pair, 8)].reshape(640, C)
        second = field[pl.ds(16 * pair + 8, 8)].reshape(640, C)
        y_store(big, jnp.concatenate([first, second], axis=1), ay, pair)
        return carry

    lax.fori_loop(0, 5, y_step, 0)


def start_of(pick):
    depth = pick & 3
    first, second = (pick >> 2) & 127, pick >> 9

    def choose(zero, one, two):
        return jnp.where(depth == 0, zero, jnp.where(depth == 1, one, two))

    last = choose(SIDE - BLK, SIDE // 2 - BLK, 0)
    sx = jnp.minimum(choose(first, first >> 1, first >> 2), last)
    sy = jnp.minimum(choose(second, second >> 1, second >> 2), last)
    return depth, sx, sy


def pick_of(picks, row, col, d):
    target = lax.rem(row - STEP_ROWS[d] + ROWS, ROWS) * COLS
    return picks[target + lax.rem(col - STEP_COLS[d] + COLS, COLS), d]


def pick_blocks(picks, row, col, field, grid, tmp, blocks):
    def widen(x, carry):
        grid[x, pl.ds(0, SIDE)] = field[x].astype(F32)
        return carry

    lax.fori_loop(0, SIDE, widen, 0, unroll=4)

    def pool1(x, carry):
        total = jnp.zeros((40, C), F32)
        for a in range(2):
            for b in range(2):
                total = total + grid[2 * x + a, pl.ds(b, 40, stride=2)]
        grid[SIDE + x, pl.ds(0, 40)] = (total * 0.25).astype(BF).astype(F32)
        return carry

    lax.fori_loop(0, 40, pool1, 0, unroll=4)

    def pool2(x, carry):
        total = jnp.zeros((20, C), F32)
        for a in range(4):
            for b in range(4):
                total = total + grid[4 * x + a, pl.ds(b, 20, stride=4)]
        grid[SIDE + 40 + x, pl.ds(0, 20)] = (total * 0.0625).astype(BF).astype(F32)
        return carry

    lax.fori_loop(0, 20, pool2, 0, unroll=4)
    for d in range(8):
        depth, sx, sy = start_of(pick_of(picks, row, col, d))
        base = sx + jnp.where(depth == 0, 0, jnp.where(depth == 1, SIDE, SIDE + 40))
        for a in range(BLK):
            tmp[pl.ds(BLK * a, 24)] = grid[base + a, pl.ds(sy, 24)]
        blocks[d] = tmp[pl.ds(0, 400)].astype(BF)


def exchange_kernel(back, *refs):
    refs = list(refs)

    def take(n):
        taken = refs[:n]
        del refs[:n]
        return taken

    if back:
        cells_in = take(10)
        tx, big_in, w = take(3)
        layer_out, pre_out, z, bo, u, to = take(6)
    else:
        picks, field, ty, tx, w = take(5)
        z, bo, u, big_out = take(4)
    r0, sa, sb, r1a, r1b, acca, accb, r2a, r2b, ab, r3, zs, zz, za, zb, wv = take(16)
    core_a, core_b, one_a, one_b, two_a, two_b, three, wide3 = take(8)
    wide2_a, wide2_b, wide1_a, wide1_b, share_a, share_b, blocks, local = take(8)
    if back:
        t0, t1s, t1, t2s, t2, t3s, t3, tall = take(8)
        core_t, one_t, two_t, three_t, wide2_t, wide1_t, share_t = take(7)
        s, b, big, ay, tx_own, t = take(6)
        step = pl.program_id(0)
    else:
        s, b, big, ay, tx_own, grid, tmp, ty_own = take(8)
    i, j = lax.axis_index("px"), lax.axis_index("py")
    y, zh = i // 2, i % 2
    zl, x, c = j // 8, (j // 2) % 4, j % 2
    spot = 2 * zl + zh
    sibling = (i, 8 * zl + 2 * x + 1 - c)

    def at_x(n):
        return (i, 8 * zl + 2 * n + c)

    def at_y(n):
        return (2 * n + zh, j)

    def at_z(n):
        return (2 * y + n % 2, 8 * (n // 2) + 2 * x + c)

    def remote(src, dst, sems, sent, landed, device):
        return pltpu.make_async_remote_copy(
            src_ref=src,
            dst_ref=dst,
            send_sem=sems.at[0, sent],
            recv_sem=sems.at[1, landed],
            device_id=device,
            device_id_type=MESH,
        )

    def neighbour(d, sign):
        return (
            (i + sign * STEP_ROWS[d] + ROWS) % ROWS,
            (j + sign * STEP_COLS[d] + COLS) % COLS,
        )

    def band(n, size=32):
        return pl.ds(pl.multiple_of(n * size, size), size)

    barrier = pltpu.get_barrier_semaphore()
    partners = [sibling]
    for r in (1, 2, 3):
        partners += [at_x((x + r) % 4), at_y((y + r) % 4), at_z((spot + r) % 4)]
    partners += [neighbour(d, 1) for d in range(8)]
    weights = pltpu.make_async_copy(w, wv, local.at[0])
    table_x = pltpu.make_async_copy(tx.at[i], tx_own, local.at[4])
    if back:
        keep = pltpu.make_async_copy(big_in, big, local.at[5])
    else:
        keep = pltpu.make_async_copy(big, big_out, local.at[5])

    def greet():
        for device in partners:
            pl.semaphore_signal(barrier, inc=1, device_id=device, device_id_type=MESH)
        weights.start()
        table_x.start()

    if back:

        @pl.when(step == 0)
        def _():
            keep.start()
            greet()

        tail = cells_body(
            step, i, j, keep, cells_in, layer_out, pre_out, ay, big, b, t, refs
        )
    else:
        greet()
        table_y = pltpu.make_async_copy(ty.at[j], ty_own, local.at[3])
        table_y.start()
        pick_blocks(picks, i, j, field, grid, tmp, b)

    def run():
        pl.semaphore_wait(barrier, len(partners))
        waits = []

        def begin(copy):
            copy.start()
            waits.append(copy)

        def core_copy_a(n):
            return remote(s.at[:, n, 1 - c, 0:2], r0.at[:, n, 0:2], core_a, n, n, sibling)

        def core_copy_b(n):
            src = s.at[:, :, 1 - c, 2:4, band(n)]
            return remote(src, r0.at[:, :, 2:4, band(n)], core_b, n, n, sibling)

        def block_copy(d):
            device = neighbour(d, 1 if back else -1)
            return remote(b.at[d], bo.at[d], blocks, d, d, device)

        def fill(n, half):
            def step(m, carry):
                a, e = m // 2, m % 2
                ky = 4 * (8 * a + 2 * n + e) + 2 * half
                first, second = x_to_modes(tx_own[...], ay, (ky, ky + 1))
                s[a, n, e, 2 * half] = first
                s[a, n, e, 2 * half + 1] = second
                return carry

            lax.fori_loop(0, 4, step, 0, unroll=4)

        if not back:
            for d in range(8):
                begin(block_copy(d))
            table_y.wait()
            build_to_modes(ty_own[...], big)
            keep.start()
            y_to_modes(big, field, ay)
        table_x.wait()
        for r in (2, 1, 3, 0):
            n = (x + r) % 4
            fill(n, 0)
            begin(core_copy_a(n))
        if back:

            def core_copy_t():
                return remote(t.at[1 - c], t0, core_t, 0, 0, sibling)

        def one_copy_a(n, slot, device):
            return remote(sa.at[n], r1a.at[slot], one_a, n, slot, device)

        def one_copy_b(n, slot, device):
            return remote(sb.at[n], r1b.at[slot], one_b, n, slot, device)

        def sum_a(n):
            core_copy_a(n).wait_recv()
            return s[:, n, c, 0:2].astype(F32) + r0[:, n, 0:2].astype(F32)

        def sum_b(n):
            core_copy_b(n).wait_recv()
            rows = band(n)
            return s[:, :, c, 2:4, rows].astype(F32) + r0[:, :, 2:4, rows].astype(F32)

        def pass_a(r):
            n = (x + r) % 4
            sa[n] = sum_a(n).astype(BF)
            begin(one_copy_a(n, x, at_x(n)))

        def pass_b(r):
            n = (y + r) % 4
            sb[n] = sum_b(n).astype(BF)
            begin(one_copy_b(n, y, at_y(n)))

        for r in (2, 1, 3, 0):
            fill((x + r) % 4, 1)
            if r:
                pass_a(r)
        for r in (2, 1, 3, 0):
            begin(core_copy_b((y + r) % 4))
        for r in (2, 1, 3):
            pass_b(r)
        if back:
            tail()
            begin(core_copy_t())
            for d in range(8):
                begin(block_copy(d))
        acca[...] = sum_a(x)
        accb[...] = sum_b(y)
        if back:

            def one_copy_t(n, slot, device):
                return remote(t1s.at[n], t1.at[slot], one_t, n, slot, device)

            core_copy_t().wait_recv()
            t1s[...] = (t[c].astype(F32) + t0[...].astype(F32)).astype(BF)
            for r in (2, 1, 3):
                n = (x + r) % 4
                begin(one_copy_t(n, x, at_x(n)))
        for r in (1, 3, 2):
            n = (x + r) % 4
            one_copy_a(n, n, at_x(n)).wait_recv()
            acca[...] = acca[...] + r1a[n].astype(F32)

        def two_copy_a(n, slot, device):
            return remote(acca.at[:, :, band(n)], r2a.at[slot], two_a, n, slot, device)

        def two_copy_b(n, slot, device):
            return remote(accb.at[:, n], r2b.at[slot], two_b, n, slot, device)

        for r in (2, 1, 3):
            n = (y + r) % 4
            begin(two_copy_a(n, y, at_y(n)))
        for r in (1, 3, 2):
            n = (y + r) % 4
            one_copy_b(n, n, at_y(n)).wait_recv()
            accb[...] = accb[...] + r1b[n].astype(F32)
        for r in (2, 1, 3):
            n = (x + r) % 4
            begin(two_copy_b(n, x, at_x(n)))
        ab[:, 0:2] = acca[:, :, band(y)]
        ab[:, 2:4] = accb[:, x]
        for r in (1, 3, 2):
            n = (y + r) % 4
            two_copy_a(n, n, at_y(n)).wait_recv()
            ab[:, 0:2] = ab[:, 0:2] + r2a[n]
        for r in (1, 3, 2):
            n = (x + r) % 4
            two_copy_b(n, n, at_x(n)).wait_recv()
            ab[:, 2:4] = ab[:, 2:4] + r2b[n]

        def three_copy(n, slot, device):
            return remote(ab.at[n // 2, :, band(n % 2, 16)], r3.at[slot], three, n, slot, device)

        for r in (2, 1, 3):
            n = (spot + r) % 4
            begin(three_copy(n, spot, at_z(n)))
        if back:

            def two_copy_t(n, slot, device):
                return remote(t2s.at[n], t2.at[slot], two_t, n, slot, device)

            total = t1s[x].astype(F32)
            for r in (1, 3, 2):
                n = (x + r) % 4
                one_copy_t(n, n, at_x(n)).wait_recv()
                total = total + t1[n].astype(F32)
            t2s[...] = total.astype(BF)
            for r in (2, 1, 3):
                n = (y + r) % 4
                begin(two_copy_t(n, y, at_y(n)))
        u[...] = ab[zl, :, band(zh, 16)]
        for r in (1, 3, 2):
            n = (spot + r) % 4
            three_copy(n, n, at_z(n)).wait_recv()
            u[...] = u[...] + r3[n]
        if back:
            u[...] = u[...] * math.sqrt(NX * NY / (MX * MY))
        weights.wait()
        same = iota((16, 16), 0) ^ 1
        turn = jnp.where(iota((16, 16), 1) == same, 1.0, 0.0)
        odd = (iota((16, 16), 0) & 1) == 1
        flip = odd if back else jnp.logical_not(odd)
        turn = jnp.where(flip, -turn, turn).astype(BF)

        def mix(ky, carry):
            first = u[ky]
            high = first.astype(BF)
            low = (first - high.astype(F32)).astype(BF)
            both = jnp.concatenate([high, low], axis=0)
            turned = jnp.concatenate([dot(turn, high), dot(turn, low)], axis=0).astype(BF)
            both = jnp.concatenate([both, turned], axis=1)
            total = jnp.zeros((16, C), F32)
            for kx in range(8):
                if back:
                    mat = jnp.concatenate([wv[0, kx, ky], wv[1, kx, ky]], axis=1).astype(BF)
                    res = dot_tb(both, mat)
                else:
                    mat = jnp.concatenate([wv[0, kx, ky], wv[1, kx, ky]], axis=0).astype(BF)
                    res = dot(both, mat)
                total = jnp.where((iota((16, C), 0) >> 1) == kx, res[:16] + res[16:], total)
            zs[ky] = total.astype(BF)
            return carry

        lax.fori_loop(0, 4, mix, 0)

        def wide_copy3(slot, sent, device):
            dst = zz.at[slot // 2, :, band(slot % 2, 16)]
            return remote(zs, dst, wide3, sent, slot, device)

        for r in (2, 1, 3):
            n = (spot + r) % 4
            begin(wide_copy3(spot, n, at_z(n)))
        zz[zl, :, band(zh, 16)] = zs[...]
        if back:
            t3s[...] = t2s[y]
            total = t3s[...].astype(F32)
            for r in (1, 3, 2):
                n = (y + r) % 4
                two_copy_t(n, n, at_y(n)).wait_recv()
                total = total + t2[n].astype(F32)
            t3s[...] = total.astype(BF)
            t3[spot] = t3s[...]

            def three_copy_t(slot, sent, device):
                return remote(t3s, t3.at[slot], three_t, sent, slot, device)

            for r in (2, 1, 3):
                n = (spot + r) % 4
                begin(three_copy_t(spot, n, at_z(n)))
        for r in (1, 3, 2):
            n = (spot + r) % 4
            wide_copy3(n, n, at_z(n)).wait_recv()

        def wide_copy2_a(slot, sent, device):
            return remote(zz.at[:, 0:2], za.at[:, :, band(slot)], wide2_a, sent, slot, device)

        def wide_copy2_b(slot, sent, device):
            return remote(zz.at[:, 2:4], zb.at[:, slot], wide2_b, sent, slot, device)

        for r in (2, 1, 3):
            n = (y + r) % 4
            begin(wide_copy2_a(y, n, at_y(n)))
            n = (x + r) % 4
            begin(wide_copy2_b(x, n, at_x(n)))
        za[:, :, band(y)] = zz[:, 0:2]
        zb[:, x] = zz[:, 2:4]

        def part_a(n, core):
            return z.at[:, n, core, 0:2]

        def part_b(n, core):
            return z.at[:, :, core, 2:4, band(n)]

        def wide_copy1_a(slot, sent, device):
            return remote(za, part_a(slot, c), wide1_a, sent, slot, device)

        def wide_copy1_b(slot, sent, device):
            return remote(zb, part_b(slot, c), wide1_b, sent, slot, device)

        for r in (1, 3, 2):
            n = (y + r) % 4
            wide_copy2_a(n, n, at_y(n)).wait_recv()
        for r in (2, 1, 3):
            n = (x + r) % 4
            begin(wide_copy1_a(x, n, at_x(n)))
        for r in (1, 3, 2):
            n = (x + r) % 4
            wide_copy2_b(n, n, at_x(n)).wait_recv()
        for r in (2, 1, 3):
            n = (y + r) % 4
            begin(wide_copy1_b(y, n, at_y(n)))
        own_a = pltpu.make_async_copy(za, part_a(x, c), local.at[1])
        own_a.start()
        own_b = pltpu.make_async_copy(zb, part_b(y, c), local.at[2])
        own_b.start()
        begin(remote(za, part_a(x, c), share_a, x, x, sibling))
        begin(remote(zb, part_b(y, c), share_b, y, y, sibling))
        if back:
            for r in (1, 3, 2):
                n = (spot + r) % 4
                three_copy_t(n, n, at_z(n)).wait_recv()
            total = t3[0].astype(F32)
            for n in range(1, 4):
                total = total + t3[n].astype(F32)
            tall[x, y] = total.astype(BF)

            def wide_copy2_t(slot, sent, device):
                piece = tall.at[x, slot]
                return remote(piece, piece, wide2_t, sent, slot, device)

            for r in (2, 1, 3):
                n = (y + r) % 4
                begin(wide_copy2_t(y, n, at_y(n)))
            for r in (1, 3, 2):
                n = (y + r) % 4
                wide_copy2_t(n, n, at_y(n)).wait_recv()

            def wide_copy1_t(slot, sent, device):
                piece = tall.at[slot]
                return remote(piece, piece, wide1_t, sent, slot, device)

            for r in (2, 1, 3):
                n = (x + r) % 4
                begin(wide_copy1_t(x, n, at_x(n)))

        def share_copy_a(n, core):
            return remote(part_a(n, core), part_a(n, core), share_a, n, n, sibling)

        def share_copy_b(n, core):
            return remote(part_b(n, core), part_b(n, core), share_b, n, n, sibling)

        for r in (1, 3, 2):
            n = (x + r) % 4
            wide_copy1_a(n, n, at_x(n)).wait_recv()
            begin(share_copy_a(n, c))
            n = (y + r) % 4
            wide_copy1_b(n, n, at_y(n)).wait_recv()
            begin(share_copy_b(n, c))
        if back:
            for r in (1, 3, 2):
                n = (x + r) % 4
                wide_copy1_t(n, n, at_x(n)).wait_recv()
            share = remote(tall, to.at[c], share_t, 0, 0, sibling)
            begin(share)
            own_t = pltpu.make_async_copy(tall, to.at[c], local.at[3])
            own_t.start()
        for n in range(4):
            share_copy_a(n, 1 - c).wait_recv()
            share_copy_b(n, 1 - c).wait_recv()
        for d in range(8):
            block_copy(d).wait_recv()
        own_a.wait()
        own_b.wait()
        if back:
            share.wait_recv()
            own_t.wait()
        else:
            keep.wait()
        for copy in waits:
            copy.wait_send()

    if back:
        pl.when(step == 4)(run)
    else:
        run()


def whole(*shape):
    zeros = (0,) * len(shape)
    return pl.BlockSpec(shape, lambda n: zeros)


def exchange(back, *operands):
    shape = jax.ShapeDtypeStruct
    out_shape = [shape((2, 4, 2, 4, 128, C), BF), shape((8, 400, C), BF), shape((4, 16, C), F32)]
    if back:
        tile = pl.BlockSpec((16, SIDE, C), lambda n: (n, 0, 0))
        field = shape((SIDE, SIDE, C), BF)
        out_shape = [field, field] + out_shape + [shape((2, 4, 4, PIECE, C), BF)]
        out_specs = [tile, tile, HB, HB, whole(4, 16, C), HB]
        in_specs = [tile, tile, whole(64, 128, C), whole(8, 400, C), whole(C, C)]
        in_specs += [whole(8, C, C), whole(C, H), whole(H, C), whole(COLS, SIDE, 128)]
        in_specs += [whole(ROWS, 160, 256), HB, HB, HB]
    else:
        out_shape.append(shape((1024, 640), BF))
        out_specs = [HB, HB, VM, HB]
        in_specs = [SM, VM, HB, HB, HB]
    sem = pltpu.SemaphoreType.DMA((2, 4))
    scratch = [
        pltpu.VMEM((2, 4, 4, 128, C), BF),
        pltpu.VMEM((4, 2, 2, 128, C), BF),
        pltpu.VMEM((4, 2, 4, 2, 32, C), BF),
        pltpu.VMEM((4, 2, 2, 128, C), BF),
        pltpu.VMEM((4, 2, 4, 2, 32, C), BF),
        pltpu.VMEM((2, 2, 128, C), F32),
        pltpu.VMEM((2, 4, 2, 32, C), F32),
        pltpu.VMEM((4, 2, 2, 32, C), F32),
        pltpu.VMEM((4, 2, 2, 32, C), F32),
        pltpu.VMEM((2, 4, 32, C), F32),
        pltpu.VMEM((4, 4, 16, C), F32),
        pltpu.VMEM((4, 16, C), BF),
        pltpu.VMEM((2, 4, 32, C), BF),
        pltpu.VMEM((2, 2, 128, C), BF),
        pltpu.VMEM((2, 4, 2, 32, C), BF),
        pltpu.VMEM((2, 8, 4, C, C), F32),
    ]
    scratch += [sem] * 14 + [pltpu.SemaphoreType.DMA((2, 8)), pltpu.SemaphoreType.DMA((6,))]
    if back:
        scratch += [
            pltpu.VMEM((4, 4, PIECE, C), BF),
            pltpu.VMEM((4, 4, PIECE, C), BF),
            pltpu.VMEM((4, 4, PIECE, C), BF),
            pltpu.VMEM((4, PIECE, C), BF),
            pltpu.VMEM((4, PIECE, C), BF),
            pltpu.VMEM((PIECE, C), BF),
            pltpu.VMEM((4, PIECE, C), BF),
            pltpu.VMEM((4, 4, PIECE, C), BF),
        ] + [sem] * 7
    scratch += [
        pltpu.VMEM((2, 4, 2, 4, 128, C), BF),
        pltpu.VMEM((8, 400, C), BF),
        pltpu.VMEM((1024, 640), BF),
        pltpu.VMEM((10, 128, 8, C), F32),
        pltpu.VMEM((128, 480), BF),
    ]
    if back:
        scratch += [
            pltpu.VMEM((2, 4, 4, PIECE, C), BF),
            pltpu.VMEM((10, 128, 8, C), F32),
            pltpu.VMEM((640, 1024), BF),
            pltpu.VMEM((1280, 160), BF),
            pltpu.VMEM((80, 1280), BF),
            pltpu.VMEM((400, C), F32),
            pltpu.VMEM((400, C), F32),
            pltpu.VMEM((1280, C), F32),
            pltpu.VMEM((1280, C), F32),
            pltpu.VMEM((1280, C), BF),
            pltpu.VMEM((1280, H), F32),
            pltpu.VMEM((1280, H), F32),
            pltpu.VMEM((1280, H), BF),
            pltpu.VMEM((1280, H), BF),
            pltpu.VMEM((C, C), F32),
            pltpu.VMEM((C, H), F32),
            pltpu.VMEM((C, H), F32),
        ]
    else:
        scratch += [
            pltpu.VMEM((SIDE + 60, 88, C), F32),
            pltpu.VMEM((408, C), F32),
            pltpu.VMEM((128, SIDE), BF),
        ]
    return pl.pallas_call(
        functools.partial(exchange_kernel, back),
        out_shape=tuple(out_shape),
        in_specs=in_specs,
        out_specs=tuple(out_specs),
        scratch_shapes=scratch,
        grid=(5,) if back else (),
        compiler_params=pltpu.CompilerParams(
            collective_id=2 if back else 1,
            has_side_effects=True,
            vmem_limit_bytes=VMEM_LIMIT,
        ),
        name="cells_and_exchange" if back else "forward_and_exchange",
    )(*operands)


def gelu_both(v):
    square = v * v
    t = jnp.tanh(v * (TANH_SCALE + (TANH_SCALE * CUBIC_TERM) * square))
    half = 0.5 + 0.5 * t
    inner = (0.5 * TANH_SCALE) + (1.5 * TANH_SCALE * CUBIC_TERM) * square
    return v * half, half + v * (1.0 - t * t) * inner


def store_rows(tot, first, rows):
    done = 0
    while done < rows.shape[0]:
        place, inside = divmod(first + done, PIECE)
        count = min(PIECE - inside, rows.shape[0] - done)
        spot = (place // 16, place // 4 % 4, place % 4)
        tot[spot + (pl.ds(inside, count),)] = rows[done : done + count]
        done += count


def cells_body(step, row, col, keep, inputs, layer, pre_out, ay, big, bgrad, tot, scratch):
    field, cot, z, blk, skip, ctx, up, down, gy, gx = inputs
    p, cells_big, spread, gather, coarse, cell, pre, slope, mid = scratch[:9]
    lifted, dh, hid, lg, acc_skip, acc_up, acc_down = scratch[9:]

    @pl.when(step == 0)
    def _():
        x_to_cells(gx[row], z, p)
        build_to_cells(gy[col], cells_big)
        total = dot(blk[0], ctx[0])
        for d in range(1, 8):
            total = total + dot(blk[d], ctx[d])
        coarse[...] = total
        n, l = iota((1280, 160), 0), iota((1280, 160), 1)
        l = jnp.where(l >= 80, l - 80, l)
        x = over_80(n)
        y = n - 80 * x
        a = over_20(l)
        hit = ((x >> 2) == a) & ((y >> 2) == l - 20 * a)
        spread[...] = jnp.where(hit, 1.0, 0.0).astype(BF)
        l, n = iota((80, 1280), 0), iota((80, 1280), 1)
        x = over_80(n)
        y = n - 80 * x
        a = over_20(l)
        hit = ((x >> 2) == a) & ((y >> 2) == l - 20 * a)
        gather[...] = jnp.where(hit, 1.0, 0.0).astype(BF)
        acc_skip[...] = jnp.zeros_like(acc_skip)
        acc_up[...] = jnp.zeros_like(acc_up)
        acc_down[...] = jnp.zeros_like(acc_down)

    own_rows = pl.ds(pl.multiple_of(80 * step, 8), 80)
    flat = field[...].reshape(1280, C)
    flat_cot = cot[...].reshape(1280, C)
    wide = jnp.concatenate(
        [p[2 * step].reshape(1024, C).astype(BF), p[2 * step + 1].reshape(1024, C).astype(BF)],
        axis=1,
    )
    own = coarse[own_rows]
    high = own.astype(BF)
    low = (own - high.astype(F32)).astype(BF)
    rest = dot(flat, skip[...]) + dot(spread[...], jnp.concatenate([high, low], axis=0))
    for part in range(640 // 160):
        lo, hi = 160 * part, 160 * part + 160
        spectral = dot(cells_big[pl.ds(lo, 160)], wide)
        pre[pl.ds(lo, 160)] = spectral[:, :C].astype(BF).astype(F32) + rest[lo:hi]
        pre[pl.ds(640 + lo, 160)] = spectral[:, C:].astype(BF).astype(F32) + rest[640 + lo : 640 + hi]

    def activate(n, carry):
        rows = pl.ds(pl.multiple_of(64 * n, 64), 64)
        value, slant = gelu_both(pre[rows])
        mid[rows] = value.astype(BF)
        slope[rows] = slant
        return carry

    lax.fori_loop(0, 20, activate, 0, unroll=20)
    lifted[...] = dot(mid[...], up[...])
    dh[...] = dot_tb(flat_cot, down[...])

    def activate_wide(n, carry):
        rows = pl.ds(pl.multiple_of(16 * n, 16), 16)
        value, slant = gelu_both(lifted[rows])
        hid[rows] = value.astype(BF)
        lg[rows] = (dh[rows] * slant).astype(BF)
        return carry

    lax.fori_loop(0, 80, activate_wide, 0, unroll=80)
    result = mid[...].astype(F32) + dot(hid[...], down[...])
    layer[...] = result.astype(BF).reshape(16, SIDE, C)
    grad = flat_cot.astype(F32) + dot_tb(lg[...], up[...])
    grad = (grad * slope[...]).astype(BF)
    pre_out[...] = grad.reshape(16, SIDE, C)
    acc_skip[...] += dot_ta(flat, grad)
    acc_up[...] += dot_ta(mid[...], lg[...])
    acc_down[...] += dot_ta(flat_cot, hid[...])
    cell[own_rows] = dot(gather[...], grad)
    pl.when(step == 0)(keep.wait)
    y_store(big, jnp.concatenate([grad[:640], grad[640:]], axis=1), ay, step)

    def tail():
        narrow = cell[...].astype(BF)
        store_rows(tot, 0, acc_skip[...].astype(BF))
        for d in range(8):
            store_rows(tot, 128 + 128 * d, dot_ta(blk[d], narrow).astype(BF))
            bgrad[d] = dot_tb(narrow, ctx[d]).astype(BF)
        for part in range(4):
            cut = slice(128 * part, 128 * part + 128)
            store_rows(tot, 1152 + 128 * part, acc_up[:, cut].astype(BF))
            store_rows(tot, 1664 + 128 * part, acc_down[:, cut].T.astype(BF))
        store_rows(tot, 2176, jnp.zeros((TOT - 2176, C), BF))

    return tail


def outer(u, g, spec):
    turn = jnp.where(iota((16, 16), 1) == (iota((16, 16), 0) ^ 1), 1.0, 0.0)
    turn = jnp.where((iota((16, 16), 0) & 1) == 1, -turn, turn).astype(BF)
    left_high = u.astype(BF)
    left_low = (u - left_high.astype(F32)).astype(BF)
    right_high = g.astype(BF)
    right_low = (g - right_high.astype(F32)).astype(BF)
    high = jnp.concatenate([right_high, dot(turn, right_high).astype(BF)], axis=1)
    low = jnp.concatenate([right_low, dot(turn, right_low).astype(BF)], axis=1)
    lefts = jnp.concatenate([left_high, left_high, left_low], axis=0).astype(F32).T.astype(BF)
    rights = jnp.concatenate([high, low, high], axis=0)
    row = (iota((48, 2 * C), 0) & 15) >> 1
    for kx in range(8):
        res = dot(lefts, jnp.where(row == kx, rights, jnp.zeros_like(rights)))
        spec[0, kx, 0] = res[:, :C]
        spec[1, kx, 0] = res[:, C:]


def weight_sums(tot, skip, ctx, up, down):
    inv = 1.0 / math.sqrt(NX * NY)
    skip[...] = tot[pl.ds(0, 128)].astype(F32) * inv
    for d in range(8):
        ctx[d] = tot[pl.ds(128 + 128 * d, 128)].astype(F32) * inv
    for part in range(4):
        cut = slice(128 * part, 128 * part + 128)
        up[:, cut] = tot[pl.ds(1152 + 128 * part, 128)].astype(F32) * inv
    down[...] = tot[pl.ds(1664, 512)].astype(F32) * inv


def last_kernel(
    picks, pre, z, back, skip, gy, gx, u, g, tot,
    out, spec, skip_out, ctx_out, up_out, down_out, p, cells_big, place, grads, wide,
):
    step = pl.program_id(0)
    row, col = lax.axis_index("px"), lax.axis_index("py")
    starts = [start_of(pick_of(picks, row, col, d)) for d in range(8)]

    @pl.when(step == 0)
    def _():
        x_to_cells(gx[row], z, p)
        build_to_cells(gy[col], cells_big)
        y, lane = iota((SIDE, 192), 0), iota((SIDE, 192), 1)
        total = jnp.zeros((SIDE, 192), F32)
        for d in range(8):
            depth, sx, sy = starts[d]
            share = jnp.where(depth == 0, 1.0, jnp.where(depth == 1, 0.25, 0.0625))
            spot = lane - 24 * d
            line = jnp.where(depth == 0, y, jnp.where(depth == 1, y >> 1, y >> 2))
            hit = (spot >= 0) & (spot < BLK) & (line - sy == spot)
            total = jnp.where(hit, share, total)
        place[...] = total.astype(BF)
        wide[pl.ds(400, 8)] = jnp.zeros((8, C), F32)
        for d in range(8):
            wide[pl.ds(0, 400)] = back[d].astype(F32)
            for a in range(BLK):
                grads[d, a] = wide[pl.ds(BLK * a, 24)]
            grads[d, BLK] = jnp.zeros((24, C), F32)

    @pl.when(step < 4)
    def _():
        outer(u[step], g[step], spec)

    pl.when(step == 4)(lambda: weight_sums(tot, skip_out, ctx_out, up_out, down_out))
    both = jnp.concatenate(
        [p[2 * step].reshape(1024, C).astype(BF), p[2 * step + 1].reshape(1024, C).astype(BF)],
        axis=1,
    )
    factor = math.sqrt(MX * MY / (NX * NY))
    straight = dot_tb(pre[...].reshape(1280, C), skip[...])
    for k in range(8):
        spectral = dot(cells_big[pl.ds(SIDE * k, SIDE)], both) * factor
        wide_pieces = []
        for x in (k, k + 8):
            pieces = []
            for d in range(8):
                depth, sx, sy = starts[d]
                a = ((16 * step + x) >> depth) - sx
                a = jnp.where((a >= 0) & (a < BLK), a, BLK)
                pieces.append(grads[d, a])
            wide_pieces.append(jnp.concatenate(pieces, axis=0).astype(BF))
        total = spectral + dot(place[...], jnp.concatenate(wide_pieces, axis=1))
        out[k] = (total[:, :C] + straight[80 * k : 80 * k + 80]).astype(BF)
        x = k + 8
        out[x] = (total[:, C:] + straight[80 * x : 80 * x + 80]).astype(BF)


def last_call(picks, pre, z, back, skip, gy, gx, u, g, tot):
    tile = pl.BlockSpec((16, SIDE, C), lambda n: (n, 0, 0))
    shape = jax.ShapeDtypeStruct
    return pl.pallas_call(
        last_kernel,
        grid=(5,),
        out_shape=(
            shape((SIDE, SIDE, C), BF),
            shape((2, 8, 4, C, C), F32),
            shape((C, C), F32),
            shape((8, C, C), F32),
            shape((C, H), F32),
            shape((H, C), F32),
        ),
        in_specs=[
            SM, tile, whole(64, 128, C), whole(8, 400, C), whole(C, C),
            whole(COLS, SIDE, 128), whole(ROWS, 160, 256), whole(4, 16, C), whole(4, 16, C),
            whole(TOT, C),
        ],
        out_specs=(
            tile,
            pl.BlockSpec((2, 8, 1, C, C), lambda n: (0, 0, jnp.minimum(n, 3), 0, 0)),
            whole(C, C),
            whole(8, C, C),
            whole(C, H),
            whole(H, C),
        ),
        scratch_shapes=[
            pltpu.VMEM((10, 128, 8, C), F32),
            pltpu.VMEM((640, 1024), BF),
            pltpu.VMEM((SIDE, 192), BF),
            pltpu.VMEM((8, BLK + 1, 24, C), F32),
            pltpu.VMEM((408, C), F32),
        ],
        compiler_params=pltpu.CompilerParams(vmem_limit_bytes=VMEM_LIMIT),
        name="field_gradient",
    )(picks, pre, z, back, skip, gy, gx, u, g, tot)


def shards(
    flow_field, cotangent, spec_weight, skip_weight, ctx_weight, up_weight, down_weight,
    ctx_level, ctx_offset,
):
    ty, gy, tx, gx = (jnp.asarray(t) for t in wave_tables())
    picks = ctx_level + (ctx_offset[:, :, 0] << 2) + (ctx_offset[:, :, 1] << 9)
    z, arrived, u, big = exchange(False, picks, flow_field, ty, tx, spec_weight)
    layer, pre, z, back, g, tot = exchange(
        True, flow_field, cotangent, z.reshape(64, 128, C), arrived, skip_weight, ctx_weight,
        up_weight, down_weight, gy, gx, tx, big, spec_weight,
    )
    grad, spec, skip, ctx, up, down = last_call(
        picks, pre, z.reshape(64, 128, C), back, skip_weight, gy, gx, u, g, tot.reshape(TOT, C)
    )
    return layer, grad, spec, skip, ctx, up, down


def solution(mesh):
    return jax.shard_map(
        shards,
        mesh=mesh,
        in_specs=(
            P("px", "py", None),
            P("px", "py", None),
            P(None, "px", "py", None, None),
            P(),
            P(),
            P(),
            P(),
            P(),
            P(),
        ),
        out_specs=(
            P("px", "py", None),
            P("px", "py", None),
            P(None, "px", "py", None, None),
            P(),
            P(),
            P(),
            P(),
        ),
        check_vma=False,
    )
```

time: 176 us -> 153 us (0.87)
  Pallas kernels: 173 us -> 148 us
    pallas_call x3 -> x1, Pallas kernels: 61.3 us -> 13.2 us  [last_call(): pl.pallas_call(last_kernel, grid=(5,), out_shape=(shape((SIDE, SIDE, C),...]
    pallas_call x2, Pallas kernels: 112 us -> 135 us  [exchange(): pl.pallas_call(functools.partial(exchange_kernel, back), out_shape=tuple(...]
where the time goes in v3:
time: 153 us; the launch traced here: 152 us
  Pallas kernels  148 us (97%)
  local copies, waits for them, and re-layouts  2.94 us (2%)
    pallas_call x2, Pallas kernels, exchange(): pl.pallas_call(functools.partial(exchange_kernel, back), out_shape=tuple(...  135 us
    pallas_call x1, Pallas kernels, last_call(): pl.pallas_call(last_kernel, grid=(5,), out_shape=(shape((SIDE, SIDE, C),...  13.2 us

profile of v3, /device:TPU:1, one launch (start us, length us, event | category | flops | bytes accessed | tf_op | source)
XLA Modules:
  0.0 152.4 jit_solution(4725468059237908894)
XLA Ops:
  0.6 0.8 fusion
  1.4 0.1 copy.20
  1.5 0.1 copy.22
  1.6 0.8 copy.21
  2.4 0.6 bitcast_add_fusion.refs_0_.picks
  3.0 55.7 %forward_and_exchange.1 = (bf16[2,4,2,4,128,128]{5,4,3,2,1,0:T(8,128)(2,1)}, bf16[8,400,128]{2,1,0:T(8,128)(2,1)}, f32[4,16,128]{2,1,0:T(8,128)}, bf16[1024,640]{1,0:T(8,128)(2,1)}) custom-call(s32[128,8]{1,0:T(8,128)} %bitcast_add_fusion.refs_0_.picks, bf16[80,80,128]{2,1,0:T(8,128)(2,1)} %refs_0_.1, bf16[16,128,80]{2,1,0:T(8,128)(2,1)} %constant.12.clone.refs_2_, ...), custom_call_target="tpu_custom_call" | custom-call | tf_op jit(solution)/shard_map/forward_and_exchange/pallas_call | solution.py:703
  58.8 79.2 %cells_and_exchange.1 = (bf16[80,80,128]{2,1,0:T(8,128)(2,1)}, bf16[80,80,128]{2,1,0:T(8,128)(2,1)}, bf16[2,4,2,4,128,128]{5,4,3,2,1,0:T(8,128)(2,1)}, bf16[8,40...) custom-call(bf16[80,80,128]{2,1,0:T(8,128)(2,1)} %refs_0_.1, ...), custom_call_target="tpu_custom_call" | custom-call | tf_op jit(solution)/shard_map/cells_and_exchange/pallas_call | solution.py:703
  138.0 0.0 copy-start
  138.0 13.2 %field_gradient.1 = (bf16[80,80,128]{2,1,0:T(8,128)(2,1)}, f32[2,8,4,128,128]{4,3,2,1,0:T(8,128)}, f32[128,128]{1,0:T(8,128)}, f32[8,128,128]{2,1,0:T(8,128)}, f32[128,512]{1,0:T(8,128)}, /*index=5*/f32[512,128]{1,0:T(8,128)}) custom-call(s32[128,8]{1,0:T(8,128)} %bitcast_add_fusion.refs_0_.picks, bf16[80,80,128]{2,1,0:T(8,128)(2,1)} %get-tuple-element.27.pre, ...), custom_call_target="tpu_custom_call" | custom-call | tf_op jit(solution)/shard_map/field_gradient/pallas_call | solution.py:919
  151.2 0.0 copy-done
  151.2 1.2 copy.24
Async XLA Ops:
  138.0 13.2 %copy-start = (bf16[80,80,128]{2,1,0:T(8,128)(2,1)S(1)}, bf16[80,80,128]{2,1,0:T(8,128)(2,1)}, u32[]{:S(2)}) copy-start(bf16[80,80,128]{2,1,0:T(8,128)(2,1)} %get-tuple-element.48) | copy-start | bytes 4915204

commit v4 on v3

--- a/solution.py
+++ b/solution.py
@@ -1,4 +1,3 @@
-import functools
 import math
 
 import jax
@@ -197,7 +196,7 @@
         blocks[d] = tmp[pl.ds(0, 400)].astype(BF)
 
 
-def exchange_kernel(back, *refs):
+def forward_kernel(*refs):
     refs = list(refs)
 
     def take(n):
@@ -205,23 +204,12 @@
         del refs[:n]
         return taken
 
-    if back:
-        cells_in = take(10)
-        tx, big_in, w = take(3)
-        layer_out, pre_out, z, bo, u, to = take(6)
-    else:
-        picks, field, ty, tx, w = take(5)
-        z, bo, u, big_out = take(4)
-    r0, sa, sb, r1a, r1b, acca, accb, r2a, r2b, ab, r3, zs, zz, za, zb, wv = take(16)
-    core_a, core_b, one_a, one_b, two_a, two_b, three, wide3 = take(8)
-    wide2_a, wide2_b, wide1_a, wide1_b, share_a, share_b, blocks, local = take(8)
-    if back:
-        t0, t1s, t1, t2s, t2, t3s, t3, tall = take(8)
-        core_t, one_t, two_t, three_t, wide2_t, wide1_t, share_t = take(7)
-        s, b, big, ay, tx_own, t = take(6)
-        step = pl.program_id(0)
-    else:
-        s, b, big, ay, tx_own, grid, tmp, ty_own = take(8)
+    picks, field, ty, tx, w = take(5)
+    z, bo, u, big_out = take(4)
+    r0, sa, sb, r1a, r1b, acca, accb, r2a, r2b, zs, za, zb, wv = take(13)
+    core_a, core_b, one_a, one_b, wide1_a, wide1_b, share_a, share_b = take(8)
+    two_a, two_b, wide2_a, wide2_b, blocks, local = take(6)
+    s, b, big, ay, tx_own, grid, tmp, ty_own = take(8)
     i, j = lax.axis_index("px"), lax.axis_index("py")
     y, zh = i // 2, i % 2
     zl, x, c = j // 8, (j // 2) % 4, j % 2
@@ -236,6 +224,25 @@
 
     def at_z(n):
         return (2 * y + n % 2, 8 * (n // 2) + 2 * x + c)
+
+    def at_yz(n):
+        return (2 * (n // 4) + n % 2, 8 * (n // 2 % 2) + 2 * x + c)
+
+    def at_xz(n):
+        return (2 * y + n % 2, 8 * (n // 2 % 2) + 2 * (n // 4) + c)
+
+    def partner(base, r):
+        return 4 * ((base + r // 4) % 4) + (spot + r % 4) % 4
+
+    def sender(base, r):
+        return 4 * ((base - r // 4 + 4) % 4) + (spot - r % 4 + 4) % 4
+
+    def loop15(body):
+        def step(r, carry):
+            body(r)
+            return carry
+
+        lax.fori_loop(1, 16, step, 0)
 
     def remote(src, dst, sems, sent, landed, device):
         return pltpu.make_async_remote_copy(
@@ -258,15 +265,14 @@
 
     barrier = pltpu.get_barrier_semaphore()
     partners = [sibling]
-    for r in (1, 2, 3):
-        partners += [at_x((x + r) % 4), at_y((y + r) % 4), at_z((spot + r) % 4)]
+    for r in range(1, 16):
+        partners.append(at_yz(partner(y, r)))
+        if r > 3:
+            partners.append(at_xz(partner(x, r)))
     partners += [neighbour(d, 1) for d in range(8)]
     weights = pltpu.make_async_copy(w, wv, local.at[0])
     table_x = pltpu.make_async_copy(tx.at[i], tx_own, local.at[4])
-    if back:
-        keep = pltpu.make_async_copy(big_in, big, local.at[5])
-    else:
-        keep = pltpu.make_async_copy(big, big_out, local.at[5])
+    keep = pltpu.make_async_copy(big, big_out, local.at[5])
 
     def greet():
         for device in partners:
@@ -274,21 +280,10 @@
         weights.start()
         table_x.start()
 
-    if back:
-
-        @pl.when(step == 0)
-        def _():
-            keep.start()
-            greet()
-
-        tail = cells_body(
-            step, i, j, keep, cells_in, layer_out, pre_out, ay, big, b, t, refs
-        )
-    else:
-        greet()
-        table_y = pltpu.make_async_copy(ty.at[j], ty_own, local.at[3])
-        table_y.start()
-        pick_blocks(picks, i, j, field, grid, tmp, b)
+    greet()
+    table_y = pltpu.make_async_copy(ty.at[j], ty_own, local.at[3])
+    table_y.start()
+    pick_blocks(picks, i, j, field, grid, tmp, b)
 
     def run():
         pl.semaphore_wait(barrier, len(partners))
@@ -306,7 +301,7 @@
             return remote(src, r0.at[:, :, 2:4, band(n)], core_b, n, n, sibling)
 
         def block_copy(d):
-            device = neighbour(d, 1 if back else -1)
+            device = neighbour(d, -1)
             return remote(b.at[d], bo.at[d], blocks, d, d, device)
 
         def fill(n, half):
@@ -320,23 +315,17 @@
 
             lax.fori_loop(0, 4, step, 0, unroll=4)
 
-        if not back:
-            for d in range(8):
-                begin(block_copy(d))
-            table_y.wait()
-            build_to_modes(ty_own[...], big)
-            keep.start()
-            y_to_modes(big, field, ay)
+        for d in range(8):
+            begin(block_copy(d))
+        table_y.wait()
+        build_to_modes(ty_own[...], big)
+        keep.start()
+        y_to_modes(big, field, ay)
         table_x.wait()
         for r in (2, 1, 3, 0):
             n = (x + r) % 4
             fill(n, 0)
             begin(core_copy_a(n))
-        if back:
-
-            def core_copy_t():
-                return remote(t.at[1 - c], t0, core_t, 0, 0, sibling)
-
         def one_copy_a(n, slot, device):
             return remote(sa.at[n], r1a.at[slot], one_a, n, slot, device)
 
@@ -370,87 +359,55 @@
             begin(core_copy_b((y + r) % 4))
         for r in (2, 1, 3):
             pass_b(r)
-        if back:
-            tail()
-            begin(core_copy_t())
-            for d in range(8):
-                begin(block_copy(d))
         acca[...] = sum_a(x)
         accb[...] = sum_b(y)
-        if back:
-
-            def one_copy_t(n, slot, device):
-                return remote(t1s.at[n], t1.at[slot], one_t, n, slot, device)
-
-            core_copy_t().wait_recv()
-            t1s[...] = (t[c].astype(F32) + t0[...].astype(F32)).astype(BF)
-            for r in (2, 1, 3):
-                n = (x + r) % 4
-                begin(one_copy_t(n, x, at_x(n)))
         for r in (1, 3, 2):
             n = (x + r) % 4
             one_copy_a(n, n, at_x(n)).wait_recv()
             acca[...] = acca[...] + r1a[n].astype(F32)
 
         def two_copy_a(n, slot, device):
-            return remote(acca.at[:, :, band(n)], r2a.at[slot], two_a, n, slot, device)
+            src = acca.at[n // 2 % 2, :, band(2 * (n // 4) + n % 2, 16)]
+            return remote(src, r2a.at[slot], two_a, n, slot, device)
 
         def two_copy_b(n, slot, device):
-            return remote(accb.at[:, n], r2b.at[slot], two_b, n, slot, device)
-
-        for r in (2, 1, 3):
-            n = (y + r) % 4
-            begin(two_copy_a(n, y, at_y(n)))
+            src = accb.at[n // 2 % 2, n // 4, :, band(n % 2, 16)]
+            return remote(src, r2b.at[slot], two_b, n, slot, device)
+
+        def send_two_a(r):
+            n = partner(y, r)
+            two_copy_a(n, 4 * y + spot, at_yz(n)).start()
+
+        def send_two_b(r):
+            n = partner(x, r)
+            two_copy_b(n, 4 * x + spot, at_xz(n)).start()
+
+        loop15(send_two_a)
         for r in (1, 3, 2):
             n = (y + r) % 4
             one_copy_b(n, n, at_y(n)).wait_recv()
             accb[...] = accb[...] + r1b[n].astype(F32)
-        for r in (2, 1, 3):
-            n = (x + r) % 4
-            begin(two_copy_b(n, x, at_x(n)))
-        ab[:, 0:2] = acca[:, :, band(y)]
-        ab[:, 2:4] = accb[:, x]
-        for r in (1, 3, 2):
-            n = (y + r) % 4
-            two_copy_a(n, n, at_y(n)).wait_recv()
-            ab[:, 0:2] = ab[:, 0:2] + r2a[n]
-        for r in (1, 3, 2):
-            n = (x + r) % 4
-            two_copy_b(n, n, at_x(n)).wait_recv()
-            ab[:, 2:4] = ab[:, 2:4] + r2b[n]
-
-        def three_copy(n, slot, device):
-            return remote(ab.at[n // 2, :, band(n % 2, 16)], r3.at[slot], three, n, slot, device)
-
-        for r in (2, 1, 3):
-            n = (spot + r) % 4
-            begin(three_copy(n, spot, at_z(n)))
-        if back:
-
-            def two_copy_t(n, slot, device):
-                return remote(t2s.at[n], t2.at[slot], two_t, n, slot, device)
-
-            total = t1s[x].astype(F32)
-            for r in (1, 3, 2):
-                n = (x + r) % 4
-                one_copy_t(n, n, at_x(n)).wait_recv()
-                total = total + t1[n].astype(F32)
-            t2s[...] = total.astype(BF)
-            for r in (2, 1, 3):
-                n = (y + r) % 4
-                begin(two_copy_t(n, y, at_y(n)))
-        u[...] = ab[zl, :, band(zh, 16)]
-        for r in (1, 3, 2):
-            n = (spot + r) % 4
-            three_copy(n, n, at_z(n)).wait_recv()
-            u[...] = u[...] + r3[n]
-        if back:
-            u[...] = u[...] * math.sqrt(NX * NY / (MX * MY))
+        loop15(send_two_b)
+        u[0:2] = acca[zl, :, band(i, 16)]
+        u[2:4] = accb[zl, x, :, band(zh, 16)]
+
+        def gather_two_a(r):
+            n = sender(y, r)
+            two_copy_a(n, n, at_yz(n)).wait_recv()
+            u[0:2] = u[0:2] + r2a[n]
+
+        def gather_two_b(r):
+            n = sender(x, r)
+            two_copy_b(n, n, at_xz(n)).wait_recv()
+            u[2:4] = u[2:4] + r2b[n]
+
+        loop15(gather_two_a)
+        loop15(gather_two_b)
         weights.wait()
         same = iota((16, 16), 0) ^ 1
         turn = jnp.where(iota((16, 16), 1) == same, 1.0, 0.0)
         odd = (iota((16, 16), 0) & 1) == 1
-        flip = odd if back else jnp.logical_not(odd)
+        flip = jnp.logical_not(odd)
         turn = jnp.where(flip, -turn, turn).astype(BF)
 
         def mix(ky, carry):
@@ -462,60 +419,34 @@
             both = jnp.concatenate([both, turned], axis=1)
             total = jnp.zeros((16, C), F32)
             for kx in range(8):
-                if back:
-                    mat = jnp.concatenate([wv[0, kx, ky], wv[1, kx, ky]], axis=1).astype(BF)
-                    res = dot_tb(both, mat)
-                else:
-                    mat = jnp.concatenate([wv[0, kx, ky], wv[1, kx, ky]], axis=0).astype(BF)
-                    res = dot(both, mat)
+                mat = jnp.concatenate([wv[0, kx, ky], wv[1, kx, ky]], axis=0).astype(BF)
+                res = dot(both, mat)
                 total = jnp.where((iota((16, C), 0) >> 1) == kx, res[:16] + res[16:], total)
             zs[ky] = total.astype(BF)
             return carry
 
         lax.fori_loop(0, 4, mix, 0)
 
-        def wide_copy3(slot, sent, device):
-            dst = zz.at[slot // 2, :, band(slot % 2, 16)]
-            return remote(zs, dst, wide3, sent, slot, device)
-
-        for r in (2, 1, 3):
-            n = (spot + r) % 4
-            begin(wide_copy3(spot, n, at_z(n)))
-        zz[zl, :, band(zh, 16)] = zs[...]
-        if back:
-            t3s[...] = t2s[y]
-            total = t3s[...].astype(F32)
-            for r in (1, 3, 2):
-                n = (y + r) % 4
-                two_copy_t(n, n, at_y(n)).wait_recv()
-                total = total + t2[n].astype(F32)
-            t3s[...] = total.astype(BF)
-            t3[spot] = t3s[...]
-
-            def three_copy_t(slot, sent, device):
-                return remote(t3s, t3.at[slot], three_t, sent, slot, device)
-
-            for r in (2, 1, 3):
-                n = (spot + r) % 4
-                begin(three_copy_t(spot, n, at_z(n)))
-        for r in (1, 3, 2):
-            n = (spot + r) % 4
-            wide_copy3(n, n, at_z(n)).wait_recv()
-
         def wide_copy2_a(slot, sent, device):
-            return remote(zz.at[:, 0:2], za.at[:, :, band(slot)], wide2_a, sent, slot, device)
+            dst = za.at[slot // 2 % 2, :, band(2 * (slot // 4) + slot % 2, 16)]
+            return remote(zs.at[0:2], dst, wide2_a, sent, slot, device)
 
         def wide_copy2_b(slot, sent, device):
-            return remote(zz.at[:, 2:4], zb.at[:, slot], wide2_b, sent, slot, device)
-
-        for r in (2, 1, 3):
-            n = (y + r) % 4
-            begin(wide_copy2_a(y, n, at_y(n)))
-            n = (x + r) % 4
-            begin(wide_copy2_b(x, n, at_x(n)))
-        za[:, :, band(y)] = zz[:, 0:2]
-        zb[:, x] = zz[:, 2:4]
-
+            dst = zb.at[slot // 2 % 2, slot // 4, :, band(slot % 2, 16)]
+            return remote(zs.at[2:4], dst, wide2_b, sent, slot, device)
+
+        def send_wide_a(r):
+            n = partner(y, r)
+            wide_copy2_a(4 * y + spot, n, at_yz(n)).start()
+
+        def send_wide_b(r):
+            n = partner(x, r)
+            wide_copy2_b(4 * x + spot, n, at_xz(n)).start()
+
+        loop15(send_wide_a)
+        loop15(send_wide_b)
+        za[zl, :, band(i, 16)] = zs[0:2]
+        zb[zl, x, :, band(zh, 16)] = zs[2:4]
         def part_a(n, core):
             return z.at[:, n, core, 0:2]
 
@@ -528,15 +459,19 @@
         def wide_copy1_b(slot, sent, device):
             return remote(zb, part_b(slot, c), wide1_b, sent, slot, device)
 
-        for r in (1, 3, 2):
-            n = (y + r) % 4
-            wide_copy2_a(n, n, at_y(n)).wait_recv()
+        def gather_wide_a(r):
+            n = sender(y, r)
+            wide_copy2_a(n, n, at_yz(n)).wait_recv()
+
+        def gather_wide_b(r):
+            n = sender(x, r)
+            wide_copy2_b(n, n, at_xz(n)).wait_recv()
+
+        loop15(gather_wide_a)
         for r in (2, 1, 3):
             n = (x + r) % 4
             begin(wide_copy1_a(x, n, at_x(n)))
-        for r in (1, 3, 2):
-            n = (x + r) % 4
-            wide_copy2_b(n, n, at_x(n)).wait_recv()
+        loop15(gather_wide_b)
         for r in (2, 1, 3):
             n = (y + r) % 4
             begin(wide_copy1_b(y, n, at_y(n)))
@@ -546,34 +481,6 @@
         own_b.start()
         begin(remote(za, part_a(x, c), share_a, x, x, sibling))
         begin(remote(zb, part_b(y, c), share_b, y, y, sibling))
-        if back:
-            for r in (1, 3, 2):
-                n = (spot + r) % 4
-                three_copy_t(n, n, at_z(n)).wait_recv()
-            total = t3[0].astype(F32)
-            for n in range(1, 4):
-                total = total + t3[n].astype(F32)
-            tall[x, y] = total.astype(BF)
-
-            def wide_copy2_t(slot, sent, device):
-                piece = tall.at[x, slot]
-                return remote(piece, piece, wide2_t, sent, slot, device)
-
-            for r in (2, 1, 3):
-                n = (y + r) % 4
-                begin(wide_copy2_t(y, n, at_y(n)))
-            for r in (1, 3, 2):
-                n = (y + r) % 4
-                wide_copy2_t(n, n, at_y(n)).wait_recv()
-
-            def wide_copy1_t(slot, sent, device):
-                piece = tall.at[slot]
-                return remote(piece, piece, wide1_t, sent, slot, device)
-
-            for r in (2, 1, 3):
-                n = (x + r) % 4
-                begin(wide_copy1_t(x, n, at_x(n)))
-
         def share_copy_a(n, core):
             return remote(part_a(n, core), part_a(n, core), share_a, n, n, sibling)
 
@@ -587,14 +494,6 @@
             n = (y + r) % 4
             wide_copy1_b(n, n, at_y(n)).wait_recv()
             begin(share_copy_b(n, c))
-        if back:
-            for r in (1, 3, 2):
-                n = (x + r) % 4
-                wide_copy1_t(n, n, at_x(n)).wait_recv()
-            share = remote(tall, to.at[c], share_t, 0, 0, sibling)
-            begin(share)
-            own_t = pltpu.make_async_copy(tall, to.at[c], local.at[3])
-            own_t.start()
         for n in range(4):
             share_copy_a(n, 1 - c).wait_recv()
             share_copy_b(n, 1 - c).wait_recv()
@@ -602,18 +501,396 @@
             block_copy(d).wait_recv()
         own_a.wait()
         own_b.wait()
-        if back:
-            share.wait_recv()
-            own_t.wait()
-        else:
-            keep.wait()
+        keep.wait()
         for copy in waits:
             copy.wait_send()
 
-    if back:
-        pl.when(step == 4)(run)
-    else:
-        run()
+        def settle(r):
+            n, m = partner(y, r), partner(x, r)
+            two_copy_a(n, 4 * y + spot, at_yz(n)).wait_send()
+            two_copy_b(m, 4 * x + spot, at_xz(m)).wait_send()
+            wide_copy2_a(4 * y + spot, n, at_yz(n)).wait_send()
+            wide_copy2_b(4 * x + spot, m, at_xz(m)).wait_send()
+
+        loop15(settle)
+
+    run()
+
+
+def cells_kernel(*refs):
+    refs = list(refs)
+
+    def take(n):
+        taken = refs[:n]
+        del refs[:n]
+        return taken
+
+    cells_in = take(10)
+    tx, big_in, w = take(3)
+    layer_out, pre_out, z, bo, u, to = take(6)
+    r0, sa, sb, r1a, r1b, acca, accb, r2a, r2b, ab, r3, zs, zz, za, zb, wv = take(16)
+    core_a, core_b, one_a, one_b, two_a, two_b, three, wide3 = take(8)
+    wide2_a, wide2_b, wide1_a, wide1_b, share_a, share_b, blocks, local = take(8)
+    t0, t1s, t1, t2s, t2, t3s, t3, tall = take(8)
+    core_t, one_t, two_t, three_t, wide2_t, wide1_t, share_t = take(7)
+    s, b, big, ay, tx_own, t = take(6)
+    step = pl.program_id(0)
+    i, j = lax.axis_index("px"), lax.axis_index("py")
+    y, zh = i // 2, i % 2
+    zl, x, c = j // 8, (j // 2) % 4, j % 2
+    spot = 2 * zl + zh
+    sibling = (i, 8 * zl + 2 * x + 1 - c)
+
+    def at_x(n):
+        return (i, 8 * zl + 2 * n + c)
+
+    def at_y(n):
+        return (2 * n + zh, j)
+
+    def at_z(n):
+        return (2 * y + n % 2, 8 * (n // 2) + 2 * x + c)
+
+    def remote(src, dst, sems, sent, landed, device):
+        return pltpu.make_async_remote_copy(
+            src_ref=src,
+            dst_ref=dst,
+            send_sem=sems.at[0, sent],
+            recv_sem=sems.at[1, landed],
+            device_id=device,
+            device_id_type=MESH,
+        )
+
+    def neighbour(d, sign):
+        return (
+            (i + sign * STEP_ROWS[d] + ROWS) % ROWS,
+            (j + sign * STEP_COLS[d] + COLS) % COLS,
+        )
+
+    def band(n, size=32):
+        return pl.ds(pl.multiple_of(n * size, size), size)
+
+    barrier = pltpu.get_barrier_semaphore()
+    partners = [sibling]
+    for r in (1, 2, 3):
+        partners += [at_x((x + r) % 4), at_y((y + r) % 4), at_z((spot + r) % 4)]
+    partners += [neighbour(d, 1) for d in range(8)]
+    weights = pltpu.make_async_copy(w, wv, local.at[0])
+    table_x = pltpu.make_async_copy(tx.at[i], tx_own, local.at[4])
+    keep = pltpu.make_async_copy(big_in, big, local.at[5])
+    def greet():
+        for device in partners:
+            pl.semaphore_signal(barrier, inc=1, device_id=device, device_id_type=MESH)
+        weights.start()
+        table_x.start()
+
+
+    @pl.when(step == 0)
+    def _():
+        keep.start()
+        greet()
+
+    tail = cells_body(
+        step, i, j, keep, cells_in, layer_out, pre_out, ay, big, b, t, refs
+    )
+    def run():
+        pl.semaphore_wait(barrier, len(partners))
+        waits = []
+
+        def begin(copy):
+            copy.start()
+            waits.append(copy)
+
+        def core_copy_a(n):
+            return remote(s.at[:, n, 1 - c, 0:2], r0.at[:, n, 0:2], core_a, n, n, sibling)
+
+        def core_copy_b(n):
+            src = s.at[:, :, 1 - c, 2:4, band(n)]
+            return remote(src, r0.at[:, :, 2:4, band(n)], core_b, n, n, sibling)
+
+        def block_copy(d):
+            device = neighbour(d, 1)
+            return remote(b.at[d], bo.at[d], blocks, d, d, device)
+
+        def fill(n, half):
+            def step(m, carry):
+                a, e = m // 2, m % 2
+                ky = 4 * (8 * a + 2 * n + e) + 2 * half
+                first, second = x_to_modes(tx_own[...], ay, (ky, ky + 1))
+                s[a, n, e, 2 * half] = first
+                s[a, n, e, 2 * half + 1] = second
+                return carry
+
+            lax.fori_loop(0, 4, step, 0, unroll=4)
+
+        table_x.wait()
+        for r in (2, 1, 3, 0):
+            n = (x + r) % 4
+            fill(n, 0)
+            begin(core_copy_a(n))
+
+        def core_copy_t():
+            return remote(t.at[1 - c], t0, core_t, 0, 0, sibling)
+
+        def one_copy_a(n, slot, device):
+            return remote(sa.at[n], r1a.at[slot], one_a, n, slot, device)
+
+        def one_copy_b(n, slot, device):
+            return remote(sb.at[n], r1b.at[slot], one_b, n, slot, device)
+
+        def sum_a(n):
+            core_copy_a(n).wait_recv()
+            return s[:, n, c, 0:2].astype(F32) + r0[:, n, 0:2].astype(F32)
+
+        def sum_b(n):
+            core_copy_b(n).wait_recv()
+            rows = band(n)
+            return s[:, :, c, 2:4, rows].astype(F32) + r0[:, :, 2:4, rows].astype(F32)
+
+        def pass_a(r):
+            n = (x + r) % 4
+            sa[n] = sum_a(n).astype(BF)
+            begin(one_copy_a(n, x, at_x(n)))
+
+        def pass_b(r):
+            n = (y + r) % 4
+            sb[n] = sum_b(n).astype(BF)
+            begin(one_copy_b(n, y, at_y(n)))
+
+        for r in (2, 1, 3, 0):
+            fill((x + r) % 4, 1)
+            if r:
+                pass_a(r)
+        for r in (2, 1, 3, 0):
+            begin(core_copy_b((y + r) % 4))
+        for r in (2, 1, 3):
+            pass_b(r)
+        tail()
+        begin(core_copy_t())
+        for d in range(8):
+            begin(block_copy(d))
+        acca[...] = sum_a(x)
+        accb[...] = sum_b(y)
+
+        def one_copy_t(n, slot, device):
+            return remote(t1s.at[n], t1.at[slot], one_t, n, slot, device)
+
+        core_copy_t().wait_recv()
+        t1s[...] = (t[c].astype(F32) + t0[...].astype(F32)).astype(BF)
+        for r in (2, 1, 3):
+            n = (x + r) % 4
+            begin(one_copy_t(n, x, at_x(n)))
+        for r in (1, 3, 2):
+            n = (x + r) % 4
+            one_copy_a(n, n, at_x(n)).wait_recv()
+            acca[...] = acca[...] + r1a[n].astype(F32)
+
+        def two_copy_a(n, slot, device):
+            return remote(acca.at[:, :, band(n)], r2a.at[slot], two_a, n, slot, device)
+
+        def two_copy_b(n, slot, device):
+            return remote(accb.at[:, n], r2b.at[slot], two_b, n, slot, device)
+
+        for r in (2, 1, 3):
+            n = (y + r) % 4
+            begin(two_copy_a(n, y, at_y(n)))
+        for r in (1, 3, 2):
+            n = (y + r) % 4
+            one_copy_b(n, n, at_y(n)).wait_recv()
+            accb[...] = accb[...] + r1b[n].astype(F32)
+        for r in (2, 1, 3):
+            n = (x + r) % 4
+            begin(two_copy_b(n, x, at_x(n)))
+        ab[:, 0:2] = acca[:, :, band(y)]
+        ab[:, 2:4] = accb[:, x]
+        for r in (1, 3, 2):
+            n = (y + r) % 4
+            two_copy_a(n, n, at_y(n)).wait_recv()
+            ab[:, 0:2] = ab[:, 0:2] + r2a[n]
+        for r in (1, 3, 2):
+            n = (x + r) % 4
+            two_copy_b(n, n, at_x(n)).wait_recv()
+            ab[:, 2:4] = ab[:, 2:4] + r2b[n]
+
+        def three_copy(n, slot, device):
+            return remote(ab.at[n // 2, :, band(n % 2, 16)], r3.at[slot], three, n, slot, device)
+
+        for r in (2, 1, 3):
+            n = (spot + r) % 4
+            begin(three_copy(n, spot, at_z(n)))
+
+        def two_copy_t(n, slot, device):
+            return remote(t2s.at[n], t2.at[slot], two_t, n, slot, device)
+
+        total = t1s[x].astype(F32)
+        for r in (1, 3, 2):
+            n = (x + r) % 4
+            one_copy_t(n, n, at_x(n)).wait_recv()
+            total = total + t1[n].astype(F32)
+        t2s[...] = total.astype(BF)
+        for r in (2, 1, 3):
+            n = (y + r) % 4
+            begin(two_copy_t(n, y, at_y(n)))
+        u[...] = ab[zl, :, band(zh, 16)]
+        for r in (1, 3, 2):
+            n = (spot + r) % 4
+            three_copy(n, n, at_z(n)).wait_recv()
+            u[...] = u[...] + r3[n]
+        u[...] = u[...] * math.sqrt(NX * NY / (MX * MY))
+        weights.wait()
+        same = iota((16, 16), 0) ^ 1
+        turn = jnp.where(iota((16, 16), 1) == same, 1.0, 0.0)
+        odd = (iota((16, 16), 0) & 1) == 1
+        flip = odd
+        turn = jnp.where(flip, -turn, turn).astype(BF)
+
+        def mix(ky, carry):
+            first = u[ky]
+            high = first.astype(BF)
+            low = (first - high.astype(F32)).astype(BF)
+            both = jnp.concatenate([high, low], axis=0)
+            turned = jnp.concatenate([dot(turn, high), dot(turn, low)], axis=0).astype(BF)
+            both = jnp.concatenate([both, turned], axis=1)
+            total = jnp.zeros((16, C), F32)
+            for kx in range(8):
+                mat = jnp.concatenate([wv[0, kx, ky], wv[1, kx, ky]], axis=1).astype(BF)
+                res = dot_tb(both, mat)
+                total = jnp.where((iota((16, C), 0) >> 1) == kx, res[:16] + res[16:], total)
+            zs[ky] = total.astype(BF)
+            return carry
+
+        lax.fori_loop(0, 4, mix, 0)
+
+        def wide_copy3(slot, sent, device):
+            dst = zz.at[slot // 2, :, band(slot % 2, 16)]
+            return remote(zs, dst, wide3, sent, slot, device)
+
+        for r in (2, 1, 3):
+            n = (spot + r) % 4
+            begin(wide_copy3(spot, n, at_z(n)))
+        zz[zl, :, band(zh, 16)] = zs[...]
+        t3s[...] = t2s[y]
+        total = t3s[...].astype(F32)
+        for r in (1, 3, 2):
+            n = (y + r) % 4
+            two_copy_t(n, n, at_y(n)).wait_recv()
+            total = total + t2[n].astype(F32)
+        t3s[...] = total.astype(BF)
+        t3[spot] = t3s[...]
+
+        def three_copy_t(slot, sent, device):
+            return remote(t3s, t3.at[slot], three_t, sent, slot, device)
+
+        for r in (2, 1, 3):
+            n = (spot + r) % 4
+            begin(three_copy_t(spot, n, at_z(n)))
+        for r in (1, 3, 2):
+            n = (spot + r) % 4
+            wide_copy3(n, n, at_z(n)).wait_recv()
+
+        def wide_copy2_a(slot, sent, device):
+            return remote(zz.at[:, 0:2], za.at[:, :, band(slot)], wide2_a, sent, slot, device)
+
+        def wide_copy2_b(slot, sent, device):
+            return remote(zz.at[:, 2:4], zb.at[:, slot], wide2_b, sent, slot, device)
+
+        for r in (2, 1, 3):
+            n = (y + r) % 4
+            begin(wide_copy2_a(y, n, at_y(n)))
+            n = (x + r) % 4
+            begin(wide_copy2_b(x, n, at_x(n)))
+        za[:, :, band(y)] = zz[:, 0:2]
+        zb[:, x] = zz[:, 2:4]
+        for r in (1, 3, 2):
+            n = (spot + r) % 4
+            three_copy_t(n, n, at_z(n)).wait_recv()
+        total = t3[0].astype(F32)
+        for n in range(1, 4):
+            total = total + t3[n].astype(F32)
+        tall[x, y] = total.astype(BF)
+
+        def wide_copy2_t(slot, sent, device):
+            piece = tall.at[x, slot]
+            return remote(piece, piece, wide2_t, sent, slot, device)
+
+        for r in (2, 1, 3):
+            n = (y + r) % 4
+            begin(wide_copy2_t(y, n, at_y(n)))
+
+        def part_a(n, core):
+            return z.at[:, n, core, 0:2]
+
+        def part_b(n, core):
+            return z.at[:, :, core, 2:4, band(n)]
+
+        def wide_copy1_a(slot, sent, device):
+            return remote(za, part_a(slot, c), wide1_a, sent, slot, device)
+
+        def wide_copy1_b(slot, sent, device):
+            return remote(zb, part_b(slot, c), wide1_b, sent, slot, device)
+
+        for r in (1, 3, 2):
+            n = (y + r) % 4
+            wide_copy2_a(n, n, at_y(n)).wait_recv()
+        for r in (2, 1, 3):
+            n = (x + r) % 4
+            begin(wide_copy1_a(x, n, at_x(n)))
+        for r in (1, 3, 2):
+            n = (x + r) % 4
+            wide_copy2_b(n, n, at_x(n)).wait_recv()
+        for r in (2, 1, 3):
+            n = (y + r) % 4
+            begin(wide_copy1_b(y, n, at_y(n)))
+        own_a = pltpu.make_async_copy(za, part_a(x, c), local.at[1])
+        own_a.start()
+        own_b = pltpu.make_async_copy(zb, part_b(y, c), local.at[2])
+        own_b.start()
+        begin(remote(za, part_a(x, c), share_a, x, x, sibling))
+        begin(remote(zb, part_b(y, c), share_b, y, y, sibling))
+        for r in (1, 3, 2):
+            n = (y + r) % 4
+            wide_copy2_t(n, n, at_y(n)).wait_recv()
+
+        def wide_copy1_t(slot, sent, device):
+            piece = tall.at[slot]
+            return remote(piece, piece, wide1_t, sent, slot, device)
+
+        for r in (2, 1, 3):
+            n = (x + r) % 4
+            begin(wide_copy1_t(x, n, at_x(n)))
+
+        def share_copy_a(n, core):
+            return remote(part_a(n, core), part_a(n, core), share_a, n, n, sibling)
+
+        def share_copy_b(n, core):
+            return remote(part_b(n, core), part_b(n, core), share_b, n, n, sibling)
+
+        for r in (1, 3, 2):
+            n = (x + r) % 4
+            wide_copy1_a(n, n, at_x(n)).wait_recv()
+            begin(share_copy_a(n, c))
+            n = (y + r) % 4
+            wide_copy1_b(n, n, at_y(n)).wait_recv()
+            begin(share_copy_b(n, c))
+        for r in (1, 3, 2):
+            n = (x + r) % 4
+            wide_copy1_t(n, n, at_x(n)).wait_recv()
+        share = remote(tall, to.at[c], share_t, 0, 0, sibling)
+        begin(share)
+        own_t = pltpu.make_async_copy(tall, to.at[c], local.at[3])
+        own_t.start()
+        for n in range(4):
+            share_copy_a(n, 1 - c).wait_recv()
+            share_copy_b(n, 1 - c).wait_recv()
+        for d in range(8):
+            block_copy(d).wait_recv()
+        own_a.wait()
+        own_b.wait()
+        share.wait_recv()
+        own_t.wait()
+        for copy in waits:
+            copy.wait_send()
+
+    pl.when(step == 4)(run)
 
 
 def whole(*shape):
@@ -621,21 +898,66 @@
     return pl.BlockSpec(shape, lambda n: zeros)
 
 
-def exchange(back, *operands):
+def forward_call(*operands):
     shape = jax.ShapeDtypeStruct
     out_shape = [shape((2, 4, 2, 4, 128, C), BF), shape((8, 400, C), BF), shape((4, 16, C), F32)]
-    if back:
-        tile = pl.BlockSpec((16, SIDE, C), lambda n: (n, 0, 0))
-        field = shape((SIDE, SIDE, C), BF)
-        out_shape = [field, field] + out_shape + [shape((2, 4, 4, PIECE, C), BF)]
-        out_specs = [tile, tile, HB, HB, whole(4, 16, C), HB]
-        in_specs = [tile, tile, whole(64, 128, C), whole(8, 400, C), whole(C, C)]
-        in_specs += [whole(8, C, C), whole(C, H), whole(H, C), whole(COLS, SIDE, 128)]
-        in_specs += [whole(ROWS, 160, 256), HB, HB, HB]
-    else:
-        out_shape.append(shape((1024, 640), BF))
-        out_specs = [HB, HB, VM, HB]
-        in_specs = [SM, VM, HB, HB, HB]
+    out_shape.append(shape((1024, 640), BF))
+    out_specs = [HB, HB, VM, HB]
+    in_specs = [SM, VM, HB, HB, HB]
+    sem = pltpu.SemaphoreType.DMA((2, 4))
+    scratch = [
+        pltpu.VMEM((2, 4, 4, 128, C), BF),
+        pltpu.VMEM((4, 2, 2, 128, C), BF),
+        pltpu.VMEM((4, 2, 4, 2, 32, C), BF),
+        pltpu.VMEM((4, 2, 2, 128, C), BF),
+        pltpu.VMEM((4, 2, 4, 2, 32, C), BF),
+        pltpu.VMEM((2, 2, 128, C), F32),
+        pltpu.VMEM((2, 4, 2, 32, C), F32),
+        pltpu.VMEM((16, 2, 16, C), F32),
+        pltpu.VMEM((16, 2, 16, C), F32),
+        pltpu.VMEM((4, 16, C), BF),
+        pltpu.VMEM((2, 2, 128, C), BF),
+        pltpu.VMEM((2, 4, 2, 32, C), BF),
+        pltpu.VMEM((2, 8, 4, C, C), F32),
+    ]
+    scratch += [sem] * 8 + [pltpu.SemaphoreType.DMA((2, 16))] * 4 + [pltpu.SemaphoreType.DMA((2, 8)), pltpu.SemaphoreType.DMA((6,))]
+    scratch += [
+        pltpu.VMEM((2, 4, 2, 4, 128, C), BF),
+        pltpu.VMEM((8, 400, C), BF),
+        pltpu.VMEM((1024, 640), BF),
+        pltpu.VMEM((10, 128, 8, C), F32),
+        pltpu.VMEM((128, 480), BF),
+    ]
+    scratch += [
+        pltpu.VMEM((SIDE + 60, 88, C), F32),
+        pltpu.VMEM((408, C), F32),
+        pltpu.VMEM((128, SIDE), BF),
+    ]
+    return pl.pallas_call(
+        forward_kernel,
+        out_shape=tuple(out_shape),
+        in_specs=in_specs,
+        out_specs=tuple(out_specs),
+        scratch_shapes=scratch,
+        compiler_params=pltpu.CompilerParams(
+            collective_id=1,
+            has_side_effects=True,
+            vmem_limit_bytes=VMEM_LIMIT,
+        ),
+        name="forward_and_exchange",
+    )(*operands)
+
+
+def cells_call(*operands):
+    shape = jax.ShapeDtypeStruct
+    out_shape = [shape((2, 4, 2, 4, 128, C), BF), shape((8, 400, C), BF), shape((4, 16, C), F32)]
+    tile = pl.BlockSpec((16, SIDE, C), lambda n: (n, 0, 0))
+    field = shape((SIDE, SIDE, C), BF)
+    out_shape = [field, field] + out_shape + [shape((2, 4, 4, PIECE, C), BF)]
+    out_specs = [tile, tile, HB, HB, whole(4, 16, C), HB]
+    in_specs = [tile, tile, whole(64, 128, C), whole(8, 400, C), whole(C, C)]
+    in_specs += [whole(8, C, C), whole(C, H), whole(H, C), whole(COLS, SIDE, 128)]
+    in_specs += [whole(ROWS, 160, 256), HB, HB, HB]
     sem = pltpu.SemaphoreType.DMA((2, 4))
     scratch = [
         pltpu.VMEM((2, 4, 4, 128, C), BF),
@@ -656,17 +978,16 @@
         pltpu.VMEM((2, 8, 4, C, C), F32),
     ]
     scratch += [sem] * 14 + [pltpu.SemaphoreType.DMA((2, 8)), pltpu.SemaphoreType.DMA((6,))]
-    if back:
-        scratch += [
-            pltpu.VMEM((4, 4, PIECE, C), BF),
-            pltpu.VMEM((4, 4, PIECE, C), BF),
-            pltpu.VMEM((4, 4, PIECE, C), BF),
-            pltpu.VMEM((4, PIECE, C), BF),
-            pltpu.VMEM((4, PIECE, C), BF),
-            pltpu.VMEM((PIECE, C), BF),
-            pltpu.VMEM((4, PIECE, C), BF),
-            pltpu.VMEM((4, 4, PIECE, C), BF),
-        ] + [sem] * 7
+    scratch += [
+        pltpu.VMEM((4, 4, PIECE, C), BF),
+        pltpu.VMEM((4, 4, PIECE, C), BF),
+        pltpu.VMEM((4, 4, PIECE, C), BF),
+        pltpu.VMEM((4, PIECE, C), BF),
+        pltpu.VMEM((4, PIECE, C), BF),
+        pltpu.VMEM((PIECE, C), BF),
+        pltpu.VMEM((4, PIECE, C), BF),
+        pltpu.VMEM((4, 4, PIECE, C), BF),
+    ] + [sem] * 7
     scratch += [
         pltpu.VMEM((2, 4, 2, 4, 128, C), BF),
         pltpu.VMEM((8, 400, C), BF),
@@ -674,45 +995,38 @@
         pltpu.VMEM((10, 128, 8, C), F32),
         pltpu.VMEM((128, 480), BF),
     ]
-    if back:
-        scratch += [
-            pltpu.VMEM((2, 4, 4, PIECE, C), BF),
-            pltpu.VMEM((10, 128, 8, C), F32),
-            pltpu.VMEM((640, 1024), BF),
-            pltpu.VMEM((1280, 160), BF),
-            pltpu.VMEM((80, 1280), BF),
-            pltpu.VMEM((400, C), F32),
-            pltpu.VMEM((400, C), F32),
-            pltpu.VMEM((1280, C), F32),
-            pltpu.VMEM((1280, C), F32),
-            pltpu.VMEM((1280, C), BF),
-            pltpu.VMEM((1280, H), F32),
-            pltpu.VMEM((1280, H), F32),
-            pltpu.VMEM((1280, H), BF),
-            pltpu.VMEM((1280, H), BF),
-            pltpu.VMEM((C, C), F32),
-            pltpu.VMEM((C, H), F32),
-            pltpu.VMEM((C, H), F32),
-        ]
-    else:
-        scratch += [
-            pltpu.VMEM((SIDE + 60, 88, C), F32),
-            pltpu.VMEM((408, C), F32),
-            pltpu.VMEM((128, SIDE), BF),
-        ]
+    scratch += [
+        pltpu.VMEM((2, 4, 4, PIECE, C), BF),
+        pltpu.VMEM((10, 128, 8, C), F32),
+        pltpu.VMEM((640, 1024), BF),
+        pltpu.VMEM((1280, 160), BF),
+        pltpu.VMEM((80, 1280), BF),
+        pltpu.VMEM((400, C), F32),
+        pltpu.VMEM((400, C), F32),
+        pltpu.VMEM((1280, C), F32),
+        pltpu.VMEM((1280, C), F32),
+        pltpu.VMEM((1280, C), BF),
+        pltpu.VMEM((1280, H), F32),
+        pltpu.VMEM((1280, H), F32),
+        pltpu.VMEM((1280, H), BF),
+        pltpu.VMEM((1280, H), BF),
+        pltpu.VMEM((C, C), F32),
+        pltpu.VMEM((C, H), F32),
+        pltpu.VMEM((C, H), F32),
+    ]
     return pl.pallas_call(
-        functools.partial(exchange_kernel, back),
+        cells_kernel,
         out_shape=tuple(out_shape),
         in_specs=in_specs,
         out_specs=tuple(out_specs),
         scratch_shapes=scratch,
-        grid=(5,) if back else (),
+        grid=(5,),
         compiler_params=pltpu.CompilerParams(
-            collective_id=2 if back else 1,
+            collective_id=2,
             has_side_effects=True,
             vmem_limit_bytes=VMEM_LIMIT,
         ),
-        name="cells_and_exchange" if back else "forward_and_exchange",
+        name="cells_and_exchange",
     )(*operands)
 
 
@@ -958,9 +1272,9 @@
 ):
     ty, gy, tx, gx = (jnp.asarray(t) for t in wave_tables())
     picks = ctx_level + (ctx_offset[:, :, 0] << 2) + (ctx_offset[:, :, 1] << 9)
-    z, arrived, u, big = exchange(False, picks, flow_field, ty, tx, spec_weight)
-    layer, pre, z, back, g, tot = exchange(
-        True, flow_field, cotangent, z.reshape(64, 128, C), arrived, skip_weight, ctx_weight,
+    z, arrived, u, big = forward_call(picks, flow_field, ty, tx, spec_weight)
+    layer, pre, z, back, g, tot = cells_call(
+        flow_field, cotangent, z.reshape(64, 128, C), arrived, skip_weight, ctx_weight,
         up_weight, down_weight, gy, gx, tx, big, spec_weight,
     )
     grad, spec, skip, ctx, up, down = last_call(

time: 153 us -> 148 us (0.967)
  Pallas kernels: 148 us -> 144 us
    pallas_call x2, Pallas kernels: 135 us -> 131 us  [the longest x1 76.2 us: cells_call(): pl.pallas_call(cells_kernel, out_shape=tuple(out_shape), in_specs=in_spec...]
where the time goes in v4:
time: 148 us
  Pallas kernels  144 us (97%)
  local copies, waits for them, and re-layouts  2.94 us (2%)
    pallas_call x1, Pallas kernels, cells_call(): pl.pallas_call(cells_kernel, out_shape=tuple(out_shape), in_specs=in_spec...  76.2 us
    pallas_call x1, Pallas kernels, forward_call(): pl.pallas_call(forward_kernel, out_shape=tuple(out_shape), in_specs=in_sp...  54.4 us
    pallas_call x1, Pallas kernels, last_call(): pl.pallas_call(last_kernel, grid=(5,), out_shape=(shape((SIDE, SIDE, C),...  13.2 us

profile of v4, /device:TPU:1, one launch (start us, length us, event | category | flops | bytes accessed | tf_op | source)
XLA Modules:
  0.0 148.1 jit_solution(16912443028381369285)
XLA Ops:
  0.6 0.8 fusion
  1.4 0.1 copy.20
  1.5 0.1 copy.22
  1.6 0.8 copy.21
  2.4 0.6 bitcast_add_fusion.refs_0_.picks
  3.0 54.4 %forward_and_exchange.1 = (bf16[2,4,2,4,128,128]{5,4,3,2,1,0:T(8,128)(2,1)}, bf16[8,400,128]{2,1,0:T(8,128)(2,1)}, f32[4,16,128]{2,1,0:T(8,128)}, bf16[1024,640]{1,0:T(8,128)(2,1)}) custom-call(s32[128,8]{1,0:T(8,128)} %bitcast_add_fusion.refs_0_.picks, bf16[80,80,128]{2,1,0:T(8,128)(2,1)} %refs_0_.1, bf16[16,128,80]{2,1,0:T(8,128)(2,1)} %constant.12.clone.refs_2_, ...), custom_call_target="tpu_custom_call" | custom-call | tf_op jit(solution)/shard_map/forward_and_exchange/pallas_call | solution.py:936
  57.5 76.2 %cells_and_exchange.1 = (bf16[80,80,128]{2,1,0:T(8,128)(2,1)}, bf16[80,80,128]{2,1,0:T(8,128)(2,1)}, bf16[2,4,2,4,128,128]{5,4,3,2,1,0:T(8,128)(2,1)}, bf16[8,40...) custom-call(bf16[80,80,128]{2,1,0:T(8,128)(2,1)} %refs_0_.1, ...), custom_call_target="tpu_custom_call" | custom-call | tf_op jit(solution)/shard_map/cells_and_exchange/pallas_call | solution.py:1017
  133.7 0.0 copy-start
  133.7 13.2 %field_gradient.1 = (bf16[80,80,128]{2,1,0:T(8,128)(2,1)}, f32[2,8,4,128,128]{4,3,2,1,0:T(8,128)}, f32[128,128]{1,0:T(8,128)}, f32[8,128,128]{2,1,0:T(8,128)}, f32[128,512]{1,0:T(8,128)}, /*index=5*/f32[512,128]{1,0:T(8,128)}) custom-call(s32[128,8]{1,0:T(8,128)} %bitcast_add_fusion.refs_0_.picks, bf16[80,80,128]{2,1,0:T(8,128)(2,1)} %get-tuple-element.27.pre, ...), custom_call_target="tpu_custom_call" | custom-call | tf_op jit(solution)/shard_map/field_gradient/pallas_call | solution.py:1233
  146.9 0.0 copy-done
  146.9 1.2 copy.24
Async XLA Ops:
  133.7 13.2 %copy-start = (bf16[80,80,128]{2,1,0:T(8,128)(2,1)S(1)}, bf16[80,80,128]{2,1,0:T(8,128)(2,1)}, u32[]{:S(2)}) copy-start(bf16[80,80,128]{2,1,0:T(8,128)(2,1)} %get-tuple-element.48) | copy-start | bytes 4915204

commit v5 on v4

--- a/solution.py
+++ b/solution.py
@@ -123,7 +123,7 @@
                 p_ref[:, 2 * (2 * pair + h) + r] = piece.reshape(10, 8, C)
         return carry
 
-    lax.fori_loop(0, 32, step, 0, unroll=16)
+    lax.fori_loop(0, 32, step, 0, unroll=32)
 
 
 def y_store(big, pair_cells, ay_ref, pair):
@@ -159,7 +159,7 @@
 
 def pick_of(picks, row, col, d):
     target = lax.rem(row - STEP_ROWS[d] + ROWS, ROWS) * COLS
-    return picks[target + lax.rem(col - STEP_COLS[d] + COLS, COLS), d]
+    return picks[d, target + lax.rem(col - STEP_COLS[d] + COLS, COLS)]
 
 
 def pick_blocks(picks, row, col, field, grid, tmp, blocks):
@@ -1271,7 +1271,7 @@
     ctx_level, ctx_offset,
 ):
     ty, gy, tx, gx = (jnp.asarray(t) for t in wave_tables())
-    picks = ctx_level + (ctx_offset[:, :, 0] << 2) + (ctx_offset[:, :, 1] << 9)
+    picks = ctx_level.T + (ctx_offset[:, :, 0].T << 2) + (ctx_offset[:, :, 1].T << 9)
     z, arrived, u, big = forward_call(picks, flow_field, ty, tx, spec_weight)
     layer, pre, z, back, g, tot = cells_call(
         flow_field, cotangent, z.reshape(64, 128, C), arrived, skip_weight, ctx_weight,

time: 148 us -> 147 us (level)
  no operation moved by 1% of the time
where the time goes in v5:
time: 147 us
  Pallas kernels  143 us (97%)
  local copies, waits for them, and re-layouts  1.95 us (1%)
    pallas_call x1, Pallas kernels, cells_call(): pl.pallas_call(cells_kernel, out_shape=tuple(out_shape), in_specs=in_spec...  75.9 us
    pallas_call x1, Pallas kernels, forward_call(): pl.pallas_call(forward_kernel, out_shape=tuple(out_shape), in_specs=in_sp...  54.1 us
    pallas_call x1, Pallas kernels, last_call(): pl.pallas_call(last_kernel, grid=(5,), out_shape=(shape((SIDE, SIDE, C),...  13.1 us

profile of v5, /device:TPU:1, one launch (start us, length us, event | category | flops | bytes accessed | tf_op | source)
XLA Modules:
  0.0 147.0 jit_solution(2033977147711940042)
XLA Ops:
  0.6 0.8 fusion.1
  1.4 1.3 fusion.refs_0_.picks
  2.7 54.1 %forward_and_exchange.1 = (bf16[2,4,2,4,128,128]{5,4,3,2,1,0:T(8,128)(2,1)}, bf16[8,400,128]{2,1,0:T(8,128)(2,1)}, f32[4,16,128]{2,1,0:T(8,128)}, bf16[1024,640]{1,0:T(8,128)(2,1)}) custom-call(s32[8,128]{1,0:T(8,128)} %fusion.refs_0_.picks, bf16[80,80,128]{2,1,0:T(8,128)(2,1)} %refs_0_.1, bf16[16,128,80]{2,1,0:T(8,128)(2,1)} %constant.12.clone.refs_2_, ...), custom_call_target="tpu_custom_call" | custom-call | tf_op jit(solution)/shard_map/forward_and_exchange/pallas_call | solution.py:936
  56.8 75.9 %cells_and_exchange.1 = (bf16[80,80,128]{2,1,0:T(8,128)(2,1)}, bf16[80,80,128]{2,1,0:T(8,128)(2,1)}, bf16[2,4,2,4,128,128]{5,4,3,2,1,0:T(8,128)(2,1)}, bf16[8,40...) custom-call(bf16[80,80,128]{2,1,0:T(8,128)(2,1)} %refs_0_.1, ...), custom_call_target="tpu_custom_call" | custom-call | tf_op jit(solution)/shard_map/cells_and_exchange/pallas_call | solution.py:1017
  132.7 0.0 copy-start
  132.7 13.1 %field_gradient.1 = (bf16[80,80,128]{2,1,0:T(8,128)(2,1)}, f32[2,8,4,128,128]{4,3,2,1,0:T(8,128)}, f32[128,128]{1,0:T(8,128)}, f32[8,128,128]{2,1,0:T(8,128)}, f32[128,512]{1,0:T(8,128)}, /*index=5*/f32[512,128]{1,0:T(8,128)}) custom-call(s32[8,128]{1,0:T(8,128)} %fusion.refs_0_.picks, bf16[80,80,128]{2,1,0:T(8,128)(2,1)} %get-tuple-element.27.pre, ...), custom_call_target="tpu_custom_call" | custom-call | tf_op jit(solution)/shard_map/field_gradient/pallas_call | solution.py:1233
  145.8 0.0 copy-done
  145.8 1.2 copy.25
Async XLA Ops:
  132.7 13.1 %copy-start = (bf16[80,80,128]{2,1,0:T(8,128)(2,1)S(1)}, bf16[80,80,128]{2,1,0:T(8,128)(2,1)}, u32[]{:S(2)}) copy-start(bf16[80,80,128]{2,1,0:T(8,128)(2,1)} %get-tuple-element.48) | copy-start | bytes 4915204
